TPU v7x, 512 devices: a whole 4x4x16 slice. The times are simulated.
512 devices in a mesh: blk: 64 (over z, y), obs: 8 (over x, core).
Axes of the slice: x: 4, y: 4, z: 16, core: 2. Of those that a mesh axis runs over, the one named last changes fastest.
Arguments:
- populations: float32 [64, 19, 32, 1024], P('blk', None, 'obs'), may hold values from 0.011111111 to 0.533333333, as said below
- block_faces: int32 [64, 4], P('blk'), may hold values from 0 to 63, as said below
- block_edges: int32 [64, 4], P('blk'), may hold values from 0 to 63, as said below
- probe_cell: int32 [65536], P(('blk', 'obs')), may hold values from 0 to 4095
- history: bfloat16 [65536, 512], P(('blk', 'obs')), may hold values from -6 to 6
- panel_count: int32 [512], P(('blk', 'obs')), may hold values from 0 to 128, as said below
- panel_owner: int32 [65536], P(('blk', 'obs')), may hold values from 0 to 4095, as said below
- panel_pos: bfloat16 [3, 32768], P(None, ('blk', 'obs')), may hold values from -1 to 1
- panel_normal: bfloat16 [3, 32768], P(None, ('blk', 'obs')), may hold values from -0.15625 to 0.15625
- observers: float32 [3, 1024], P(None, 'obs'), may hold values from -8 to 8, as said below
Outputs:
- populations_out: float32 [64, 19, 32, 1024], P('blk', None, 'obs')
- spectrum: float32 [8, 128, 128], P('obs', 'blk')
Inputs may be any that keep to these rules, and one draw needn't show every extreme that they name: `populations`: every population is positive. The blocks form a lattice of 16 by 4 blocks along y and z, periodic in both, one block deep in x; block_faces[b] names the blocks beside b at -y, +y, -z, +z. block_edges[b] names the blocks at (-y,-z), (-y,+z), (+y,-z), (+y,+z) of b: the y neighbour's z neighbour, which is the z neighbour's y neighbour. The eight face and edge neighbours of a block are distinct and differ from it. The live slots of a device are its first panel_count slots. The counts of the devices at one obs index sum to 4096. `panel_owner`: in a live slot of the device at blk index b and obs index o the value is q * 64 + j: slot j of the owner at blk index q and the same obs index. Every owner slot receives exactly one live panel. A device sends at most 2 live panels to one owner, and its live panels go to the owners in numbers that differ by at most one. Dead slots hold arbitrary values of the range. `observers`: every observer lies at a distance of 4 to 8 from the anchor (0, 0, 0).
All inputs are finite; a program needn't handle non-finite values.
Results may differ from a plain program's by a relative error of at most 0.0032.
The roundings to bfloat16 on the way count: a program that leaves them out, or rounds other values in their place, can miss the bound.
Values may be sent and summed in bfloat16 or wider, within the bound.
No kernel may reach another device: no remote copies, remote signals or barrier semaphores. Data moves between devices by JAX's collectives and lax.ppermute only.
A program may use at most 128 MiB of HBM per device.

v0:
```python
import math

import jax
import jax.numpy as jnp
from jax import lax
from jax.sharding import PartitionSpec as P

BS = 32
STEPS = 4
SAMPLES = 256
BINS = 64
P_OWN = 64


velocity_list = [
    (0, 0, 0),
    (1, 0, 0),
    (-1, 0, 0),
    (0, 1, 0),
    (0, -1, 0),
    (0, 0, 1),
    (0, 0, -1),
    (1, 1, 0),
    (-1, -1, 0),
    (1, -1, 0),
    (-1, 1, 0),
    (1, 0, 1),
    (-1, 0, -1),
    (1, 0, -1),
    (-1, 0, 1),
    (0, 1, 1),
    (0, -1, -1),
    (0, 1, -1),
    (0, -1, 1),
]
weight_list = [1.0 / 3.0] + [1.0 / 18.0] * 6 + [1.0 / 36.0] * 12
x_moving = [1, 2, 7, 8, 9, 10, 11, 12, 13, 14]
y_upward = [3, 7, 10, 15, 17]
y_downward = [4, 8, 9, 16, 18]
z_upward = [5, 11, 14, 15, 18]
z_downward = [6, 12, 13, 16, 17]
relax_rate = 1.6
pressure_gain = 60.0
sound_speed = 0.5


def padded(block, sides, width):
    for axis, dim in sides:
        count = lax.axis_size(axis)
        forward = [(i, i + 1) for i in range(count - 1)]
        forward.append((count - 1, 0))
        backward = [(target, source) for source, target in forward]
        low = lax.ppermute(
            lax.slice_in_dim(block, block.shape[dim] - width, None, axis=dim), axis, forward
        )
        high = lax.ppermute(lax.slice_in_dim(block, 0, width, axis=dim), axis, backward)
        block = jnp.concatenate([low, block, high], axis=dim)
    return block


def rows_first(arrays, axis, dims):
    turned = [jnp.moveaxis(a, dim, 0) for a, dim in zip(arrays, dims)]
    both = jnp.concatenate([t.reshape(len(t), -1) for t in turned], axis=1)
    out, at, done = (lax.all_gather(both, axis, axis=0, tiled=True), 0, [])
    for t, dim in zip(turned, dims):
        piece = out[:, at : at + t[0].size].reshape(-1, *t.shape[1:])
        done.append(jnp.moveaxis(piece, 0, dim))
        at += t[0].size
    return tuple(done)


def in_blocks(shard, dim, count):
    shape = shard.shape
    blocks = shard.reshape(*shape[:dim], count, shape[dim] // count, *shape[dim + 1 :])
    return jnp.moveaxis(blocks, dim, 0)


def summed_on_arrival(shard, axis, dim):
    count = lax.axis_size(axis)
    blocks = lax.all_to_all(in_blocks(shard, dim, count), axis, 0, 0, tiled=True)
    return jnp.sum(blocks, axis=0)


def component(axis_number, extra):
    values = jnp.array([velocity[axis_number] for velocity in velocity_list], jnp.float32)
    return values.reshape((19,) + extra)


def collide(field):
    extra = (1,) * (field.ndim - 1)
    along_x = component(0, extra)
    along_y = component(1, extra)
    along_z = component(2, extra)
    weights = jnp.array(weight_list, jnp.float32).reshape((19,) + extra)
    density = jnp.sum(field, axis=0)
    speed_x = jnp.sum(along_x * field, axis=0) / density
    speed_y = jnp.sum(along_y * field, axis=0) / density
    speed_z = jnp.sum(along_z * field, axis=0) / density
    projected = along_x * speed_x + along_y * speed_y + along_z * speed_z
    squared = speed_x * speed_x + speed_y * speed_y + speed_z * speed_z
    equilibrium = (
        weights * density * (1.0 + 3.0 * projected + 4.5 * projected * projected - 1.5 * squared)
    )
    return field + relax_rate * (equilibrium - field)


def stream_merged(widened, planes):
    below_plane, above_plane, near_plane, far_plane = planes
    slab_depth = widened.shape[1] - 2
    lane_count = widened.shape[2]
    lane_index = jnp.arange(lane_count, dtype=jnp.int32)
    lane_row = lane_index // BS
    lane_column = lane_index % BS
    parts = []
    for number, velocity in enumerate(velocity_list):
        shift_x, shift_y, shift_z = velocity
        begin = 1 - shift_x
        moved = jnp.roll(
            widened[number, begin : begin + slab_depth], shift_y * BS + shift_z, axis=-1
        )
        if shift_y != 0:
            source_plane = below_plane if shift_y == 1 else above_plane
            row_values = jnp.roll(
                source_plane[number, begin : begin + slab_depth], shift_z, axis=-1
            )
            edge_index = 0 if shift_y == 1 else BS - 1
            moved = jnp.where(
                (lane_row == edge_index)[None, :], jnp.tile(row_values, (1, BS)), moved
            )
        if shift_z != 0:
            source_plane = near_plane if shift_z == 1 else far_plane
            column_values = source_plane[
                number, begin : begin + slab_depth, 1 - shift_y : 1 - shift_y + BS
            ]
            edge_index = 0 if shift_z == 1 else BS - 1
            moved = jnp.where(
                (lane_column == edge_index)[None, :], jnp.repeat(column_values, BS, axis=-1), moved
            )
        parts.append(moved)
    return jnp.stack(parts)


def place_pieces(pieces, targets, blocks):
    onehot = (targets[:, None] == jnp.arange(blocks, dtype=jnp.int32)[None, :]).astype(jnp.float32)
    return jnp.einsum("kn,kf->nf", onehot, pieces, precision=lax.Precision.HIGHEST)


def spread_pops(piece, chosen, shape):
    return jnp.zeros(shape, jnp.float32).at[jnp.array(chosen)].set(piece)


def direct_halo(widened, block_faces, block_edges, blocks):
    depth_x = widened.shape[1]
    lane_count = widened.shape[2]

    def corner_piece(number, lane_at):
        return jnp.zeros((5, depth_x, BS), jnp.float32).at[0, :, 0].set(widened[number, :, lane_at])

    def corner_plane(number, vector):
        return jnp.zeros((19, depth_x, 1), jnp.float32).at[number, :, 0].set(vector)

    outgoing = jnp.stack(
        [
            widened[jnp.array(y_downward), :, 0:BS],
            widened[jnp.array(y_upward), :, lane_count - BS :],
            widened[jnp.array(z_downward), :, 0::BS],
            widened[jnp.array(z_upward), :, BS - 1 :: BS],
            corner_piece(16, 0),
            corner_piece(18, BS - 1),
            corner_piece(17, (BS - 1) * BS),
            corner_piece(15, BS * BS - 1),
        ]
    ).reshape(8, -1)
    targets = jnp.concatenate([block_faces, block_edges])
    received = lax.all_to_all(
        place_pieces(outgoing, targets, blocks), "blk", split_axis=0, concat_axis=0, tiled=True
    )
    chosen = jnp.take(received, targets, axis=0).reshape(8, 5, depth_x, BS)
    below_plane = spread_pops(chosen[0], y_upward, (19, depth_x, BS))
    above_plane = spread_pops(chosen[1], y_downward, (19, depth_x, BS))
    near_core = spread_pops(chosen[2], z_upward, (19, depth_x, BS))
    far_core = spread_pops(chosen[3], z_downward, (19, depth_x, BS))
    near_plane = jnp.concatenate(
        [corner_plane(15, chosen[4, 0, :, 0]), near_core, corner_plane(18, chosen[6, 0, :, 0])],
        axis=2,
    )
    far_plane = jnp.concatenate(
        [corner_plane(17, chosen[5, 0, :, 0]), far_core, corner_plane(16, chosen[7, 0, :, 0])],
        axis=2,
    )
    return (below_plane, above_plane, near_plane, far_plane)


def transform_table():
    moments = jnp.arange(SAMPLES, dtype=jnp.int32)[:, None]
    harmonics = jnp.arange(BINS, dtype=jnp.int32)[None, :] + 1
    turns = moments * harmonics % SAMPLES
    phases = turns.astype(jnp.float32) * (2.0 * math.pi / SAMPLES)
    return jnp.concatenate([jnp.cos(phases), -jnp.sin(phases)], axis=1).astype(jnp.bfloat16)


def radiate(spectra, place, normal, listen):
    values = spectra.astype(jnp.float32)
    press_real = values[0:BINS].T
    press_imag = values[BINS : 2 * BINS].T
    rate_real = values[2 * BINS : 3 * BINS].T
    rate_imag = values[3 * BINS : 4 * BINS].T
    offsets = listen[:, None, :] - place.astype(jnp.float32)[:, :, None]
    distance_sq = jnp.sum(offsets * offsets, axis=0)
    distance = jnp.sqrt(distance_sq)
    facing = jnp.sum(normal.astype(jnp.float32)[:, :, None] * offsets, axis=0)
    far_term = facing / (4.0 * math.pi * sound_speed * distance_sq)
    near_term = facing / (4.0 * math.pi * distance_sq * distance)
    angular = (jnp.arange(BINS, dtype=jnp.float32) + 1.0) * (2.0 * math.pi / SAMPLES)
    phases = angular[None, :, None] * (distance / sound_speed)[:, None, :]
    cosine = jnp.cos(phases)
    sine_part = jnp.sin(phases)
    weight_real = (
        far_term[:, None, :] * rate_real[:, :, None]
        + near_term[:, None, :] * press_real[:, :, None]
    )
    weight_imag = (
        far_term[:, None, :] * rate_imag[:, :, None]
        + near_term[:, None, :] * press_imag[:, :, None]
    )
    real_part = jnp.sum(weight_real * cosine + weight_imag * sine_part, axis=0)
    imag_part = jnp.sum(weight_imag * cosine - weight_real * sine_part, axis=0)
    return jnp.concatenate([real_part, imag_part], axis=0).T


def radiate_blocks(spectra, place, normal, listen):
    count_panels = spectra.shape[1]
    listener_count = listen.shape[1]
    block_size = 128
    while block_size > 1 and (
        count_panels % block_size != 0 or block_size * listener_count > 16384
    ):
        block_size = block_size // 2

    def radiate_accumulate(block_number, total):
        begin = block_number * block_size
        return total + radiate(
            lax.dynamic_slice_in_dim(spectra, begin, block_size, 1),
            lax.dynamic_slice_in_dim(place, begin, block_size, 1),
            lax.dynamic_slice_in_dim(normal, begin, block_size, 1),
            listen,
        )

    return lax.fori_loop(
        0,
        count_panels // block_size,
        radiate_accumulate,
        jnp.zeros((listener_count, 2 * BINS), jnp.float32),
    )


def route_slots(payload, owners, alive_slot, blocks):
    count_slots = payload.shape[0]
    capacity = -(-count_slots // blocks)
    target = owners // P_OWN
    member = (
        (target[:, None] == jnp.arange(blocks, dtype=jnp.int32)[None, :]) & alive_slot[:, None]
    ).astype(jnp.int32)
    before = jnp.cumsum(member, axis=0) - member
    order_within = jnp.sum(before * member, axis=1)
    slot_label = jnp.where(alive_slot, target * capacity + order_within, -1)
    matches = slot_label[:, None] == jnp.arange(blocks * capacity, dtype=jnp.int32)[None, :]
    source = jnp.sum(
        jnp.where(matches, jnp.arange(count_slots, dtype=jnp.int32)[:, None], 0), axis=0
    )
    filled = jnp.any(matches, axis=0)
    outgoing = jnp.take(payload, source, axis=0).reshape(blocks, capacity, payload.shape[1])
    tagged = jnp.where(filled, jnp.take(owners, source), -1).reshape(blocks, capacity)
    return (outgoing, tagged)


def settle(incoming, tagged):
    keeper = lax.axis_index("blk")
    flat_tags = tagged.reshape(-1)
    slot_here = flat_tags - keeper * P_OWN
    choose = (
        (slot_here[:, None] == jnp.arange(P_OWN, dtype=jnp.int32)[None, :])
        & (flat_tags[:, None] >= 0)
    ).astype(jnp.bfloat16)
    return jnp.einsum(
        "rw,rp->wp",
        incoming.reshape(-1, incoming.shape[-1]),
        choose,
        preferred_element_type=jnp.float32,
    ).astype(jnp.bfloat16)


def body(
    populations,
    block_faces,
    block_edges,
    probe_cell,
    history,
    panel_count,
    panel_owner,
    panel_pos,
    panel_normal,
    observers,
):
    blocks = lax.axis_size("blk")
    lattice_state = populations[0]
    slab_depth = lattice_state.shape[1]
    lane_count = lattice_state.shape[2]
    faces_here = block_faces[0]
    edges_here = block_edges[0]
    readings = []
    for turn_index in range(STEPS):
        collided = collide(lattice_state)
        slab_edges = padded(collided[jnp.array(x_moving)], (("obs", 1),), 1)
        lower_plane = spread_pops(slab_edges[:, 0:1], x_moving, (19, 1, lane_count))
        upper_plane = spread_pops(slab_edges[:, -1:], x_moving, (19, 1, lane_count))
        widened = jnp.concatenate([lower_plane, collided, upper_plane], axis=1)
        planes = direct_halo(widened, faces_here, edges_here, blocks)
        lattice_state = stream_merged(widened, planes)
        density = jnp.sum(lattice_state, axis=0).reshape(-1)
        readings.append(jnp.take(density, probe_cell))
    populations_out = lattice_state.reshape(1, 19, slab_depth, lane_count)
    gained = pressure_gain * (jnp.stack(readings, axis=1) - 1.0)
    previous = jnp.concatenate(
        [history[:, SAMPLES - 1 : SAMPLES].astype(jnp.float32), gained[:, :-1]], axis=1
    )
    rate_values = gained - previous
    recent = jnp.concatenate(
        [
            history[:, STEPS:SAMPLES],
            gained.astype(jnp.bfloat16),
            history[:, SAMPLES + STEPS :],
            rate_values.astype(jnp.bfloat16),
        ],
        axis=1,
    )
    transform = transform_table()
    count_slots = recent.shape[0]
    alive_slot = jnp.arange(count_slots, dtype=jnp.int32) < panel_count[0]
    local_spectra = (
        jnp.dot(
            recent.reshape(count_slots * 2, SAMPLES), transform, preferred_element_type=jnp.float32
        )
        .astype(jnp.bfloat16)
        .reshape(count_slots, 4 * BINS)
    )
    outgoing, tagged = route_slots(local_spectra, panel_owner, alive_slot, blocks)
    incoming, tags_in = (
        lax.all_to_all(outgoing, "blk", split_axis=0, concat_axis=0, tiled=True),
        lax.all_to_all(tagged, "blk", split_axis=0, concat_axis=0, tiled=True),
    )
    spectra = settle(incoming, tags_in)
    pieces = rows_first((spectra, panel_pos, panel_normal), "obs", (1, 1, 1))
    partial_value = radiate_blocks(pieces[0], pieces[1], pieces[2], observers)
    summed = summed_on_arrival(partial_value, "blk", 0)
    return (populations_out, summed.reshape(1, -1, 2 * BINS))


def solution(mesh):
    placed = (
        P("blk", None, "obs", None),
        P("blk", None),
        P("blk", None),
        P(("blk", "obs")),
        P(("blk", "obs"), None),
        P(("blk", "obs")),
        P(("blk", "obs")),
        P(None, ("blk", "obs")),
        P(None, ("blk", "obs")),
        P(None, "obs"),
    )
    return jax.shard_map(
        body,
        mesh=mesh,
        in_specs=placed,
        out_specs=(P("blk", None, "obs", None), P("obs", "blk", None)),
        check_vma=False,
    )
```

profile of v0, /device:TPU:1, one launch (start us, length us, event | category | flops | bytes accessed | tf_op | source)
XLA Modules:
  0.0 458.9 jit_solution(12704072648931359649)
XLA Ops:
  3.6 1.6 fusion.16
  5.9 2.6 collective-permute-start
  8.6 4.3 collective-permute-start.1
  17.7 1.6 gather_fusion.20
  28.9 5.3 %copy.822 = f32[19,6,1024]{1,2,0:T(8,128)} copy(f32[19,6,1024]{2,1,0:T(8,128)S(1)} %pad_maximum_fusion) | data formatting | bytes 933888 | tf_op jit(solution)/shard_map/concatenate | solution.py:317
  34.2 7.2 %copy.818 = f32[19,6,1024]{1,0,2:T(8,128)} copy(f32[19,6,1024]{2,1,0:T(8,128)S(1)} %pad_maximum_fusion) | data formatting | bytes 933888 | tf_op jit(solution)/shard_map/concatenate | solution.py:317
  42.1 2.7 gather_fusion.4
  44.8 2.7 gather_fusion.3
  47.8 1.5 gather_fusion.2
  49.4 1.5 gather_fusion.1
  52.7 14.3 %all-to-all-start = ((f32[64,1,960]{2,1,0:T(1,128)}), f32[64,1,960]{2,1,0:T(1,128)S(1)}, u32[]{:S(2)}, u32[]{:S(2)}) async-start(f32[64,1,960]{2,1,0:T(1,128)} %copy.830), calls=%async_computation | async-start | bytes 524288 | tf_op jit(solution)/shard_map/all_to_all | solution.py:175
  67.9 17.5 %all-to-all-done = f32[64,1,960]{2,1,0:T(1,128)S(1)} async-done(((f32[64,1,960]{2,1,0:T(1,128)}), f32[64,1,960]{2,1,0:T(1,128)S(1)}, u32[]{:S(2)}, u32[]{:S(2)}) %all-to-all-start) | async-done | bytes 245792 | tf_op jit(solution)/shard_map/all_to_all | solution.py:175
  98.4 6.2 %collective-permute-start.2 = (f32[10,1,1024]{2,1,0:T(1,128)S(1)}, f32[10,1,1024]{2,1,0:T(1,128)S(1)}, u32[]{:S(2)}, u32[]{:S(2)}) collective-permute-start(f32[10,1,1024]{2,1,0:T(1,128)S(1)} %get-tuple-element.786), channel_id=1, source_target_pairs={{0,1},{1,2},{2,3},{3,4},{4,5},{5,6},{6,7},{7,0},{8,9},{9,10},{10,1... | collective-permute-start | bytes 122888 | tf_op jit(solution)/shard_map/ppermute | solution.py:53
  105.9 2.2 collective-permute-done.3
  111.5 5.2 %copy.845 = f32[19,6,1024]{1,2,0:T(8,128)} copy(f32[19,6,1024]{2,1,0:T(8,128)S(1)} %pad_maximum_fusion.1) | data formatting | bytes 933888 | tf_op jit(solution)/shard_map/concatenate | solution.py:317
  116.7 2.7 gather_fusion.9
  119.4 2.7 gather_fusion.8
  122.1 7.2 %copy.841 = f32[19,6,1024]{1,0,2:T(8,128)} copy(f32[19,6,1024]{2,1,0:T(8,128)S(1)} %pad_maximum_fusion.1) | data formatting | bytes 933888 | tf_op jit(solution)/shard_map/concatenate | solution.py:317
  130.8 1.5 gather_fusion.6
  135.2 4.8 %all-to-all-start.1 = ((f32[64,1,960]{2,1,0:T(1,128)}), f32[64,1,960]{2,1,0:T(1,128)S(1)}, u32[]{:S(2)}, u32[]{:S(2)}) async-start(f32[64,1,960]{2,1,0:T(1,128)} %copy.853), calls=%async_computation.1 | async-start | bytes 524288 | tf_op jit(solution)/shard_map/all_to_all | solution.py:175
  140.9 19.9 %all-to-all-done.1 = f32[64,1,960]{2,1,0:T(1,128)S(1)} async-done(((f32[64,1,960]{2,1,0:T(1,128)}), f32[64,1,960]{2,1,0:T(1,128)S(1)}, u32[]{:S(2)}, u32[]{:S(2)}) %all-to-all-start.1) | async-done | bytes 245792 | tf_op jit(solution)/shard_map/all_to_all | solution.py:175
  173.9 2.0 collective-permute-start.4
  177.7 1.6 collective-permute-done.5
  182.7 5.2 %copy.868 = f32[19,6,1024]{1,2,0:T(8,128)} copy(f32[19,6,1024]{2,1,0:T(8,128)S(1)} %pad_maximum_fusion.2) | data formatting | bytes 933888 | tf_op jit(solution)/shard_map/concatenate | solution.py:317
  187.9 2.7 gather_fusion.14
  190.7 2.7 gather_fusion.13
  193.4 7.2 %copy.864 = f32[19,6,1024]{1,0,2:T(8,128)} copy(f32[19,6,1024]{2,1,0:T(8,128)S(1)} %pad_maximum_fusion.2) | data formatting | bytes 933888 | tf_op jit(solution)/shard_map/concatenate | solution.py:317
  206.5 5.7 %all-to-all-start.2 = ((f32[64,1,960]{2,1,0:T(1,128)}), f32[64,1,960]{2,1,0:T(1,128)S(1)}, u32[]{:S(2)}, u32[]{:S(2)}) async-start(f32[64,1,960]{2,1,0:T(1,128)} %copy.876), calls=%async_computation.2 | async-start | bytes 524288 | tf_op jit(solution)/shard_map/all_to_all | solution.py:175
  213.1 18.4 %all-to-all-done.2 = f32[64,1,960]{2,1,0:T(1,128)S(1)} async-done(((f32[64,1,960]{2,1,0:T(1,128)}), f32[64,1,960]{2,1,0:T(1,128)S(1)}, u32[]{:S(2)}, u32[]{:S(2)}) %all-to-all-start.2) | async-done | bytes 245792 | tf_op jit(solution)/shard_map/all_to_all | solution.py:175
  244.5 3.8 collective-permute-start.6
  250.0 1.7 collective-permute-done.7
  254.6 5.2 %copy.891 = f32[19,6,1024]{1,2,0:T(8,128)} copy(f32[19,6,1024]{2,1,0:T(8,128)S(1)} %pad_maximum_fusion.3) | data formatting | bytes 933888 | tf_op jit(solution)/shard_map/concatenate | solution.py:317
  259.8 2.7 gather_fusion.19
  262.5 2.7 gather_fusion.18
  265.2 7.2 %copy.887 = f32[19,6,1024]{1,0,2:T(8,128)} copy(f32[19,6,1024]{2,1,0:T(8,128)S(1)} %pad_maximum_fusion.3) | data formatting | bytes 933888 | tf_op jit(solution)/shard_map/concatenate | solution.py:317
  273.9 1.5 gather_fusion.16
  278.4 5.8 %all-to-all-start.3 = ((f32[64,1,960]{2,1,0:T(1,128)}), f32[64,1,960]{2,1,0:T(1,128)S(1)}, u32[]{:S(2)}, u32[]{:S(2)}) async-start(f32[64,1,960]{2,1,0:T(1,128)} %copy.899), calls=%async_computation.3 | async-start | bytes 524288 | tf_op jit(solution)/shard_map/all_to_all | solution.py:175
  284.7 19.5 %all-to-all-done.3 = f32[64,1,960]{2,1,0:T(1,128)S(1)} async-done(((f32[64,1,960]{2,1,0:T(1,128)}), f32[64,1,960]{2,1,0:T(1,128)S(1)}, u32[]{:S(2)}, u32[]{:S(2)}) %all-to-all-start.3) | async-done | bytes 245792 | tf_op jit(solution)/shard_map/all_to_all | solution.py:175
  304.2 6.7 %all-to-all-start.4 = ((s32[64,1,2]{2,1,0:T(1,128)}), s32[64,1,2]{2,1,0:T(1,128)S(1)}, u32[]{:S(2)}, u32[]{:S(2)}) async-start(s32[64,1,2]{2,1,0:T(1,128)} %bitcast.324), calls=%async_computation.4 | async-start | bytes 65536 | tf_op jit(solution)/shard_map/all_to_all | solution.py:350
  325.7 14.5 %all-to-all-start.5 = ((bf16[64,2,256]{2,1,0:T(2,128)(2,1)}), bf16[64,2,256]{2,1,0:T(2,128)(2,1)S(1)}, u32[]{:S(2)}, u32[]{:S(2)}) async-start(bf16[64,2,256]{2,1,0:T(2,128)(2,1)} %broadcast_select_fusion), calls=%async_computation.5 | async-start | bytes 131072 | tf_op jit(solution)/shard_map/all_to_all | solution.py:349
  340.7 13.7 %all-to-all-done.5 = bf16[64,2,256]{2,1,0:T(2,128)(2,1)S(1)} async-done(((bf16[64,2,256]{2,1,0:T(2,128)(2,1)}), bf16[64,2,256]{2,1,0:T(2,128)(2,1)S(1)}, u32[]{:S(2)}, u32[]{:S(2)}) %all-to-all-start.5) | async-done | bytes 65568 | tf_op jit(solution)/shard_map/all_to_all | solution.py:349
  354.8 16.4 %all_gather.3 = bf16[512,262]{1,0:T(8,128)(2,1)S(1)} all-gather(bf16[64,262]{1,0:T(8,128)(2,1)S(1)} %pad_maximum_fusion.5), channel_id=1, replica_groups=mesh['blk'=64,'obs'=8] {'obs'}, dimensions={0}, use_global_device_ids=true | all-gather | bytes 301824 | tf_op jit(solution)/shard_map/all_gather | solution.py:64
  371.5 68.5 %while.46 = (s32[]{:T(128)}, f32[128,128]{0,1:T(8,128)S(1)}, bf16[3,512]{1,0:T(4,128)(2,1)S(1)}, f32[3,128]{1,0:T(4,128)S(1)}, bf16[3,512]{1,0:T(4,128)(2,1)S(1)...) while((s32[]{:T(128)}, f32[128,128]{0,1:T(8,128)S(1)}, ...), condition=%wide.region_46.49_spmd.clone, body=%wide.region_41.48_spmd.clone.sunk | while | flops 16106375 | bytes 1517229 | solution.py:249
  371.9 16.7 %fusion.374 = (f32[64,128]{1,0:T(8,128)S(1)}, f32[64,128]{1,0:T(8,128)S(1)}) fusion(f32[128,64]{1,0:T(8,128)S(1)} %get-tuple-element.1251, f32[128,64]{1,0:T(8,128)S(1)} %get-tuple-element.1252, f32[128,128]{1,0:T(8,128)S(1)} %get-tuple-element.1257, f32[64]{0:T(128)S(1)} %add_multiply_fusion.3, f32[128,64]{1,0:T(8,128)S(1)} %get-tuple-element.1258, ...), kind=kLoop, calls=%fused_computation.61.clone.1 | loop fusion | flops 15712256 | bytes 393472 | tf_op jit(solution)/shard_map/while/body/eval_jaxpr/reduce_sum | solution.py:226
  389.0 16.7 %fusion.374 = (f32[64,128]{1,0:T(8,128)S(1)}, f32[64,128]{1,0:T(8,128)S(1)}) fusion(f32[128,64]{1,0:T(8,128)S(1)} %get-tuple-element.1251, f32[128,64]{1,0:T(8,128)S(1)} %get-tuple-element.1252, f32[128,128]{1,0:T(8,128)S(1)} %get-tuple-element.1257, f32[64]{0:T(128)S(1)} %add_multiply_fusion.3, f32[128,64]{1,0:T(8,128)S(1)} %get-tuple-element.1258, ...), kind=kLoop, calls=%fused_computation.61.clone.1 | loop fusion | flops 15712256 | bytes 393472 | tf_op jit(solution)/shard_map/while/body/eval_jaxpr/reduce_sum | solution.py:226
  406.1 16.7 %fusion.374 = (f32[64,128]{1,0:T(8,128)S(1)}, f32[64,128]{1,0:T(8,128)S(1)}) fusion(f32[128,64]{1,0:T(8,128)S(1)} %get-tuple-element.1251, f32[128,64]{1,0:T(8,128)S(1)} %get-tuple-element.1252, f32[128,128]{1,0:T(8,128)S(1)} %get-tuple-element.1257, f32[64]{0:T(128)S(1)} %add_multiply_fusion.3, f32[128,64]{1,0:T(8,128)S(1)} %get-tuple-element.1258, ...), kind=kLoop, calls=%fused_computation.61.clone.1 | loop fusion | flops 15712256 | bytes 393472 | tf_op jit(solution)/shard_map/while/body/eval_jaxpr/reduce_sum | solution.py:226
  423.3 16.7 %fusion.374 = (f32[64,128]{1,0:T(8,128)S(1)}, f32[64,128]{1,0:T(8,128)S(1)}) fusion(f32[128,64]{1,0:T(8,128)S(1)} %get-tuple-element.1251, f32[128,64]{1,0:T(8,128)S(1)} %get-tuple-element.1252, f32[128,128]{1,0:T(8,128)S(1)} %get-tuple-element.1257, f32[64]{0:T(128)S(1)} %add_multiply_fusion.3, f32[128,64]{1,0:T(8,128)S(1)} %get-tuple-element.1258, ...), kind=kLoop, calls=%fused_computation.61.clone.1 | loop fusion | flops 15712256 | bytes 393472 | tf_op jit(solution)/shard_map/while/body/eval_jaxpr/reduce_sum | solution.py:226
  440.1 17.9 %all_to_all.64 = f32[64,2,128]{2,1,0:T(2,128)S(1)} all-to-all(f32[64,2,128]{2,1,0:T(2,128)S(1)} %bitcast.1430), channel_id=1, replica_groups=mesh['blk'=64,'obs'=8] {'blk'}, dimensions={0} | all-to-all | bytes 131072 | tf_op jit(solution)/shard_map/all_to_all | solution.py:80
  (875 shorter events, 108.3 us)
Async XLA Ops:
  5.9 20.4 %collective-permute-start = (f32[10,1,1024]{2,1,0:T(1,128)S(1)}, f32[10,1,1024]{2,1,0:T(1,128)S(1)}, u32[]{:S(2)}, u32[]{:S(2)}) collective-permute-start(f32[10,1,1024]{2,1,0:T(1,128)S(1)} %get-tuple-element.788), channel_id=1, source_target_pairs={{0,1},{1,2},{2,3},{3,4},{4,5},{5,6},{6,7},{7,0},{8,9},{9,10},{10,1... | collective-permute-start | bytes 122888 | tf_op jit(solution)/shard_map/ppermute | solution.py:53
  8.6 16.8 %collective-permute-start.1 = (f32[10,1,1024]{2,1,0:T(1,128)S(1)}, f32[10,1,1024]{2,1,0:T(1,128)S(1)}, u32[]{:S(2)}, u32[]{:S(2)}) collective-permute-start(f32[10,1,1024]{2,1,0:T(1,128)S(1)} %get-tuple-element.789), channel_id=1, source_target_pairs={{1,0},{2,1},{3,2},{4,3},{5,4},{6,5},{7,6},{0,7},{9,8},{10,9},{11,1... | collective-permute-start | bytes 122888 | tf_op jit(solution)/shard_map/ppermute | solution.py:56
  28.9 19.0 %copy-start.1 = (s32[5]{0:T(128)S(1)}, s32[5]{0:T(128)}, u32[]{:S(2)}) copy-start(s32[5]{0:T(128)} %constant.1311) | copy-start | bytes 64
  28.9 20.5 %copy-start = (s32[5]{0:T(128)S(1)}, s32[5]{0:T(128)}, u32[]{:S(2)}) copy-start(s32[5]{0:T(128)} %constant.1303) | copy-start | bytes 64
  34.2 52.0 %copy-start.8 = (s32[5]{0:T(128)S(1)}, s32[5]{0:T(128)}, u32[]{:S(2)}) copy-start(s32[5]{0:T(128)} %constant.1295) | copy-start | bytes 64
  34.2 56.5 %copy-start.6 = (s32[5]{0:T(128)S(1)}, s32[5]{0:T(128)}, u32[]{:S(2)}) copy-start(s32[5]{0:T(128)} %constant.1315) | copy-start | bytes 64
  34.2 57.9 %copy-start.7 = (s32[5]{0:T(128)S(1)}, s32[5]{0:T(128)}, u32[]{:S(2)}) copy-start(s32[5]{0:T(128)} %constant.1313) | copy-start | bytes 64
  34.2 62.4 %copy-start.3 = (f32[19]{0:T(128)S(1)}, f32[19]{0:T(128)}, u32[]{:S(2)}) copy-start(f32[19]{0:T(128)} %constant.966.clone) | copy-start | bytes 232
  34.2 62.4 %copy-start.4 = (f32[19]{0:T(128)S(1)}, f32[19]{0:T(128)}, u32[]{:S(2)}) copy-start(f32[19]{0:T(128)} %constant.965.clone) | copy-start | bytes 232
  34.2 62.4 %copy-start.5 = (f32[19]{0:T(128)S(1)}, f32[19]{0:T(128)}, u32[]{:S(2)}) copy-start(f32[19]{0:T(128)} %constant.964.clone) | copy-start | bytes 232
  34.2 62.9 %copy-start.9 = (f32[19]{0:T(128)S(1)}, f32[19]{0:T(128)}, u32[]{:S(2)}) copy-start(f32[19]{0:T(128)} %constant.967.clone) | copy-start | bytes 232
  41.4 64.5 %copy-start.11 = (s32[128]{0:T(128)S(1)}, s32[128]{0:T(128)}, u32[]{:S(2)}) copy-start(s32[128]{0:T(128)} %param.143) | copy-start | bytes 1540
  52.7 32.6 %all-to-all-start = ((f32[64,1,960]{2,1,0:T(1,128)}), f32[64,1,960]{2,1,0:T(1,128)S(1)}, u32[]{:S(2)}, u32[]{:S(2)}) async-start(f32[64,1,960]{2,1,0:T(1,128)} %copy.830), calls=%async_computation | async-start | bytes 524288 | tf_op jit(solution)/shard_map/all_to_all | solution.py:175
  98.4 10.5 %collective-permute-start.2 = (f32[10,1,1024]{2,1,0:T(1,128)S(1)}, f32[10,1,1024]{2,1,0:T(1,128)S(1)}, u32[]{:S(2)}, u32[]{:S(2)}) collective-permute-start(f32[10,1,1024]{2,1,0:T(1,128)S(1)} %get-tuple-element.786), channel_id=1, source_target_pairs={{0,1},{1,2},{2,3},{3,4},{4,5},{5,6},{6,7},{7,0},{8,9},{9,10},{10,1... | collective-permute-start | bytes 122888 | tf_op jit(solution)/shard_map/ppermute | solution.py:53
  104.7 3.4 collective-permute-start.3
  135.2 25.6 %all-to-all-start.1 = ((f32[64,1,960]{2,1,0:T(1,128)}), f32[64,1,960]{2,1,0:T(1,128)S(1)}, u32[]{:S(2)}, u32[]{:S(2)}) async-start(f32[64,1,960]{2,1,0:T(1,128)} %copy.853), calls=%async_computation.1 | async-start | bytes 524288 | tf_op jit(solution)/shard_map/all_to_all | solution.py:175
  173.9 6.3 %collective-permute-start.4 = (f32[10,1,1024]{2,1,0:T(1,128)S(1)}, f32[10,1,1024]{2,1,0:T(1,128)S(1)}, u32[]{:S(2)}, u32[]{:S(2)}) collective-permute-start(f32[10,1,1024]{2,1,0:T(1,128)S(1)} %get-tuple-element.784), channel_id=1, source_target_pairs={{0,1},{1,2},{2,3},{3,4},{4,5},{5,6},{6,7},{7,0},{8,9},{9,10},{10,1... | collective-permute-start | bytes 122888 | tf_op jit(solution)/shard_map/ppermute | solution.py:53
  175.9 3.4 collective-permute-start.5
  206.5 24.9 %all-to-all-start.2 = ((f32[64,1,960]{2,1,0:T(1,128)}), f32[64,1,960]{2,1,0:T(1,128)S(1)}, u32[]{:S(2)}, u32[]{:S(2)}) async-start(f32[64,1,960]{2,1,0:T(1,128)} %copy.876), calls=%async_computation.2 | async-start | bytes 524288 | tf_op jit(solution)/shard_map/all_to_all | solution.py:175
  244.5 8.1 %collective-permute-start.6 = (f32[10,1,1024]{2,1,0:T(1,128)S(1)}, f32[10,1,1024]{2,1,0:T(1,128)S(1)}, u32[]{:S(2)}, u32[]{:S(2)}) collective-permute-start(f32[10,1,1024]{2,1,0:T(1,128)S(1)} %get-tuple-element.782), channel_id=1, source_target_pairs={{0,1},{1,2},{2,3},{3,4},{4,5},{5,6},{6,7},{7,0},{8,9},{9,10},{10,1... | collective-permute-start | bytes 122888 | tf_op jit(solution)/shard_map/ppermute | solution.py:53
  248.3 3.4 collective-permute-start.7
  272.4 99.1 %copy-start.2 = (f32[3,128]{1,0:T(4,128)S(1)}, f32[3,128]{1,0:T(4,128)}, u32[]{:S(2)}) copy-start(f32[3,128]{1,0:T(4,128)} %param.149) | copy-start | bytes 4612
  278.4 25.9 %all-to-all-start.3 = ((f32[64,1,960]{2,1,0:T(1,128)}), f32[64,1,960]{2,1,0:T(1,128)S(1)}, u32[]{:S(2)}, u32[]{:S(2)}) async-start(f32[64,1,960]{2,1,0:T(1,128)} %copy.899), calls=%async_computation.3 | async-start | bytes 524288 | tf_op jit(solution)/shard_map/all_to_all | solution.py:175
  304.2 21.5 %all-to-all-start.4 = ((s32[64,1,2]{2,1,0:T(1,128)}), s32[64,1,2]{2,1,0:T(1,128)S(1)}, u32[]{:S(2)}, u32[]{:S(2)}) async-start(s32[64,1,2]{2,1,0:T(1,128)} %bitcast.324), calls=%async_computation.4 | async-start | bytes 65536 | tf_op jit(solution)/shard_map/all_to_all | solution.py:350
  322.1 49.4 %copy-start.10 = (f32[19,4,1024]{2,1,0:T(4,128)}, f32[19,4,1024]{2,1,0:T(4,128)S(1)}, u32[]{:S(2)}) copy-start(f32[19,4,1024]{2,1,0:T(4,128)S(1)} %get-tuple-element.912) | copy-start | bytes 933892
  325.7 28.7 %all-to-all-start.5 = ((bf16[64,2,256]{2,1,0:T(2,128)(2,1)}), bf16[64,2,256]{2,1,0:T(2,128)(2,1)S(1)}, u32[]{:S(2)}, u32[]{:S(2)}) async-start(bf16[64,2,256]{2,1,0:T(2,128)(2,1)} %broadcast_select_fusion), calls=%async_computation.5 | async-start | bytes 131072 | tf_op jit(solution)/shard_map/all_to_all | solution.py:349
where the time goes:
time: 468 us; the launch traced here: 459 us
  local copies, waits for them, and re-layouts  158 us (34%)
  waiting for transfers between devices  94.5 us (20%)
  other arithmetic  94.3 us (20%)
  starting transfers between devices  71.8 us (15%)
  blocking collectives  34.3 us (7%)
    all_to_all x4, waiting for transfers between devices, direct_halo(): lax.all_to_all(place_pieces(outgoing, targets, blocks), 'blk', split_axis...  75.2 us
    reduce_sum x4, other arithmetic, radiate(): real_part = jnp.sum(weight_real * cosine + weight_imag * sine_part, axis=0)  66.7 us
    concatenate x8, local copies, waits for them, and re-layouts, body(): widened = jnp.concatenate([lower_plane, collided, upper_plane], axis=1)  49.6 us
    all_to_all x4, starting transfers between devices, direct_halo(): lax.all_to_all(place_pieces(outgoing, targets, blocks), 'blk', split_axis...  30.7 us
    scatter x32, local copies, waits for them, and re-layouts, spread_pops(): return jnp.zeros(shape, jnp.float32).at[jnp.array(chosen)].set(piece)  18.2 us
    all_to_all x1, blocking collectives, summed_on_arrival(): lax.all_to_all(in_blocks(shard, dim, count), axis, 0, 0, tiled=True)  17.9 us
    all_gather x1, blocking collectives, rows_first(): out, at, done = (lax.all_gather(both, axis, axis=0, tiled=True), 0, [])  16.4 us
    ppermute x4, starting transfers between devices, padded(): lax.ppermute(lax.slice_in_dim(block, block.shape[dim] - width, None, axis...  14.6 us
  transfers between devices with their start and end apart: 14, of which 8 were waited for; matrix products, arithmetic and copies ran while one was open for 8% of the time, Pallas kernels for 0%

commit v1 on v0

v1 whole, which is shorter than its diff:
```python
import functools
import math

import jax
import jax.numpy as jnp
import numpy as np
from jax import lax
from jax.experimental import pallas as pl
from jax.experimental.pallas import tpu as pltpu
from jax.sharding import PartitionSpec as P

BS = 32
STEPS = 4
SAMPLES = 256
BINS = 64
P_OWN = 64
SLAB = 4
CELLS = BS * BS
HALO = 4
PITCH = BS + 2 * HALO
LANES = 1664

VEL = [
    (0, 0, 0),
    (1, 0, 0),
    (-1, 0, 0),
    (0, 1, 0),
    (0, -1, 0),
    (0, 0, 1),
    (0, 0, -1),
    (1, 1, 0),
    (-1, -1, 0),
    (1, -1, 0),
    (-1, 1, 0),
    (1, 0, 1),
    (-1, 0, -1),
    (1, 0, -1),
    (-1, 0, 1),
    (0, 1, 1),
    (0, -1, -1),
    (0, 1, -1),
    (0, -1, 1),
]
WEIGHT = [1.0 / 3.0] + [1.0 / 18.0] * 6 + [1.0 / 36.0] * 12
PAIRS = [(1, 2), (3, 4), (5, 6), (7, 8), (9, 10), (11, 12), (13, 14), (15, 16), (17, 18)]
RELAX = 1.6
GAIN = 60.0
SOUND = 0.5
f32 = jnp.float32
bf16 = jnp.bfloat16

FACE_AXIS = [(1, -1), (1, 1), (2, -1), (2, 1)]


def classes(face):
    axis, sign = FACE_AXIS[face]
    inward = [i for i, v in enumerate(VEL) if v[axis] == sign]
    along = [i for i, v in enumerate(VEL) if v[axis] == 0]
    outward = [i for i, v in enumerate(VEL) if v[axis] == -sign]
    return inward, along, outward


def ext(y, z):
    return (y + HALO) * PITCH + z + HALO


def pick_table():
    out = np.zeros((CELLS, 640), np.float32)
    for d in range(HALO):
        for k in range(BS):
            out[d * BS + k, d * BS + k] = 1
            out[(BS - 1 - d) * BS + k, 128 + d * BS + k] = 1
            out[k * BS + d, 256 + d * BS + k] = 1
            out[k * BS + BS - 1 - d, 384 + d * BS + k] = 1
    for e in range(4):
        for dy in range(HALO):
            for dz in range(HALO):
                y = dy if e < 2 else BS - 1 - dy
                z = dz if e % 2 == 0 else BS - 1 - dz
                lane = e * 16 + dy * HALO + dz
                out[y * BS + z, 512 + lane] = 1
                out[y * BS + z, 512 + 64 + lane] = 1
    return out


def own_table():
    out = np.zeros((CELLS, LANES), np.float32)
    for y in range(BS):
        for z in range(BS):
            out[y * BS + z, ext(y, z)] = 1
    return out


def halo_table():
    out = np.zeros((640, LANES), np.float32)
    for d in range(HALO):
        for k in range(BS):
            out[d * BS + k, ext(BS + d, k)] = 1
            out[128 + d * BS + k, ext(-1 - d, k)] = 1
            out[256 + d * BS + k, ext(k, BS + d)] = 1
            out[384 + d * BS + k, ext(k, -1 - d)] = 1
    for e in range(4):
        for dy in range(HALO):
            for dz in range(HALO):
                y = BS + dy if e < 2 else -1 - dy
                z = BS + dz if e % 2 == 0 else -1 - dz
                lane = e * 16 + dy * HALO + dz
                out[512 + lane, ext(y, z)] = 1
                out[512 + 64 + lane, ext(y, z)] = 1
    return out


def tiles_of(total, step):
    return [(a, min(a + step, total)) for a in range(0, total, step)]


def band(table, lo, hi):
    rows = np.nonzero(table[:, lo:hi].any(axis=1))[0]
    if rows.size == 0:
        return 0, 128
    return int(rows[0]) // 128 * 128, -(-(int(rows[-1]) + 1) // 128) * 128


def transform_table():
    moments = np.arange(SAMPLES)[:, None]
    harmonics = np.arange(BINS)[None, :] + 1
    turns = moments * harmonics % SAMPLES
    phases = turns.astype(np.float32) * np.float32(2.0 * math.pi / SAMPLES)
    table = np.concatenate([np.cos(phases), -np.sin(phases)], axis=1).astype(np.float32)
    return table.astype(jnp.bfloat16)


def collide(fs):
    rho = fs[0]
    for f in fs[1:]:
        rho = rho + f
    speed = []
    for axis in range(3):
        up = [f for f, v in zip(fs, VEL) if v[axis] == 1]
        down = [f for f, v in zip(fs, VEL) if v[axis] == -1]
        speed.append(sum(up[1:], up[0]) - sum(down[1:], down[0]))
    inverse = 1.0 / rho
    speed = [s * inverse for s in speed]
    squared = speed[0] * speed[0] + speed[1] * speed[1] + speed[2] * speed[2]
    base = 1.0 - 1.5 * squared
    out = [None] * 19
    out[0] = (RELAX * WEIGHT[0]) * rho * base + (1.0 - RELAX) * fs[0]
    axis_scale = (RELAX / 18.0) * rho
    diagonal_scale = (RELAX / 36.0) * rho
    for a, b in PAIRS:
        along = None
        for axis in range(3):
            if VEL[a][axis] != 0:
                term = speed[axis]
                if along is None:
                    along = term if VEL[a][axis] == 1 else -term
                else:
                    along = along + term if VEL[a][axis] == 1 else along - term
        scale = axis_scale if a < 7 else diagonal_scale
        even = scale * (base + 4.5 * (along * along))
        odd = scale * (3.0 * along)
        out[a] = even + odd + (1.0 - RELAX) * fs[a]
        out[b] = even - odd + (1.0 - RELAX) * fs[b]
    return out


def pack_kernel(faces, edges, f_ref, pos_ref, nor_ref, pick_ref, c_ref, cb_ref, msg_ref, strip, packed, slots):
    for lo, hi in tiles_of(CELLS, 256):
        fs = [f_ref[0, i, :, lo:hi] for i in range(19)]
        for i, c in enumerate(collide(fs)):
            c_ref[4 * i : 4 * i + 4, lo:hi] = c - WEIGHT[i]
    c_ref[76:80, :] = jnp.zeros((4, CELLS), f32)
    rounded = c_ref[...].astype(bf16)
    cb_ref[...] = rounded
    strip[...] = jnp.dot(rounded, pick_ref[...], preferred_element_type=f32)
    lane4 = lax.broadcasted_iota(jnp.int32, (4, 128), 1)
    for face in range(4):
        inward, along, outward = classes(face)

        def rows(i):
            return strip[4 * i : 4 * i + 4, face * 128 : face * 128 + 128]

        groups = [rows(i) for i in inward] + [rows(i) for i in along]
        last = rows(outward[4])
        groups[5] = jnp.where(lane4 < 96, groups[5], pltpu.roll(last, 96, 1))
        groups[6] = jnp.where(lane4 < 96, groups[6], pltpu.roll(last, 64, 1))
        for a, b in ((0, 1), (2, 3)):
            shifted = pltpu.roll(rows(outward[b]), 64, 1)
            groups.append(jnp.where(lane4 < 64, rows(outward[a]), shifted))
        for g, value in enumerate(groups):
            packed[face * 64 + 4 * g : face * 64 + 4 * g + 4, :] = value
    lane16 = lax.broadcasted_iota(jnp.int32, (16, 128), 1)
    packed[256:320, :] = strip[0:64, 512:640]
    packed[256:272, :] = jnp.where(lane16 < 64, strip[0:16, 512:640], strip[64:80, 512:640])
    for message in range(8):
        source = min(message, 4) * 64
        for r in range(8):
            slots[message * 8 : message * 8 + 8, 128 * r : 128 * r + 128] = packed[
                source + 8 * r : source + 8 * r + 8, :
            ]
    pos = pos_ref[...].astype(f32)
    nor = nor_ref[...].astype(f32)
    pairs = [(pos[0:1], pos[1:2]), (pos[2:3], nor[0:1]), (nor[1:2], nor[2:3])]
    for r, (a, b) in enumerate(pairs):
        row = jnp.concatenate([a, b], axis=1)
        slots[:, 1024 + 128 * r : 1152 + 128 * r] = jnp.broadcast_to(row, (64, 128))
    source_of = [faces[0, 1], faces[0, 0], faces[0, 3], faces[0, 2]]
    source_of += [edges[0, 3], edges[0, 2], edges[0, 1], edges[0, 0]]
    kind = lax.broadcasted_iota(jnp.int32, (64, 128), 0) // 8
    index = jnp.zeros((64, 128), jnp.int32)
    for message in range(8):
        index = jnp.where(kind == message, source_of[message], index)
    slots[:, 1408:1536] = index.astype(f32)
    msg_ref[...] = slots[...].astype(bf16)


def forward_kernel(in_ref, out_ref):
    wanted = in_ref[:, 1408:1472].astype(f32).astype(jnp.int32)
    onehot = wanted == lax.broadcasted_iota(jnp.int32, (64, 64), 1)
    picked = jnp.dot(
        onehot.astype(f32).astype(bf16), in_ref[:, 0:1024], preferred_element_type=f32
    )
    out_ref[...] = picked.astype(bf16)


OWN_ROW, HIGH_ROW = 2, 6


def place_slab(ref, i, slab, value, lanes):
    if slab == 0:
        ref[16 * i + OWN_ROW : 16 * i + OWN_ROW + 4, lanes] = value
    elif slab == 1:
        ref[16 * i + HIGH_ROW : 16 * i + HIGH_ROW + 4, lanes] = value
    else:
        ref[16 * i + 14 : 16 * i + 16, lanes] = value[0:2]
        ref[16 * i : 16 * i + 2, lanes] = value[2:4]


def early_kernel(
    bands, count, c_ref, low_ref, high_ref, geo_ref, owner_ref, hist_ref, table_ref, last_ref,
    *rest,
):
    own_refs, (state, spec, prev, geo, rows) = rest[: len(bands)], rest[len(bands) :]
    low = low_ref[...].astype(f32)
    high = high_ref[...].astype(f32)
    for i in range(19):
        rows[16 * i + 10 : 16 * i + 14, :] = jnp.zeros((4, CELLS), f32)
        place_slab(rows, i, 0, c_ref[4 * i : 4 * i + 4, :], slice(None))
        place_slab(rows, i, -1, low[4 * i : 4 * i + 4], slice(None))
        place_slab(rows, i, 1, high[4 * i : 4 * i + 4], slice(None))
    for (lo, hi, a, b), own_ref in zip(bands, own_refs):
        part = rows[:, a:b]
        coarse = part.astype(bf16)
        fine = (part - coarse.astype(f32)).astype(bf16)
        placed = jnp.dot(coarse, own_ref[...], preferred_element_type=f32)
        placed = placed + jnp.dot(fine, own_ref[...], preferred_element_type=f32)
        state[:, lo:hi] = placed
    nt = (((1,), (1,)), ((), ()))
    spec[0:128, :] = lax.dot_general(table_ref[...], hist_ref[:, 0:256], nt, preferred_element_type=f32)
    spec[128:256, :] = lax.dot_general(table_ref[...], hist_ref[:, 256:512], nt, preferred_element_type=f32)
    prev[...] = lax.dot_general(last_ref[...], hist_ref[:, 0:256], nt, preferred_element_type=f32)
    owner = owner_ref[...]
    step = lax.broadcasted_iota(jnp.int32, (64, 128), 0)
    which = (step == owner // P_OWN).astype(f32).astype(bf16)
    place = (step == owner % P_OWN).astype(f32)
    turned = (((0,), (0,)), ((), ()))
    picked = lax.dot_general(geo_ref[:, 1024:1408], which, turned, preferred_element_type=f32)
    geo[...] = jnp.zeros((16, 128), f32)
    for c in range(6):
        geo[c : c + 1, :] = jnp.sum(picked[64 * c : 64 * c + 64] * place, axis=0, keepdims=True)
    geo[6:7, :] = jnp.full((1, 128), count[0], jnp.int32).astype(f32)


def flow_kernel(
    halo_bands, count, state_ref, own_ref, low_ref, high_ref, cell_ref, spec_ref, prev_ref, geo_ref, late_ref,
    *rest,
):
    halo_refs = rest[: len(halo_bands)]
    out_ref, field_ref, packed, halo, here, there, seen = rest[len(halo_bands) :]
    lane4 = lax.broadcasted_iota(jnp.int32, (4, 128), 1)
    lane64 = lax.broadcasted_iota(jnp.int32, (64, 128), 1)
    for i in range(19):
        halo[16 * i + 10 : 16 * i + 14, :] = jnp.zeros((4, 640), f32)
    for slab, ref in ((0, own_ref), (-1, low_ref), (1, high_ref)):
        for message in range(8):
            value = ref[:, 0:1024].astype(f32)[message * 8 : message * 8 + 8]
            for r in range(8):
                packed[message * 64 + 8 * r : message * 64 + 8 * r + 8, :] = value[:, 128 * r : 128 * r + 128]
        for face in range(4):
            inward, along, outward = classes(face)
            lanes = slice(face * 128, face * 128 + 128)

            def group(g):
                return packed[face * 64 + 4 * g : face * 64 + 4 * g + 4, :]

            for g, i in enumerate(inward + along):
                place_slab(halo, i, slab, group(g), lanes)
            for g, (a, b) in ((14, (0, 1)), (15, (2, 3))):
                place_slab(halo, outward[a], slab, group(g), lanes)
                place_slab(halo, outward[b], slab, pltpu.roll(group(g), 64, 1), lanes)
            last = jnp.where(lane4 < 32, pltpu.roll(group(5), 32, 1), pltpu.roll(group(6), 64, 1))
            place_slab(halo, outward[4], slab, last, lanes)
        corner = packed[256:320, :]
        for e in range(1, 4):
            corner = jnp.where((lane64 % 64) // 16 == e, packed[256 + 64 * e : 320 + 64 * e, :], corner)
        packed[256:320, :] = corner
        for i in range(19):
            rows = packed[256 + 4 * (i % 16) : 260 + 4 * (i % 16), :]
            rows = jnp.where((lane4 < 64) == (i < 16), rows, 0.0)
            place_slab(halo, i, slab, rows, slice(512, 640))
    for (lo, hi, a, b), halo_ref in zip(halo_bands, halo_refs):
        added = jnp.dot(halo[:, a:b].astype(bf16), halo_ref[...], preferred_element_type=f32)
        for i in range(19):
            here[i, :, lo:hi] = state_ref[16 * i : 16 * i + 16, lo:hi] + added[16 * i : 16 * i + 16] + WEIGHT[i]

    lane = lax.broadcasted_iota(jnp.int32, (1, LANES), 1)
    y, z = lane // PITCH - HALO, lane % PITCH - HALO
    inside = (y >= 0) & (y < BS) & (z >= 0) & (z < BS)
    for t in range(STEPS):
        depth_in = 16 if t < 2 else 8
        depth_out = 16 if t < 1 else 8
        for i, (cx, cy, cz) in enumerate(VEL):
            value = here[i, 0:depth_in, :]
            shift = (cy * PITCH + cz) % LANES
            if shift:
                value = pltpu.roll(value, shift, 1)
            if cx:
                value = pltpu.roll(value, cx % depth_in, 0)
            there[i, 0:depth_out, :] = value[0:depth_out]
        total = there[0, 0:8, :]
        for i in range(1, 19):
            total = total + there[i, 0:8, :]
        seen[8 * t : 8 * t + 8, :] = jnp.where(inside, total - 1.0, 0.0)
        if t < STEPS - 1:

            def one(c, _):
                at = pl.ds(pl.multiple_of(c * 128, 128), 128)
                for i, value in enumerate(collide([there[i, 0:depth_out, at] for i in range(19)])):
                    here[i, 0:depth_out, at] = value
                return 0

            lax.fori_loop(0, LANES // 128, one, 0)
    for i in range(19):
        field_ref[8 * i : 8 * i + 8, :] = jnp.where(inside, there[i, 0:8, :], 0.0)

    cell = cell_ref[...]
    across = cell % CELLS
    spot = (across // BS + HALO) * PITCH + across % BS + HALO
    onehot = (lax.broadcasted_iota(jnp.int32, (LANES, 128), 0) == spot).astype(f32).astype(bf16)
    rest_of = seen[...]
    read = jnp.zeros((8 * STEPS, 128), f32)
    for _ in range(3):
        piece = rest_of.astype(bf16)
        read = read + jnp.dot(piece, onehot, preferred_element_type=f32)
        rest_of = rest_of - piece.astype(f32)
    before = prev_ref[0:1, :]
    press, rate = [], []
    for t in range(STEPS):
        value = jnp.zeros((1, 128), f32)
        for x in range(SLAB):
            row = 8 * t + OWN_ROW + x
            value = jnp.where(cell // CELLS == x, read[row : row + 1], value)
        value = GAIN * value
        press.append(value.astype(bf16).astype(f32))
        rate.append((value - before).astype(bf16).astype(f32))
        before = value
    alive = lax.broadcasted_iota(jnp.int32, (1, 128), 1) < count[0]
    for g, late in ((0, press), (1, rate)):
        total = spec_ref[128 * g : 128 * g + 128, :]
        for t in range(STEPS):
            total = total + late_ref[:, t : t + 1] * late[t]
        out_ref[128 * g : 128 * g + 128, :] = jnp.where(alive, total, 0.0).astype(bf16)
    out_ref[256:272, :] = geo_ref[...].astype(bf16)


def field_kernel(bands, field_ref, *rest):
    own_refs, (out_ref,) = rest[: len(bands)], rest[len(bands) :]
    for (lo, hi, a, b), own_ref in zip(bands, own_refs):
        part = field_ref[:, a:b]
        coarse = part.astype(bf16)
        fine = (part - coarse.astype(f32)).astype(bf16)
        value = jnp.dot(coarse, own_ref[...], preferred_element_type=f32)
        value = value + jnp.dot(fine, own_ref[...], preferred_element_type=f32)
        for i in range(19):
            out_ref[0, i, :, lo:hi] = value[8 * i + OWN_ROW : 8 * i + OWN_ROW + 4]


def radiate_kernel(all_ref, listen_ref, out_ref, rows, spots, sums, turned):
    base = jnp.zeros((1, 128), f32)
    lane_f = lax.broadcasted_iota(jnp.int32, (128, 1024), 1).astype(f32)
    slot_f = lax.broadcasted_iota(jnp.int32, (128, 1024), 0).astype(f32)
    for o in range(8):
        live = all_ref[o, 256:272, :].astype(f32)[6:7]
        here = (lane_f - base[:, 0:1] == slot_f) & (slot_f < live[:, 0:1])
        part = jnp.dot(all_ref[o], here.astype(f32).astype(bf16), preferred_element_type=f32)
        if o == 0:
            rows[...] = part
        else:
            rows[...] += part
        base = base + live
    used = jnp.max(base).astype(jnp.int32)
    for axis in range(3):
        row = listen_ref[axis : axis + 1, :]
        spots[axis] = jnp.broadcast_to(row, (128, 128)).T
    sums[...] = jnp.zeros((128, 128, 128), f32)

    def panels(p, _):
        at = pl.ds(pl.multiple_of(p * 128, 128), 128)

        def listeners(m, _):
            ears = pl.ds(pl.multiple_of(m * 16, 16), 16)
            distance_sq = jnp.zeros((16, 128), f32)
            facing = jnp.zeros((16, 128), f32)
            for axis in range(3):
                offset = spots[axis, ears, :] - rows[256 + axis : 257 + axis, at]
                distance_sq = distance_sq + offset * offset
                facing = facing + rows[259 + axis : 260 + axis, at] * offset
            distance = jnp.sqrt(distance_sq)
            far = facing / (4.0 * math.pi * SOUND * distance_sq)
            ratio = SOUND / distance
            angle = (2.0 * math.pi / SAMPLES) * (distance / SOUND)
            cosine = jnp.cos(angle)
            double = cosine + cosine
            c_before, s_before = far, jnp.zeros((16, 128), f32)
            c_now, s_now = far * cosine, far * jnp.sin(angle)
            for k in range(BINS):
                weight_real = rows[128 + k : 129 + k, at] + ratio * rows[k : k + 1, at]
                weight_imag = rows[192 + k : 193 + k, at] + ratio * rows[64 + k : 65 + k, at]
                sums[k, ears, :] += weight_real * c_now + weight_imag * s_now
                sums[BINS + k, ears, :] += weight_imag * c_now - weight_real * s_now
                if k < BINS - 1:
                    c_now, c_before = double * c_now - c_before, c_now
                    s_now, s_before = double * s_now - s_before, s_now
            return 0

        lax.fori_loop(0, 8, listeners, 0)
        return 0

    lax.fori_loop(0, (used + 127) // 128, panels, 0)

    column = lax.broadcasted_iota(jnp.int32, (128, 128), 1)
    turned[...] = jnp.zeros((128, 128), f32)

    def fold(k, _):
        pick = (column == k).astype(f32).astype(bf16)
        value = sums[k]
        coarse = value.astype(bf16)
        fine = (value - coarse.astype(f32)).astype(bf16)
        turned[...] += jnp.dot(coarse, pick, preferred_element_type=f32) + jnp.dot(
            fine, pick, preferred_element_type=f32
        )
        return 0

    lax.fori_loop(0, 128, fold, 0)
    out_ref[...] = turned[...]


def call(kernel, outs, operands, scratch=(), scalars=0, megabytes=32, flops=0):
    smem = pl.BlockSpec(memory_space=pltpu.SMEM)
    vmem = pl.BlockSpec(memory_space=pltpu.VMEM)
    return pl.pallas_call(
        kernel,
        out_shape=tuple(jax.ShapeDtypeStruct(s, d) for s, d in outs),
        in_specs=[smem] * scalars + [vmem] * (len(operands) - scalars),
        out_specs=tuple(vmem for _ in outs),
        scratch_shapes=[pltpu.VMEM(s, f32) for s in scratch],
        compiler_params=pltpu.CompilerParams(vmem_limit_bytes=megabytes * 2**20),
        cost_estimate=pl.CostEstimate(flops=flops, bytes_accessed=2**20, transcendentals=0),
    )(*operands)


def body(
    populations,
    block_faces,
    block_edges,
    probe_cell,
    history,
    panel_count,
    panel_owner,
    panel_pos,
    panel_normal,
    observers,
):
    own = own_table()
    around = halo_table()
    bands = [(lo, hi, *band(own, lo, hi)) for lo, hi in tiles_of(LANES, 256)]
    halo_bands = [(lo, hi, *band(around, lo, hi)) for lo, hi in tiles_of(LANES, 256)]
    back = own.T
    back_bands = [(lo, hi, *band(back, lo, hi)) for lo, hi in tiles_of(CELLS, 256)]

    def cut(table, ranges):
        return [jnp.asarray(table[a:b, lo:hi].astype(jnp.bfloat16)) for lo, hi, a, b in ranges]

    table = transform_table()
    shifted = np.concatenate([np.zeros((STEPS, 128), table.dtype), table[: SAMPLES - STEPS]]).T
    late = np.zeros((128, 128), np.float32)
    late[:, :STEPS] = table[SAMPLES - STEPS :].astype(np.float32).T
    newest = np.zeros((16, SAMPLES), np.float32)
    newest[0, SAMPLES - 1] = 1

    pick = jnp.asarray(pick_table().astype(jnp.bfloat16))
    collided, rounded, message = call(
        pack_kernel,
        [((80, CELLS), f32), ((80, CELLS), bf16), ((64, 1536), bf16)],
        [block_faces, block_edges, populations, panel_pos, panel_normal, pick],
        scratch=[(80, 640), (320, 128), (64, 1536)],
        scalars=2,
    )
    ring = lax.axis_size("obs")
    up = [(i, (i + 1) % ring) for i in range(ring)]
    down = [(i, (i - 1) % ring) for i in range(ring)]

    def beside(value):
        return lax.ppermute(value, "obs", up), lax.ppermute(value, "obs", down)

    low, high = beside(rounded)
    spread = lax.all_to_all(message, "blk", 0, 0, tiled=True)
    (sent,) = call(forward_kernel, [((64, 1024), bf16)], [spread])
    arrived = lax.all_to_all(sent, "blk", 0, 0, tiled=True)
    state, spec, prev, geo = call(
        functools.partial(early_kernel, bands),
        [((304, LANES), f32), ((256, 128), f32), ((16, 128), f32), ((16, 128), f32)],
        [
            panel_count, collided, low, high, spread, panel_owner.reshape(1, 128), history,
            jnp.asarray(shifted), jnp.asarray(newest.astype(jnp.bfloat16)), *cut(own, bands),
        ],
        scratch=[(304, CELLS)],
        scalars=1,
        flops=10**9,
    )
    arrived_low, arrived_high = beside(arrived)
    payload, field = call(
        functools.partial(flow_kernel, halo_bands),
        [((272, 128), bf16), ((152, LANES), f32)],
        [
            panel_count, state, arrived, arrived_low, arrived_high, probe_cell.reshape(1, 128), spec, prev,
            geo, jnp.asarray(late), *cut(around, halo_bands),
        ],
        scratch=[(512, 128), (304, 640), (19, 16, LANES), (19, 16, LANES), (32, LANES)],
        scalars=1,
    )
    (populations_out,) = call(
        functools.partial(field_kernel, back_bands),
        [((1, 19, SLAB, CELLS), f32)],
        [field, *cut(back, back_bands)],
        flops=10**9,
    )
    gathered = lax.all_gather(payload, "obs", axis=0, tiled=False)
    (partial_value,) = call(
        radiate_kernel,
        [((128, 128), f32)],
        [gathered, observers],
        scratch=[(272, 1024), (3, 128, 128), (128, 128, 128), (128, 128)],
        megabytes=48,
    )
    pieces = lax.all_to_all(partial_value.reshape(64, 256), "blk", 0, 0, tiled=True)
    summed = jnp.sum(pieces, axis=0)
    return (populations_out, summed.reshape(1, 2, 2 * BINS))


def solution(mesh):
    placed = (
        P("blk", None, "obs", None),
        P("blk", None),
        P("blk", None),
        P(("blk", "obs")),
        P(("blk", "obs"), None),
        P(("blk", "obs")),
        P(("blk", "obs")),
        P(None, ("blk", "obs")),
        P(None, ("blk", "obs")),
        P(None, "obs"),
    )
    return jax.shard_map(
        body,
        mesh=mesh,
        in_specs=placed,
        out_specs=(P("blk", None, "obs", None), P("obs", "blk", None)),
        check_vma=False,
    )
```

time: 468 us -> 152 us (0.32); the launches traced: 459 us -> 152 us
  local copies, waits for them, and re-layouts: 158 us -> 6.71 us
  other arithmetic: 94.3 us -> 2.06 us
  waiting for transfers between devices: 94.5 us -> 26 us
  starting transfers between devices: 71.8 us -> 20.5 us
  Pallas kernels: 0 us -> 44 us
  blocking collectives: 34.3 us -> 51 us
    reduce_sum x20 -> x1, other arithmetic: 71.6 us -> 0.66 us  [body(): summed = jnp.sum(pieces, axis=0)]
    all_to_all x6 -> x2, waiting for transfers between devices: 88.9 us -> 24.9 us  [the longest x1 12.9 us: body(): lax.all_to_all(partial_value.reshape(64, 256), 'blk', 0, 0, tiled=True)]
    concatenate x28 -> x0, local copies, waits for them, and re-layouts: 50.8 us -> none  [the longest x8 49.6 us: body(): widened = jnp.concatenate([lower_plane, collided, upper_plane], axis=1)]
    gather x48 -> x0, local copies, waits for them, and re-layouts: 47.4 us -> none  [the longest x8 11.2 us: direct_halo(): widened[jnp.array(z_upward), :, BS - 1::BS]]
    pallas_call x0 -> x6, Pallas kernels: none -> 44 us  [call(): pl.pallas_call(kernel, out_shape=tuple((jax.ShapeDtypeStruct(s, d) for s,...]
    all_to_all x6 -> x2, starting transfers between devices: 51.9 us -> 12.8 us  [the longest x1 6.61 us: body(): arrived = lax.all_to_all(sent, 'blk', 0, 0, tiled=True)]
    all_to_all x1, blocking collectives: 17.9 us -> 36.4 us  [body(): spread = lax.all_to_all(message, 'blk', 0, 0, tiled=True)]
    scatter x48 -> x0, local copies, waits for them, and re-layouts: 18.3 us -> none  [the longest x32 18.2 us: spread_pops(): return jnp.zeros(shape, jnp.float32).at[jnp.array(chosen)].set(piece)]
  transfers between devices with their start and end apart: 14 -> 6, of which waited for: 8 -> 3; matrix products, arithmetic and copies ran while one was open for 8% -> 0% of each run, Pallas kernels for 0% -> 1%
where the time goes in v1:
time: 152 us
  blocking collectives  51 us (34%)
  Pallas kernels  44 us (29%)
  waiting for transfers between devices  26 us (17%)
  starting transfers between devices  20.5 us (13%)
  local copies, waits for them, and re-layouts  6.71 us (4%)
  other arithmetic  2.06 us (1%)
  between operations  1.73 us (1%)
    pallas_call x6, Pallas kernels, call(): pl.pallas_call(kernel, out_shape=tuple((jax.ShapeDtypeStruct(s, d) for s,...  44 us
    all_to_all x1, blocking collectives, body(): spread = lax.all_to_all(message, 'blk', 0, 0, tiled=True)  36.4 us
    all_gather x1, blocking collectives, body(): gathered = lax.all_gather(payload, 'obs', axis=0, tiled=False)  14.6 us
    all_to_all x1, waiting for transfers between devices, body(): lax.all_to_all(partial_value.reshape(64, 256), 'blk', 0, 0, tiled=True)  12.9 us
    all_to_all x1, waiting for transfers between devices, body(): arrived = lax.all_to_all(sent, 'blk', 0, 0, tiled=True)  12 us
    ppermute x4, starting transfers between devices, beside(): return (lax.ppermute(value, 'obs', up), lax.ppermute(value, 'obs', down))  7.76 us
    all_to_all x1, starting transfers between devices, body(): arrived = lax.all_to_all(sent, 'blk', 0, 0, tiled=True)  6.61 us
    unnamed x62, local copies, waits for them, and re-layouts  6.19 us
  transfers between devices with their start and end apart: 6, of which 3 were waited for; matrix products, arithmetic and copies ran while one was open for 0% of the time, Pallas kernels for 1%

profile of v1, /device:TPU:1, one launch (start us, length us, event | category | flops | bytes accessed | tf_op | source)
XLA Modules:
  0.0 151.9 jit_solution(548388519876286598)
XLA Ops:
  0.6 0.0 copy-start
  0.6 1.3 copy-done
  2.0 1.0 copy-done.2
  2.9 0.7 copy-done.11
  3.6 0.7 copy-done.12
  4.3 0.7 copy-done.13
  4.9 0.7 copy-done.14
  5.6 1.0 shard_map.311
  6.6 0.5 broadcast
  7.1 0.7 reduce.1
  7.9 0.0 copy-start.20
  7.9 0.0 copy-start.21
  7.9 0.0 copy-start.22
  7.9 0.0 copy-start.23
  8.0 0.0 copy-start.25
  8.0 0.0 copy-start.26
  8.0 0.0 copy-start.27
  8.0 0.1 reshape.25
  8.0 36.4 %all_to_all.31 = bf16[64,2,768]{2,1,0:T(2,128)(2,1)S(1)} all-to-all(bf16[64,2,768]{2,1,0:T(2,128)(2,1)S(1)} %reshape.25), channel_id=1, replica_groups=mesh['blk'=64,'obs'=8] {'blk'}, dimensions={0} | all-to-all | bytes 393216 | tf_op jit(solution)/shard_map/all_to_all | solution.py:517
  44.5 0.1 reshape.26
  44.7 0.2 shard_map.313
  44.8 0.7 reduce.2
  45.5 0.7 reshape.27
  46.2 6.6 %all-to-all-start.1 = ((bf16[64,2,512]{2,1,0:T(2,128)(2,1)}), bf16[64,2,512]{2,1,0:T(2,128)(2,1)S(1)}, u32[]{:S(2)}, u32[]{:S(2)}) async-start(bf16[64,2,512]{2,1,0:T(2,128)(2,1)} %reshape.27), calls=%async_computation.1 | async-start | bytes 262144 | tf_op jit(solution)/shard_map/all_to_all | solution.py:519
  52.9 2.0 %collective-permute-start.1 = (bf16[80,1024]{1,0:T(8,128)(2,1)S(1)}, bf16[80,1024]{1,0:T(8,128)(2,1)S(1)}, u32[]{:S(2)}, u32[]{:S(2)}) collective-permute-start(bf16[80,1024]{1,0:T(8,128)(2,1)S(1)} %get-tuple-element.12), channel_id=1, source_target_pairs={{0,7},{1,0},{2,1},{3,2},{4,3},{5,4},{6,5},{7,6},{8,15},{9,8},{10,9... | collective-permute-start | bytes 491528 | tf_op jit(solution)/shard_map/ppermute | solution.py:514
  54.8 1.1 collective-permute-start
  55.9 12.0 %all-to-all-done.1 = bf16[64,2,512]{2,1,0:T(2,128)(2,1)S(1)} async-done(((bf16[64,2,512]{2,1,0:T(2,128)(2,1)}), bf16[64,2,512]{2,1,0:T(2,128)(2,1)S(1)}, u32[]{:S(2)}, u32[]{:S(2)}) %all-to-all-start.1) | async-done | bytes 131104 | tf_op jit(solution)/shard_map/all_to_all | solution.py:519
  67.9 0.1 reshape.28
  68.0 0.0 copy-start.1
  68.0 0.0 copy-start.3
  68.1 0.0 copy-start.5
  68.1 0.0 copy-start.6
  68.1 0.0 copy-start.7
  68.1 0.0 copy-start.8
  68.1 0.0 copy-start.9
  68.2 3.6 %collective-permute-start.3 = (bf16[64,1024]{1,0:T(8,128)(2,1)S(1)}, bf16[64,1024]{1,0:T(8,128)(2,1)S(1)}, u32[]{:S(2)}, u32[]{:S(2)}) collective-permute-start(bf16[64,1024]{1,0:T(8,128)(2,1)S(1)} %bitcast.16), channel_id=1, source_target_pairs={{0,7},{1,0},{2,1},{3,2},{4,3},{5,4},{6,5},{7,6},{8,15},{9,8},{10,9... | collective-permute-start | bytes 393224 | tf_op jit(solution)/shard_map/ppermute | solution.py:514
  71.8 1.1 collective-permute-start.2
  73.7 1.0 shard_map.312
  74.7 1.1 collective-permute-done.3.high_ref
  75.9 0.0 copy-start.18
  75.9 0.0 copy-start.19
  75.9 4.3 %shard_map.314 = (bf16[272,128]{1,0:T(8,128)(2,1)S(1)}, f32[152,1664]{1,0:T(8,128)S(1)}) custom-call(s32[1]{0:T(128)S(6)} %copy.48.count, f32[304,1664]{1,0:T(8,128)S(1)} %get-tuple-element.14.state_ref, bf16[64,1024]{1,0:T(8,128)(2,1)S(1)} %bitcast.18, bf16[64,1024]{1,0:T(8,128)(2,1)S(1)} %collective-permute-done.2.low_ref, ...), custom_call_target="tpu_custom_call" | custom-call | bytes 1048576 | tf_op jit(solution)/shard_map/pallas_call | solution.py:461
  80.3 14.6 %all-gather = bf16[2176,128]{1,0:T(8,128)(2,1)S(1)} all-gather(bf16[272,128]{1,0:T(8,128)(2,1)S(1)} %get-tuple-element.19), channel_id=2, replica_groups=mesh['blk'=64,'obs'=8] {'obs'}, dimensions={0}, use_global_device_ids=true | all-gather | bytes 626688 | tf_op jit(solution)/shard_map/all_gather | solution.py:548
  94.8 36.2 %shard_map.316 = f32[128,128]{1,0:T(8,128)} custom-call(bf16[8,272,128]{2,1,0:T(8,128)(2,1)S(1)} %bitcast.13, f32[3,128]{1,0:T(4,128)S(1)} %copy-done.10), custom_call_target="tpu_custom_call" | custom-call | bytes 1048576 | tf_op jit(solution)/shard_map/pallas_call | solution.py:461
  131.0 6.1 %all-to-all-start.2 = ((f32[64,1,256]{2,1,0:T(1,128)}), f32[64,1,256]{2,1,0:T(1,128)S(1)}, u32[]{:S(2)}, u32[]{:S(2)}) async-start(f32[64,1,256]{2,1,0:T(1,128)} %bitcast.5), calls=%async_computation.2 | async-start | bytes 131072 | tf_op jit(solution)/shard_map/all_to_all | solution.py:556
  137.2 1.3 shard_map.315
  138.4 12.9 %all-to-all-done.2 = f32[64,1,256]{2,1,0:T(1,128)S(1)} async-done(((f32[64,1,256]{2,1,0:T(1,128)}), f32[64,1,256]{2,1,0:T(1,128)S(1)}, u32[]{:S(2)}, u32[]{:S(2)}) %all-to-all-start.2) | async-done | bytes 65568 | tf_op jit(solution)/shard_map/all_to_all | solution.py:556
  151.3 0.7 reduce_sum.9
  (39 shorter events, 0.2 us)
Async XLA Ops:
  0.6 1.3 copy-start
  2.0 1.0 copy-start.2
  2.9 0.7 copy-start.11
  3.6 0.7 copy-start.12
  4.3 0.7 copy-start.13
  4.9 0.7 copy-start.14
  7.9 65.7 %copy-start.16 = (bf16[128,512]{1,0:T(8,128)(2,1)S(1)}, bf16[128,512]{1,0:T(8,128)(2,1)}, u32[]{:S(2)}) copy-start(bf16[128,512]{1,0:T(8,128)(2,1)} %hist_ref.1) | copy-start | bytes 393220
  7.9 65.7 %copy-start.17 = (s32[128]{0:T(128)S(1)}, s32[128]{0:T(128)}, u32[]{:S(2)}) copy-start(s32[128]{0:T(128)} %param.38) | copy-start | bytes 1540
  7.9 65.7 %copy-start.20 = (bf16[384,256]{1,0:T(8,128)(2,1)S(1)}, bf16[384,256]{1,0:T(8,128)(2,1)}, u32[]{:S(2)}) copy-start(bf16[384,256]{1,0:T(8,128)(2,1)} %constant.48.clone.rest_3_) | copy-start | bytes 589828
  7.9 65.7 %copy-start.21 = (bf16[384,256]{1,0:T(8,128)(2,1)S(1)}, bf16[384,256]{1,0:T(8,128)(2,1)}, u32[]{:S(2)}) copy-start(bf16[384,256]{1,0:T(8,128)(2,1)} %constant.46.clone.rest_1_) | copy-start | bytes 589828
  7.9 65.7 %copy-start.22 = (bf16[256,256]{1,0:T(8,128)(2,1)S(1)}, bf16[256,256]{1,0:T(8,128)(2,1)}, u32[]{:S(2)}) copy-start(bf16[256,256]{1,0:T(8,128)(2,1)} %constant.49.clone.rest_4_) | copy-start | bytes 393220
  7.9 65.7 %copy-start.23 = (bf16[256,256]{1,0:T(8,128)(2,1)S(1)}, bf16[256,256]{1,0:T(8,128)(2,1)}, u32[]{:S(2)}) copy-start(bf16[256,256]{1,0:T(8,128)(2,1)} %constant.47.clone.rest_2_) | copy-start | bytes 393220
  7.9 65.7 %copy-start.24 = (bf16[128,256]{1,0:T(8,128)(2,1)S(1)}, bf16[128,256]{1,0:T(8,128)(2,1)}, u32[]{:S(2)}) copy-start(bf16[128,256]{1,0:T(8,128)(2,1)} %constant.50.clone.rest_5_) | copy-start | bytes 196612
  8.0 65.7 %copy-start.25 = (bf16[128,256]{1,0:T(8,128)(2,1)S(1)}, bf16[128,256]{1,0:T(8,128)(2,1)}, u32[]{:S(2)}) copy-start(bf16[128,256]{1,0:T(8,128)(2,1)} %constant.45.clone.rest_0_) | copy-start | bytes 196612
  8.0 65.7 %copy-start.26 = (bf16[128,256]{1,0:T(8,128)(2,1)S(1)}, bf16[128,256]{1,0:T(8,128)(2,1)}, u32[]{:S(2)}) copy-start(bf16[128,256]{1,0:T(8,128)(2,1)} %constant.43.clone.table_ref) | copy-start | bytes 196612
  8.0 65.7 %copy-start.27 = (bf16[16,256]{1,0:T(8,128)(2,1)S(1)}, bf16[16,256]{1,0:T(8,128)(2,1)}, u32[]{:S(2)}) copy-start(bf16[16,256]{1,0:T(8,128)(2,1)} %constant.44.clone.last_ref) | copy-start | bytes 24580
  46.2 21.7 %all-to-all-start.1 = ((bf16[64,2,512]{2,1,0:T(2,128)(2,1)}), bf16[64,2,512]{2,1,0:T(2,128)(2,1)S(1)}, u32[]{:S(2)}, u32[]{:S(2)}) async-start(bf16[64,2,512]{2,1,0:T(2,128)(2,1)} %reshape.27), calls=%async_computation.1 | async-start | bytes 262144 | tf_op jit(solution)/shard_map/all_to_all | solution.py:519
  52.9 20.7 %collective-permute-start.1 = (bf16[80,1024]{1,0:T(8,128)(2,1)S(1)}, bf16[80,1024]{1,0:T(8,128)(2,1)S(1)}, u32[]{:S(2)}, u32[]{:S(2)}) collective-permute-start(bf16[80,1024]{1,0:T(8,128)(2,1)S(1)} %get-tuple-element.12), channel_id=1, source_target_pairs={{0,7},{1,0},{2,1},{3,2},{4,3},{5,4},{6,5},{7,6},{8,15},{9,8},{10,9... | collective-permute-start | bytes 491528 | tf_op jit(solution)/shard_map/ppermute | solution.py:514
  54.8 18.7 %collective-permute-start = (bf16[80,1024]{1,0:T(8,128)(2,1)S(1)}, bf16[80,1024]{1,0:T(8,128)(2,1)S(1)}, u32[]{:S(2)}, u32[]{:S(2)}) collective-permute-start(bf16[80,1024]{1,0:T(8,128)(2,1)S(1)} %get-tuple-element.12), channel_id=1, source_target_pairs={{0,1},{1,2},{2,3},{3,4},{4,5},{5,6},{6,7},{7,0},{8,9},{9,10},{10,1... | collective-permute-start | bytes 491528 | tf_op jit(solution)/shard_map/ppermute | solution.py:514
  68.0 7.8 %copy-start.1 = (bf16[640,256]{1,0:T(8,128)(2,1)S(1)}, bf16[640,256]{1,0:T(8,128)(2,1)}, u32[]{:S(2)}) copy-start(bf16[640,256]{1,0:T(8,128)(2,1)} %constant.58.clone.rest_5_) | copy-start | bytes 983044
  68.0 7.8 %copy-start.3 = (bf16[512,256]{1,0:T(8,128)(2,1)S(1)}, bf16[512,256]{1,0:T(8,128)(2,1)}, u32[]{:S(2)}) copy-start(bf16[512,256]{1,0:T(8,128)(2,1)} %constant.53.clone.rest_0_) | copy-start | bytes 786436
  68.1 7.8 %copy-start.4 = (bf16[640,128]{1,0:T(8,128)(2,1)S(1)}, bf16[640,128]{1,0:T(8,128)(2,1)}, u32[]{:S(2)}) copy-start(bf16[640,128]{1,0:T(8,128)(2,1)} %constant.59.clone.rest_6_) | copy-start | bytes 491524
  68.1 7.8 %copy-start.5 = (bf16[256,256]{1,0:T(8,128)(2,1)S(1)}, bf16[256,256]{1,0:T(8,128)(2,1)}, u32[]{:S(2)}) copy-start(bf16[256,256]{1,0:T(8,128)(2,1)} %constant.57.clone.rest_4_) | copy-start | bytes 393220
  68.1 7.8 %copy-start.6 = (bf16[256,256]{1,0:T(8,128)(2,1)S(1)}, bf16[256,256]{1,0:T(8,128)(2,1)}, u32[]{:S(2)}) copy-start(bf16[256,256]{1,0:T(8,128)(2,1)} %constant.56.clone.rest_3_) | copy-start | bytes 393220
  68.1 7.8 %copy-start.7 = (bf16[256,256]{1,0:T(8,128)(2,1)S(1)}, bf16[256,256]{1,0:T(8,128)(2,1)}, u32[]{:S(2)}) copy-start(bf16[256,256]{1,0:T(8,128)(2,1)} %constant.55.clone.rest_2_) | copy-start | bytes 393220
  68.1 7.8 %copy-start.8 = (bf16[256,256]{1,0:T(8,128)(2,1)S(1)}, bf16[256,256]{1,0:T(8,128)(2,1)}, u32[]{:S(2)}) copy-start(bf16[256,256]{1,0:T(8,128)(2,1)} %constant.54.clone.rest_1_) | copy-start | bytes 393220
  68.1 7.7 %copy-start.9 = (f32[128,128]{1,0:T(8,128)S(1)}, f32[128,128]{1,0:T(8,128)}, u32[]{:S(2)}) copy-start(f32[128,128]{1,0:T(8,128)} %constant.52.clone.late_ref) | copy-start | bytes 196612
  68.1 7.7 %copy-start.15 = (s32[128]{0:T(128)S(1)}, s32[128]{0:T(128)}, u32[]{:S(2)}) copy-start(s32[128]{0:T(128)} %param.35) | copy-start | bytes 1540
  68.2 7.6 %collective-permute-start.3 = (bf16[64,1024]{1,0:T(8,128)(2,1)S(1)}, bf16[64,1024]{1,0:T(8,128)(2,1)S(1)}, u32[]{:S(2)}, u32[]{:S(2)}) collective-permute-start(bf16[64,1024]{1,0:T(8,128)(2,1)S(1)} %bitcast.16), channel_id=1, source_target_pairs={{0,7},{1,0},{2,1},{3,2},{4,3},{5,4},{6,5},{7,6},{8,15},{9,8},{10,9... | collective-permute-start | bytes 393224 | tf_op jit(solution)/shard_map/ppermute | solution.py:514
  71.8 4.0 %collective-permute-start.2 = (bf16[64,1024]{1,0:T(8,128)(2,1)S(1)}, bf16[64,1024]{1,0:T(8,128)(2,1)S(1)}, u32[]{:S(2)}, u32[]{:S(2)}) collective-permute-start(bf16[64,1024]{1,0:T(8,128)(2,1)S(1)} %bitcast.17), channel_id=1, source_target_pairs={{0,1},{1,2},{2,3},{3,4},{4,5},{5,6},{6,7},{7,0},{8,9},{9,10},{10,1... | collective-permute-start | bytes 393224 | tf_op jit(solution)/shard_map/ppermute | solution.py:514
  75.9 18.9 %copy-start.10 = (f32[3,128]{1,0:T(4,128)S(1)}, f32[3,128]{1,0:T(4,128)}, u32[]{:S(2)}) copy-start(f32[3,128]{1,0:T(4,128)} %listen_ref.1) | copy-start | bytes 4612
  75.9 61.3 %copy-start.18 = (bf16[512,256]{1,0:T(8,128)(2,1)S(1)}, bf16[512,256]{1,0:T(8,128)(2,1)}, u32[]{:S(2)}) copy-start(bf16[512,256]{1,0:T(8,128)(2,1)} %constant.61.clone.rest_1_.rest_3_) | copy-start | bytes 786436
  75.9 61.3 %copy-start.19 = (bf16[384,256]{1,0:T(8,128)(2,1)S(1)}, bf16[384,256]{1,0:T(8,128)(2,1)}, u32[]{:S(2)}) copy-start(bf16[384,256]{1,0:T(8,128)(2,1)} %constant.60.clone.rest_0_.rest_2_) | copy-start | bytes 589828
  131.0 20.3 %all-to-all-start.2 = ((f32[64,1,256]{2,1,0:T(1,128)}), f32[64,1,256]{2,1,0:T(1,128)S(1)}, u32[]{:S(2)}, u32[]{:S(2)}) async-start(f32[64,1,256]{2,1,0:T(1,128)} %bitcast.5), calls=%async_computation.2 | async-start | bytes 131072 | tf_op jit(solution)/shard_map/all_to_all | solution.py:556

commit v2 on v1

--- a/solution.py
+++ b/solution.py
@@ -62,25 +62,6 @@
 
 def ext(y, z):
     return (y + HALO) * PITCH + z + HALO
-
-
-def pick_table():
-    out = np.zeros((CELLS, 640), np.float32)
-    for d in range(HALO):
-        for k in range(BS):
-            out[d * BS + k, d * BS + k] = 1
-            out[(BS - 1 - d) * BS + k, 128 + d * BS + k] = 1
-            out[k * BS + d, 256 + d * BS + k] = 1
-            out[k * BS + BS - 1 - d, 384 + d * BS + k] = 1
-    for e in range(4):
-        for dy in range(HALO):
-            for dz in range(HALO):
-                y = dy if e < 2 else BS - 1 - dy
-                z = dz if e % 2 == 0 else BS - 1 - dz
-                lane = e * 16 + dy * HALO + dz
-                out[y * BS + z, 512 + lane] = 1
-                out[y * BS + z, 512 + 64 + lane] = 1
-    return out
 
 
 def own_table():
@@ -164,7 +145,25 @@
     return out
 
 
-def pack_kernel(faces, edges, f_ref, pos_ref, nor_ref, pick_ref, c_ref, cb_ref, msg_ref, strip, packed, slots):
+def strip_rows():
+    lane = lax.broadcasted_iota(jnp.int32, (1, 128), 1)
+    depth, along = lane // BS, lane % BS
+    edge, dy, dz = lane // 16 % 4, lane // HALO % HALO, lane % HALO
+    y = jnp.where(edge < 2, dy, BS - 1 - dy)
+    z = jnp.where(edge % 2 == 0, dz, BS - 1 - dz)
+    return jnp.concatenate([along * BS + depth, along * BS + BS - 1 - depth, y * BS + z], axis=1)
+
+
+def onehot(condition):
+    return condition.astype(f32).astype(bf16)
+
+
+def pack_kernel(f_ref, shapes_ref, links_ref, c_ref, cb_ref, msg_ref, strip, packed, slots):
+    cell = lax.broadcasted_iota(jnp.int32, (CELLS, 384), 0)
+    pick = onehot(cell == strip_rows())
+    last = lax.broadcasted_iota(jnp.int32, (128, 128), 0)
+    lane = lax.broadcasted_iota(jnp.int32, (128, 128), 1)
+    turn = onehot(last == (HALO - 1 - lane // BS) * BS + lane % BS)
     for lo, hi in tiles_of(CELLS, 256):
         fs = [f_ref[0, i, :, lo:hi] for i in range(19)]
         for i, c in enumerate(collide(fs)):
@@ -172,7 +171,9 @@
     c_ref[76:80, :] = jnp.zeros((4, CELLS), f32)
     rounded = c_ref[...].astype(bf16)
     cb_ref[...] = rounded
-    strip[...] = jnp.dot(rounded, pick_ref[...], preferred_element_type=f32)
+    strip[:, 0:128] = rounded[:, 0:128].astype(f32)
+    strip[:, 128:256] = jnp.dot(rounded[:, CELLS - 128 :], turn, preferred_element_type=f32)
+    strip[:, 256:640] = jnp.dot(rounded, pick, preferred_element_type=f32)
     lane4 = lax.broadcasted_iota(jnp.int32, (4, 128), 1)
     for face in range(4):
         inward, along, outward = classes(face)
@@ -181,9 +182,9 @@
             return strip[4 * i : 4 * i + 4, face * 128 : face * 128 + 128]
 
         groups = [rows(i) for i in inward] + [rows(i) for i in along]
-        last = rows(outward[4])
-        groups[5] = jnp.where(lane4 < 96, groups[5], pltpu.roll(last, 96, 1))
-        groups[6] = jnp.where(lane4 < 96, groups[6], pltpu.roll(last, 64, 1))
+        fifth = rows(outward[4])
+        groups[5] = jnp.where(lane4 < 96, groups[5], pltpu.roll(fifth, 96, 1))
+        groups[6] = jnp.where(lane4 < 96, groups[6], pltpu.roll(fifth, 64, 1))
         for a, b in ((0, 1), (2, 3)):
             shifted = pltpu.roll(rows(outward[b]), 64, 1)
             groups.append(jnp.where(lane4 < 64, rows(outward[a]), shifted))
@@ -192,35 +193,36 @@
     lane16 = lax.broadcasted_iota(jnp.int32, (16, 128), 1)
     packed[256:320, :] = strip[0:64, 512:640]
     packed[256:272, :] = jnp.where(lane16 < 64, strip[0:16, 512:640], strip[64:80, 512:640])
+    slots[0:32, 0:8, :] = packed[0:256, :].reshape(32, 8, 128)
+    for message in range(4, 8):
+        slots[message * 8 : message * 8 + 8, 0:8, :] = packed[256:320, :].reshape(8, 8, 128)
+    info = shapes_ref[...].astype(f32)
+    links = links_ref[...].astype(f32)
+    geometry = [jnp.concatenate([info[2 * r : 2 * r + 1], info[2 * r + 1 : 2 * r + 2]], axis=1) for r in range(3)]
+    row = lax.broadcasted_iota(jnp.int32, (8, 128), 0)
     for message in range(8):
-        source = min(message, 4) * 64
-        for r in range(8):
-            slots[message * 8 : message * 8 + 8, 128 * r : 128 * r + 128] = packed[
-                source + 8 * r : source + 8 * r + 8, :
-            ]
-    pos = pos_ref[...].astype(f32)
-    nor = nor_ref[...].astype(f32)
-    pairs = [(pos[0:1], pos[1:2]), (pos[2:3], nor[0:1]), (nor[1:2], nor[2:3])]
-    for r, (a, b) in enumerate(pairs):
-        row = jnp.concatenate([a, b], axis=1)
-        slots[:, 1024 + 128 * r : 1152 + 128 * r] = jnp.broadcast_to(row, (64, 128))
-    source_of = [faces[0, 1], faces[0, 0], faces[0, 3], faces[0, 2]]
-    source_of += [edges[0, 3], edges[0, 2], edges[0, 1], edges[0, 0]]
-    kind = lax.broadcasted_iota(jnp.int32, (64, 128), 0) // 8
-    index = jnp.zeros((64, 128), jnp.int32)
-    for message in range(8):
-        index = jnp.where(kind == message, source_of[message], index)
-    slots[:, 1408:1536] = index.astype(f32)
+        line, column = (0, (1, 0, 3, 2)[message]) if message < 4 else (1, 7 - message)
+        block = jnp.broadcast_to(links[line : line + 1, column : column + 1], (8, 128))
+        for r in range(3):
+            block = jnp.where(row == r, geometry[r], block)
+        slots[message * 8 : message * 8 + 8, 8:16, :] = jnp.broadcast_to(block[None], (8, 8, 128))
     msg_ref[...] = slots[...].astype(bf16)
 
 
-def forward_kernel(in_ref, out_ref):
-    wanted = in_ref[:, 1408:1472].astype(f32).astype(jnp.int32)
-    onehot = wanted == lax.broadcasted_iota(jnp.int32, (64, 64), 1)
-    picked = jnp.dot(
-        onehot.astype(f32).astype(bf16), in_ref[:, 0:1024], preferred_element_type=f32
-    )
-    out_ref[...] = picked.astype(bf16)
+def forward_kernel(in_ref, out_ref, geo_ref, rows, moved):
+    rows[...] = in_ref[...].astype(f32).reshape(1024, 128)
+
+    def every(r):
+        return rows[pl.ds(r, 64, stride=16), :]
+
+    wanted = every(11)[:, 0:64].astype(jnp.int32)
+    mine = onehot(wanted == lax.broadcasted_iota(jnp.int32, (64, 64), 1))
+    sent = jnp.concatenate([every(r) for r in range(8)], axis=1).astype(bf16)
+    picked = jnp.dot(mine, sent, preferred_element_type=f32)
+    for r in range(8):
+        moved[pl.ds(r, 64, stride=8), :] = picked[:, 128 * r : 128 * r + 128]
+    out_ref[...] = moved[...].reshape(64, 8, 128).astype(bf16)
+    geo_ref[...] = jnp.concatenate([every(r) for r in range(8, 11)], axis=1).astype(bf16)
 
 
 OWN_ROW, HIGH_ROW = 2, 6
@@ -236,11 +238,7 @@
         ref[16 * i : 16 * i + 2, lanes] = value[2:4]
 
 
-def early_kernel(
-    bands, count, c_ref, low_ref, high_ref, geo_ref, owner_ref, hist_ref, table_ref, last_ref,
-    *rest,
-):
-    own_refs, (state, spec, prev, geo, rows) = rest[: len(bands)], rest[len(bands) :]
+def early_kernel(bands, c_ref, low_ref, high_ref, state, rows):
     low = low_ref[...].astype(f32)
     high = high_ref[...].astype(f32)
     for i in range(19):
@@ -248,31 +246,42 @@
         place_slab(rows, i, 0, c_ref[4 * i : 4 * i + 4, :], slice(None))
         place_slab(rows, i, -1, low[4 * i : 4 * i + 4], slice(None))
         place_slab(rows, i, 1, high[4 * i : 4 * i + 4], slice(None))
-    for (lo, hi, a, b), own_ref in zip(bands, own_refs):
+    for lo, hi, a, b in bands:
+        lane = lax.broadcasted_iota(jnp.int32, (1, hi - lo), 1) + lo
+        y, z = lane // PITCH - HALO, lane % PITCH - HALO
+        inside = (y >= 0) & (y < BS) & (z >= 0) & (z < BS)
+        source = jnp.where(inside, y * BS + z, -1)
+        table = onehot(lax.broadcasted_iota(jnp.int32, (b - a, hi - lo), 0) + a == source)
         part = rows[:, a:b]
         coarse = part.astype(bf16)
         fine = (part - coarse.astype(f32)).astype(bf16)
-        placed = jnp.dot(coarse, own_ref[...], preferred_element_type=f32)
-        placed = placed + jnp.dot(fine, own_ref[...], preferred_element_type=f32)
-        state[:, lo:hi] = placed
+        placed = jnp.dot(coarse, table, preferred_element_type=f32)
+        state[:, lo:hi] = placed + jnp.dot(fine, table, preferred_element_type=f32)
+
+
+def slots_kernel(slot_ref, geo_ref, hist_ref, table_ref, spec, notes, chosen):
     nt = (((1,), (1,)), ((), ()))
     spec[0:128, :] = lax.dot_general(table_ref[...], hist_ref[:, 0:256], nt, preferred_element_type=f32)
     spec[128:256, :] = lax.dot_general(table_ref[...], hist_ref[:, 256:512], nt, preferred_element_type=f32)
-    prev[...] = lax.dot_general(last_ref[...], hist_ref[:, 0:256], nt, preferred_element_type=f32)
-    owner = owner_ref[...]
+    newest = onehot(lax.broadcasted_iota(jnp.int32, (8, 256), 1) == SAMPLES - 1)
+    notes[8:16, :] = lax.dot_general(newest, hist_ref[:, 0:256], nt, preferred_element_type=f32)
+    cell, owner, count = slot_ref[0:1, :], slot_ref[1:2, :], slot_ref[2:3, :]
     step = lax.broadcasted_iota(jnp.int32, (64, 128), 0)
-    which = (step == owner // P_OWN).astype(f32).astype(bf16)
+    which = onehot(step == owner // P_OWN)
     place = (step == owner % P_OWN).astype(f32)
     turned = (((0,), (0,)), ((), ()))
-    picked = lax.dot_general(geo_ref[:, 1024:1408], which, turned, preferred_element_type=f32)
-    geo[...] = jnp.zeros((16, 128), f32)
+    picked = lax.dot_general(geo_ref[...], which, turned, preferred_element_type=f32)
     for c in range(6):
-        geo[c : c + 1, :] = jnp.sum(picked[64 * c : 64 * c + 64] * place, axis=0, keepdims=True)
-    geo[6:7, :] = jnp.full((1, 128), count[0], jnp.int32).astype(f32)
+        notes[c : c + 1, :] = jnp.sum(picked[64 * c : 64 * c + 64] * place, axis=0, keepdims=True)
+    notes[6:7, :] = count.astype(f32)
+    notes[7:8, :] = (cell // CELLS).astype(f32)
+    across = cell % CELLS
+    spot = (across // BS + HALO) * PITCH + across % BS + HALO
+    chosen[...] = onehot(lax.broadcasted_iota(jnp.int32, (LANES, 128), 0) == spot)
 
 
 def flow_kernel(
-    halo_bands, count, state_ref, own_ref, low_ref, high_ref, cell_ref, spec_ref, prev_ref, geo_ref, late_ref,
+    halo_bands, state_ref, own_ref, low_ref, high_ref, spec_ref, notes_ref, chosen_ref, late_ref,
     *rest,
 ):
     halo_refs = rest[: len(halo_bands)]
@@ -282,10 +291,7 @@
     for i in range(19):
         halo[16 * i + 10 : 16 * i + 14, :] = jnp.zeros((4, 640), f32)
     for slab, ref in ((0, own_ref), (-1, low_ref), (1, high_ref)):
-        for message in range(8):
-            value = ref[:, 0:1024].astype(f32)[message * 8 : message * 8 + 8]
-            for r in range(8):
-                packed[message * 64 + 8 * r : message * 64 + 8 * r + 8, :] = value[:, 128 * r : 128 * r + 128]
+        packed[...] = ref[...].astype(f32).reshape(512, 128)
         for face in range(4):
             inward, along, outward = classes(face)
             lanes = slice(face * 128, face * 128 + 128)
@@ -343,34 +349,31 @@
     for i in range(19):
         field_ref[8 * i : 8 * i + 8, :] = jnp.where(inside, there[i, 0:8, :], 0.0)
 
-    cell = cell_ref[...]
-    across = cell % CELLS
-    spot = (across // BS + HALO) * PITCH + across % BS + HALO
-    onehot = (lax.broadcasted_iota(jnp.int32, (LANES, 128), 0) == spot).astype(f32).astype(bf16)
     rest_of = seen[...]
     read = jnp.zeros((8 * STEPS, 128), f32)
     for _ in range(3):
         piece = rest_of.astype(bf16)
-        read = read + jnp.dot(piece, onehot, preferred_element_type=f32)
+        read = read + jnp.dot(piece, chosen_ref[...], preferred_element_type=f32)
         rest_of = rest_of - piece.astype(f32)
-    before = prev_ref[0:1, :]
+    before = notes_ref[8:9, :]
+    layer = notes_ref[7:8, :]
     press, rate = [], []
     for t in range(STEPS):
         value = jnp.zeros((1, 128), f32)
         for x in range(SLAB):
             row = 8 * t + OWN_ROW + x
-            value = jnp.where(cell // CELLS == x, read[row : row + 1], value)
+            value = jnp.where(layer == x, read[row : row + 1], value)
         value = GAIN * value
         press.append(value.astype(bf16).astype(f32))
         rate.append((value - before).astype(bf16).astype(f32))
         before = value
-    alive = lax.broadcasted_iota(jnp.int32, (1, 128), 1) < count[0]
+    alive = lax.broadcasted_iota(jnp.int32, (1, 128), 1).astype(f32) < notes_ref[6:7, :]
     for g, late in ((0, press), (1, rate)):
         total = spec_ref[128 * g : 128 * g + 128, :]
         for t in range(STEPS):
             total = total + late_ref[:, t : t + 1] * late[t]
         out_ref[128 * g : 128 * g + 128, :] = jnp.where(alive, total, 0.0).astype(bf16)
-    out_ref[256:272, :] = geo_ref[...].astype(bf16)
+    out_ref[256:272, :] = notes_ref[...].astype(bf16)
 
 
 def field_kernel(bands, field_ref, *rest):
@@ -385,83 +388,91 @@
             out_ref[0, i, :, lo:hi] = value[8 * i + OWN_ROW : 8 * i + OWN_ROW + 4]
 
 
-def radiate_kernel(all_ref, listen_ref, out_ref, rows, spots, sums, turned):
+def series(x, coefficients):
+    value = coefficients[-1]
+    for c in coefficients[-2::-1]:
+        value = value * x + c
+    return value
+
+
+COSINE = [(-1.0) ** n / math.factorial(2 * n) for n in range(7)]
+SINE = [(-1.0) ** n / math.factorial(2 * n + 1) for n in range(7)]
+EARS = 32
+
+
+def radiate_kernel(all_ref, listen_ref, out_ref, rows, spots, sums, goal):
+    slot = lax.broadcasted_iota(jnp.int32, (128, 128), 0).astype(f32)
     base = jnp.zeros((1, 128), f32)
-    lane_f = lax.broadcasted_iota(jnp.int32, (128, 1024), 1).astype(f32)
-    slot_f = lax.broadcasted_iota(jnp.int32, (128, 1024), 0).astype(f32)
     for o in range(8):
         live = all_ref[o, 256:272, :].astype(f32)[6:7]
-        here = (lane_f - base[:, 0:1] == slot_f) & (slot_f < live[:, 0:1])
-        part = jnp.dot(all_ref[o], here.astype(f32).astype(bf16), preferred_element_type=f32)
-        if o == 0:
-            rows[...] = part
-        else:
-            rows[...] += part
+        goal[128 * o : 128 * o + 128, :] = jnp.where(slot < live, slot + base, -1.0)
         base = base + live
     used = jnp.max(base).astype(jnp.int32)
+    everything = jnp.concatenate([all_ref[o] for o in range(8)], axis=1)
     for axis in range(3):
-        row = listen_ref[axis : axis + 1, :]
-        spots[axis] = jnp.broadcast_to(row, (128, 128)).T
-    sums[...] = jnp.zeros((128, 128, 128), f32)
-
-    def panels(p, _):
-        at = pl.ds(pl.multiple_of(p * 128, 128), 128)
+        spots[axis] = jnp.broadcast_to(listen_ref[axis : axis + 1, :], (128, 128)).T
+    lane = lax.broadcasted_iota(jnp.int32, (1, 128), 1)
+
+    lanes = lax.broadcasted_iota(jnp.int32, (EARS, 128), 1)
+
+    def panels(p, first, final):
+        here = onehot(goal[...] == (lane + 128 * p).astype(f32))
+        rows[...] = jnp.dot(everything, here, preferred_element_type=f32)
 
         def listeners(m, _):
-            ears = pl.ds(pl.multiple_of(m * 16, 16), 16)
-            distance_sq = jnp.zeros((16, 128), f32)
-            facing = jnp.zeros((16, 128), f32)
+            ears = pl.ds(pl.multiple_of(m * EARS, EARS), EARS)
+            distance_sq = jnp.zeros((EARS, 128), f32)
+            facing = jnp.zeros((EARS, 128), f32)
             for axis in range(3):
-                offset = spots[axis, ears, :] - rows[256 + axis : 257 + axis, at]
+                offset = spots[axis, ears, :] - rows[256 + axis : 257 + axis, :]
                 distance_sq = distance_sq + offset * offset
-                facing = facing + rows[259 + axis : 260 + axis, at] * offset
+                facing = facing + rows[259 + axis : 260 + axis, :] * offset
             distance = jnp.sqrt(distance_sq)
             far = facing / (4.0 * math.pi * SOUND * distance_sq)
             ratio = SOUND / distance
             angle = (2.0 * math.pi / SAMPLES) * (distance / SOUND)
-            cosine = jnp.cos(angle)
+            square = angle * angle
+            cosine = series(square, COSINE)
             double = cosine + cosine
-            c_before, s_before = far, jnp.zeros((16, 128), f32)
-            c_now, s_now = far * cosine, far * jnp.sin(angle)
+            c_before, s_before = far, jnp.zeros((EARS, 128), f32)
+            c_now, s_now = far * cosine, far * (angle * series(square, SINE))
+            result = jnp.zeros((EARS, 128), f32)
             for k in range(BINS):
-                weight_real = rows[128 + k : 129 + k, at] + ratio * rows[k : k + 1, at]
-                weight_imag = rows[192 + k : 193 + k, at] + ratio * rows[64 + k : 65 + k, at]
-                sums[k, ears, :] += weight_real * c_now + weight_imag * s_now
-                sums[BINS + k, ears, :] += weight_imag * c_now - weight_real * s_now
+                weight_real = rows[128 + k : 129 + k, :] + ratio * rows[k : k + 1, :]
+                weight_imag = rows[192 + k : 193 + k, :] + ratio * rows[64 + k : 65 + k, :]
+                real = weight_real * c_now + weight_imag * s_now
+                imag = weight_imag * c_now - weight_real * s_now
+                for n, value in ((k, real), (BINS + k, imag)):
+                    at = slice(128 * n, 128 * n + 128)
+                    if first:
+                        sums[ears, at] = value
+                    elif not final:
+                        sums[ears, at] += value
+                    else:
+                        whole = jnp.sum(sums[ears, at] + value, axis=1, keepdims=True)
+                        result = jnp.where(lanes == n, whole, result)
                 if k < BINS - 1:
                     c_now, c_before = double * c_now - c_before, c_now
                     s_now, s_before = double * s_now - s_before, s_now
+            if final:
+                out_ref[ears, :] = result
             return 0
 
-        lax.fori_loop(0, 8, listeners, 0)
+        lax.fori_loop(0, 128 // EARS, listeners, 0)
         return 0
 
-    lax.fori_loop(0, (used + 127) // 128, panels, 0)
-
-    column = lax.broadcasted_iota(jnp.int32, (128, 128), 1)
-    turned[...] = jnp.zeros((128, 128), f32)
-
-    def fold(k, _):
-        pick = (column == k).astype(f32).astype(bf16)
-        value = sums[k]
-        coarse = value.astype(bf16)
-        fine = (value - coarse.astype(f32)).astype(bf16)
-        turned[...] += jnp.dot(coarse, pick, preferred_element_type=f32) + jnp.dot(
-            fine, pick, preferred_element_type=f32
-        )
-        return 0
-
-    lax.fori_loop(0, 128, fold, 0)
-    out_ref[...] = turned[...]
-
-
-def call(kernel, outs, operands, scratch=(), scalars=0, megabytes=32, flops=0):
-    smem = pl.BlockSpec(memory_space=pltpu.SMEM)
+    tiles = jnp.maximum((used + 127) // 128, 2)
+    panels(0, True, False)
+    lax.fori_loop(1, tiles - 1, lambda p, _: panels(p, False, False), 0)
+    panels(tiles - 1, False, True)
+
+
+def call(kernel, outs, operands, scratch=(), megabytes=32, flops=0):
     vmem = pl.BlockSpec(memory_space=pltpu.VMEM)
     return pl.pallas_call(
         kernel,
         out_shape=tuple(jax.ShapeDtypeStruct(s, d) for s, d in outs),
-        in_specs=[smem] * scalars + [vmem] * (len(operands) - scalars),
+        in_specs=[vmem] * len(operands),
         out_specs=tuple(vmem for _ in outs),
         scratch_shapes=[pltpu.VMEM(s, f32) for s in scratch],
         compiler_params=pltpu.CompilerParams(vmem_limit_bytes=megabytes * 2**20),
@@ -495,16 +506,14 @@
     shifted = np.concatenate([np.zeros((STEPS, 128), table.dtype), table[: SAMPLES - STEPS]]).T
     late = np.zeros((128, 128), np.float32)
     late[:, :STEPS] = table[SAMPLES - STEPS :].astype(np.float32).T
-    newest = np.zeros((16, SAMPLES), np.float32)
-    newest[0, SAMPLES - 1] = 1
-
-    pick = jnp.asarray(pick_table().astype(jnp.bfloat16))
+    shapes = jnp.concatenate([panel_pos, panel_normal])
+    links = jnp.concatenate([block_faces, block_edges])
+    slot_facts = jnp.stack([probe_cell, panel_owner, jnp.broadcast_to(panel_count, probe_cell.shape)])
     collided, rounded, message = call(
         pack_kernel,
-        [((80, CELLS), f32), ((80, CELLS), bf16), ((64, 1536), bf16)],
-        [block_faces, block_edges, populations, panel_pos, panel_normal, pick],
-        scratch=[(80, 640), (320, 128), (64, 1536)],
-        scalars=2,
+        [((80, CELLS), f32), ((80, CELLS), bf16), ((64, 16, 128), bf16)],
+        [populations, shapes, links],
+        scratch=[(80, 640), (320, 128), (64, 16, 128)],
     )
     ring = lax.axis_size("obs")
     up = [(i, (i + 1) % ring) for i in range(ring)]
@@ -515,29 +524,36 @@
 
     low, high = beside(rounded)
     spread = lax.all_to_all(message, "blk", 0, 0, tiled=True)
-    (sent,) = call(forward_kernel, [((64, 1024), bf16)], [spread])
+    sent, owners_geometry = call(
+        forward_kernel,
+        [((64, 8, 128), bf16), ((64, 384), bf16)],
+        [spread],
+        scratch=[(1024, 128), (512, 128)],
+    )
     arrived = lax.all_to_all(sent, "blk", 0, 0, tiled=True)
-    state, spec, prev, geo = call(
+    spec, notes, chosen = call(
+        slots_kernel,
+        [((256, 128), f32), ((16, 128), f32), ((LANES, 128), bf16)],
+        [slot_facts, owners_geometry, history, jnp.asarray(shifted)],
+        flops=10**8,
+    )
+    (state,) = call(
         functools.partial(early_kernel, bands),
-        [((304, LANES), f32), ((256, 128), f32), ((16, 128), f32), ((16, 128), f32)],
-        [
-            panel_count, collided, low, high, spread, panel_owner.reshape(1, 128), history,
-            jnp.asarray(shifted), jnp.asarray(newest.astype(jnp.bfloat16)), *cut(own, bands),
-        ],
+        [((304, LANES), f32)],
+        [collided, low, high],
         scratch=[(304, CELLS)],
-        scalars=1,
-        flops=10**9,
-    )
+        flops=10**8,
+    )
+    arrived, spec, notes, chosen = lax.optimization_barrier((arrived, spec, notes, chosen))
     arrived_low, arrived_high = beside(arrived)
     payload, field = call(
         functools.partial(flow_kernel, halo_bands),
         [((272, 128), bf16), ((152, LANES), f32)],
         [
-            panel_count, state, arrived, arrived_low, arrived_high, probe_cell.reshape(1, 128), spec, prev,
-            geo, jnp.asarray(late), *cut(around, halo_bands),
+            state, arrived, arrived_low, arrived_high, spec, notes, chosen, jnp.asarray(late),
+            *cut(around, halo_bands),
         ],
         scratch=[(512, 128), (304, 640), (19, 16, LANES), (19, 16, LANES), (32, LANES)],
-        scalars=1,
     )
     (populations_out,) = call(
         functools.partial(field_kernel, back_bands),
@@ -550,8 +566,8 @@
         radiate_kernel,
         [((128, 128), f32)],
         [gathered, observers],
-        scratch=[(272, 1024), (3, 128, 128), (128, 128, 128), (128, 128)],
-        megabytes=48,
+        scratch=[(272, 128), (3, 128, 128), (128, 16384), (1024, 128)],
+        megabytes=20,
     )
     pieces = lax.all_to_all(partial_value.reshape(64, 256), "blk", 0, 0, tiled=True)
     summed = jnp.sum(pieces, axis=0)

time: 152 us -> 133 us (0.88)
  Pallas kernels: 44 us -> 23.9 us
  starting transfers between devices: 20.5 us -> 25.4 us
  waiting for transfers between devices: 26 us -> 22 us
  local copies, waits for them, and re-layouts: 6.71 us -> 4.07 us
  blocking collectives: 51 us -> 53 us
    pallas_call x6 -> x7, Pallas kernels: 44 us -> 23.9 us  [call(): pl.pallas_call(kernel, out_shape=tuple((jax.ShapeDtypeStruct(s, d) for s,...]
    all_to_all x1, starting transfers between devices: 6.14 us -> 10.4 us  [body(): lax.all_to_all(partial_value.reshape(64, 256), 'blk', 0, 0, tiled=True)]
    all_to_all x1, waiting for transfers between devices: 12 us -> 8.46 us  [body(): arrived = lax.all_to_all(sent, 'blk', 0, 0, tiled=True)]
    unnamed x62 -> x32, local copies, waits for them, and re-layouts: 6.19 us -> 3.99 us
    all_to_all x1, blocking collectives: 36.4 us -> 38.4 us  [body(): spread = lax.all_to_all(message, 'blk', 0, 0, tiled=True)]
  transfers between devices with their start and end apart: 6 -> 6, of which waited for: 3 -> 3; matrix products, arithmetic and copies ran while one was open for 0% -> 1% of each run, Pallas kernels for 1% -> 2%
where the time goes in v2:
time: 133 us
  blocking collectives  53 us (40%)
  starting transfers between devices  25.4 us (19%)
  Pallas kernels  23.9 us (18%)
  waiting for transfers between devices  22 us (17%)
  local copies, waits for them, and re-layouts  4.07 us (3%)
  other arithmetic  2.78 us (2%)
  between operations  1.51 us (1%)
    all_to_all x1, blocking collectives, body(): spread = lax.all_to_all(message, 'blk', 0, 0, tiled=True)  38.4 us
    pallas_call x7, Pallas kernels, call(): pl.pallas_call(kernel, out_shape=tuple((jax.ShapeDtypeStruct(s, d) for s,...  23.9 us
    all_gather x1, blocking collectives, body(): gathered = lax.all_gather(payload, 'obs', axis=0, tiled=False)  14.5 us
    all_to_all x1, waiting for transfers between devices, body(): lax.all_to_all(partial_value.reshape(64, 256), 'blk', 0, 0, tiled=True)  11.7 us
    all_to_all x1, starting transfers between devices, body(): lax.all_to_all(partial_value.reshape(64, 256), 'blk', 0, 0, tiled=True)  10.4 us
    all_to_all x1, waiting for transfers between devices, body(): arrived = lax.all_to_all(sent, 'blk', 0, 0, tiled=True)  8.46 us
    ppermute x4, starting transfers between devices, beside(): return (lax.ppermute(value, 'obs', up), lax.ppermute(value, 'obs', down))  7.62 us
    all_to_all x1, starting transfers between devices, body(): arrived = lax.all_to_all(sent, 'blk', 0, 0, tiled=True)  7.36 us
  transfers between devices with their start and end apart: 6, of which 3 were waited for; matrix products, arithmetic and copies ran while one was open for 1% of the time, Pallas kernels for 2%

profile of v2, /device:TPU:1, one launch (start us, length us, event | category | flops | bytes accessed | tf_op | source)
XLA Modules:
  0.0 132.7 jit_solution(4427082946534093876)
XLA Ops:
  0.6 0.7 pad_add_fusion.links_ref
  1.3 0.7 pad_maximum_fusion.shapes_ref
  2.0 1.0 copy-done.1
  3.0 0.6 shard_map.233
  3.6 0.0 copy-start
  3.6 0.0 copy-start.2
  3.6 0.0 copy-start.3
  3.6 0.0 copy-start.4
  3.6 0.0 copy-start.5
  3.6 0.0 copy-start.6
  3.6 0.0 copy-start.7
  3.6 0.0 copy-start.8
  3.7 38.4 %all_to_all.19.in_ref = bf16[64,16,128]{2,1,0:T(8,128)(2,1)S(1)} all-to-all(bf16[64,16,128]{2,1,0:T(8,128)(2,1)S(1)} %get-tuple-element.18), channel_id=1, replica_groups=mesh['blk'=64,'obs'=8] {'blk'}, dimensions={0} | all-to-all | bytes 524288 | tf_op jit(solution)/shard_map/all_to_all | solution.py:526
  42.1 1.0 shard_map.235
  43.0 7.4 %all-to-all-start.1 = ((bf16[64,8,128]{2,1,0:T(8,128)(2,1)}), bf16[64,8,128]{2,1,0:T(8,128)(2,1)S(1)}, u32[]{:S(2)}, u32[]{:S(2)}) async-start(bf16[64,8,128]{2,1,0:T(8,128)(2,1)} %get-tuple-element.19), calls=%async_computation.1 | async-start | bytes 262144 | tf_op jit(solution)/shard_map/all_to_all | solution.py:533
  50.4 1.8 %collective-permute-start.1 = (bf16[80,1024]{1,0:T(8,128)(2,1)S(1)}, bf16[80,1024]{1,0:T(8,128)(2,1)S(1)}, u32[]{:S(2)}, u32[]{:S(2)}) collective-permute-start(bf16[80,1024]{1,0:T(8,128)(2,1)S(1)} %get-tuple-element.17), channel_id=1, source_target_pairs={{0,7},{1,0},{2,1},{3,2},{4,3},{5,4},{6,5},{7,6},{8,15},{9,8},{10,9... | collective-permute-start | bytes 491528 | tf_op jit(solution)/shard_map/ppermute | solution.py:523
  52.2 1.1 collective-permute-start
  54.0 0.1 pad.2.clone
  54.1 0.7 add_add_fusion.slot_ref
  54.8 0.9 copy-done.12
  55.7 0.8 copy-done.15
  56.5 0.4 shard_map.236
  57.0 8.5 %all-to-all-done.1.own_ref = bf16[64,8,128]{2,1,0:T(8,128)(2,1)S(1)} async-done(((bf16[64,8,128]{2,1,0:T(8,128)(2,1)}), bf16[64,8,128]{2,1,0:T(8,128)(2,1)S(1)}, u32[]{:S(2)}, u32[]{:S(2)}) %all-to-all-start.1) | async-done | bytes 131104 | tf_op jit(solution)/shard_map/all_to_all | solution.py:533
  65.4 3.6 %collective-permute-start.3 = (bf16[64,8,128]{2,1,0:T(8,128)(2,1)S(1)}, bf16[64,8,128]{2,1,0:T(8,128)(2,1)S(1)}, u32[]{:S(2)}, u32[]{:S(2)}) collective-permute-start(bf16[64,8,128]{2,1,0:T(8,128)(2,1)S(1)} %all-to-all-done.1.own_ref), channel_id=1, source_target_pairs={{0,7},{1,0},{2,1},{3,2},{4,3},{5,4},{6,5},{7,6},{8,15},{9,8},{10,9... | collective-permute-start | bytes 393224 | tf_op jit(solution)/shard_map/ppermute | solution.py:523
  69.0 1.1 collective-permute-start.2
  70.1 0.0 collective-permute-done.1.high_ref
  70.1 0.0 collective-permute-done.low_ref
  70.1 1.0 shard_map.234.state_ref
  71.1 0.0 copy-start.9
  71.1 0.0 copy-start.13
  71.1 0.0 copy-start.14
  71.2 1.9 %collective-permute-done.3.high_ref = bf16[64,8,128]{2,1,0:T(8,128)(2,1)S(1)} collective-permute-done((bf16[64,8,128]{2,1,0:T(8,128)(2,1)S(1)}, bf16[64,8,128]{2,1,0:T(8,128)(2,1)S(1)}, u32[]{:S(2)}, u32[]{:S(2)}) %collective-permute-start.3) | collective-permute-done | bytes 131104 | tf_op jit(solution)/shard_map/ppermute | solution.py:523
  73.1 0.0 collective-permute-done.2.low_ref
  73.1 0.0 copy-done.2
  73.1 0.0 copy-done.3
  73.1 0.0 copy-done.4
  73.1 0.0 copy-done.5
  73.1 0.0 copy-done.6
  73.1 0.0 copy-done.7
  73.1 0.0 copy-done.8
  73.1 4.2 %shard_map.237 = (bf16[272,128]{1,0:T(8,128)(2,1)S(1)}, f32[152,1664]{1,0:T(8,128)S(1)}) custom-call(f32[304,1664]{1,0:T(8,128)S(1)} %shard_map.234.state_ref, bf16[64,8,128]{2,1,0:T(8,128)(2,1)S(1)} %all-to-all-done.1.own_ref, bf16[64,8,128]{2,1,0:T(8,128)(2,1)S(1)} %collective-permute-done.2.low_ref, ...), custom_call_target="tpu_custom_call" | custom-call | bytes 1048576 | tf_op jit(solution)/shard_map/pallas_call | solution.py:472
  77.4 14.5 %all-gather = bf16[2176,128]{1,0:T(8,128)(2,1)S(1)} all-gather(bf16[272,128]{1,0:T(8,128)(2,1)S(1)} %get-tuple-element.29), channel_id=2, replica_groups=mesh['blk'=64,'obs'=8] {'obs'}, dimensions={0}, use_global_device_ids=true | all-gather | bytes 626688 | tf_op jit(solution)/shard_map/all_gather | solution.py:564
  91.9 15.6 %shard_map.239 = f32[128,128]{1,0:T(8,128)} custom-call(bf16[8,272,128]{2,1,0:T(8,128)(2,1)S(1)} %bitcast.6, f32[3,128]{1,0:T(4,128)S(1)} %copy-done.9), custom_call_target="tpu_custom_call" | custom-call | bytes 1048576 | tf_op jit(solution)/shard_map/pallas_call | solution.py:472
  107.5 10.4 %all-to-all-start.2 = ((f32[64,1,256]{2,1,0:T(1,128)}), f32[64,1,256]{2,1,0:T(1,128)S(1)}, u32[]{:S(2)}, u32[]{:S(2)}) async-start(f32[64,1,256]{2,1,0:T(1,128)} %bitcast.4), calls=%async_computation.2 | async-start | bytes 131072 | tf_op jit(solution)/shard_map/all_to_all | solution.py:572
  117.9 1.2 copy-done.11
  119.1 1.3 shard_map.238
  120.4 11.7 %all-to-all-done.2 = f32[64,1,256]{2,1,0:T(1,128)S(1)} async-done(((f32[64,1,256]{2,1,0:T(1,128)}), f32[64,1,256]{2,1,0:T(1,128)S(1)}, u32[]{:S(2)}, u32[]{:S(2)}) %all-to-all-start.2) | async-done | bytes 65568 | tf_op jit(solution)/shard_map/all_to_all | solution.py:572
  132.0 0.7 reduce_sum.9
  (10 shorter events, 0.0 us)
Async XLA Ops:
  2.0 1.0 copy-start.1
  3.6 69.5 %copy-start = (bf16[640,256]{1,0:T(8,128)(2,1)S(1)}, bf16[640,256]{1,0:T(8,128)(2,1)}, u32[]{:S(2)}) copy-start(bf16[640,256]{1,0:T(8,128)(2,1)} %constant.31.clone.rest_5_) | copy-start | bytes 983044
  3.6 69.5 %copy-start.2 = (bf16[512,256]{1,0:T(8,128)(2,1)S(1)}, bf16[512,256]{1,0:T(8,128)(2,1)}, u32[]{:S(2)}) copy-start(bf16[512,256]{1,0:T(8,128)(2,1)} %constant.26.clone.rest_0_) | copy-start | bytes 786436
  3.6 69.5 %copy-start.3 = (bf16[640,128]{1,0:T(8,128)(2,1)S(1)}, bf16[640,128]{1,0:T(8,128)(2,1)}, u32[]{:S(2)}) copy-start(bf16[640,128]{1,0:T(8,128)(2,1)} %constant.32.clone.rest_6_) | copy-start | bytes 491524
  3.6 69.5 %copy-start.4 = (bf16[256,256]{1,0:T(8,128)(2,1)S(1)}, bf16[256,256]{1,0:T(8,128)(2,1)}, u32[]{:S(2)}) copy-start(bf16[256,256]{1,0:T(8,128)(2,1)} %constant.30.clone.rest_4_) | copy-start | bytes 393220
  3.6 69.5 %copy-start.5 = (bf16[256,256]{1,0:T(8,128)(2,1)S(1)}, bf16[256,256]{1,0:T(8,128)(2,1)}, u32[]{:S(2)}) copy-start(bf16[256,256]{1,0:T(8,128)(2,1)} %constant.29.clone.rest_3_) | copy-start | bytes 393220
  3.6 69.5 %copy-start.6 = (bf16[256,256]{1,0:T(8,128)(2,1)S(1)}, bf16[256,256]{1,0:T(8,128)(2,1)}, u32[]{:S(2)}) copy-start(bf16[256,256]{1,0:T(8,128)(2,1)} %constant.28.clone.rest_2_) | copy-start | bytes 393220
  3.6 69.5 %copy-start.7 = (bf16[256,256]{1,0:T(8,128)(2,1)S(1)}, bf16[256,256]{1,0:T(8,128)(2,1)}, u32[]{:S(2)}) copy-start(bf16[256,256]{1,0:T(8,128)(2,1)} %constant.27.clone.rest_1_) | copy-start | bytes 393220
  3.6 69.5 %copy-start.8 = (f32[128,128]{1,0:T(8,128)S(1)}, f32[128,128]{1,0:T(8,128)}, u32[]{:S(2)}) copy-start(f32[128,128]{1,0:T(8,128)} %constant.25.clone.late_ref) | copy-start | bytes 196612
  43.0 22.4 %all-to-all-start.1 = ((bf16[64,8,128]{2,1,0:T(8,128)(2,1)}), bf16[64,8,128]{2,1,0:T(8,128)(2,1)S(1)}, u32[]{:S(2)}, u32[]{:S(2)}) async-start(bf16[64,8,128]{2,1,0:T(8,128)(2,1)} %get-tuple-element.19), calls=%async_computation.1 | async-start | bytes 262144 | tf_op jit(solution)/shard_map/all_to_all | solution.py:533
  50.4 19.7 %collective-permute-start.1 = (bf16[80,1024]{1,0:T(8,128)(2,1)S(1)}, bf16[80,1024]{1,0:T(8,128)(2,1)S(1)}, u32[]{:S(2)}, u32[]{:S(2)}) collective-permute-start(bf16[80,1024]{1,0:T(8,128)(2,1)S(1)} %get-tuple-element.17), channel_id=1, source_target_pairs={{0,7},{1,0},{2,1},{3,2},{4,3},{5,4},{6,5},{7,6},{8,15},{9,8},{10,9... | collective-permute-start | bytes 491528 | tf_op jit(solution)/shard_map/ppermute | solution.py:523
  52.2 17.9 %collective-permute-start = (bf16[80,1024]{1,0:T(8,128)(2,1)S(1)}, bf16[80,1024]{1,0:T(8,128)(2,1)S(1)}, u32[]{:S(2)}, u32[]{:S(2)}) collective-permute-start(bf16[80,1024]{1,0:T(8,128)(2,1)S(1)} %get-tuple-element.17), channel_id=1, source_target_pairs={{0,1},{1,2},{2,3},{3,4},{4,5},{5,6},{6,7},{7,0},{8,9},{9,10},{10,1... | collective-permute-start | bytes 491528 | tf_op jit(solution)/shard_map/ppermute | solution.py:523
  54.8 0.9 copy-start.12
  55.7 0.8 copy-start.15
  65.4 7.6 %collective-permute-start.3 = (bf16[64,8,128]{2,1,0:T(8,128)(2,1)S(1)}, bf16[64,8,128]{2,1,0:T(8,128)(2,1)S(1)}, u32[]{:S(2)}, u32[]{:S(2)}) collective-permute-start(bf16[64,8,128]{2,1,0:T(8,128)(2,1)S(1)} %all-to-all-done.1.own_ref), channel_id=1, source_target_pairs={{0,7},{1,0},{2,1},{3,2},{4,3},{5,4},{6,5},{7,6},{8,15},{9,8},{10,9... | collective-permute-start | bytes 393224 | tf_op jit(solution)/shard_map/ppermute | solution.py:523
  69.0 4.0 %collective-permute-start.2 = (bf16[64,8,128]{2,1,0:T(8,128)(2,1)S(1)}, bf16[64,8,128]{2,1,0:T(8,128)(2,1)S(1)}, u32[]{:S(2)}, u32[]{:S(2)}) collective-permute-start(bf16[64,8,128]{2,1,0:T(8,128)(2,1)S(1)} %all-to-all-done.1.own_ref), channel_id=1, source_target_pairs={{0,1},{1,2},{2,3},{3,4},{4,5},{5,6},{6,7},{7,0},{8,9},{9,10},{10,1... | collective-permute-start | bytes 393224 | tf_op jit(solution)/shard_map/ppermute | solution.py:523
  71.1 20.8 %copy-start.9 = (f32[3,128]{1,0:T(4,128)S(1)}, f32[3,128]{1,0:T(4,128)}, u32[]{:S(2)}) copy-start(f32[3,128]{1,0:T(4,128)} %listen_ref.1) | copy-start | bytes 4612
  71.1 46.8 %copy-start.13 = (bf16[512,256]{1,0:T(8,128)(2,1)S(1)}, bf16[512,256]{1,0:T(8,128)(2,1)}, u32[]{:S(2)}) copy-start(bf16[512,256]{1,0:T(8,128)(2,1)} %constant.34.clone.rest_1_.rest_3_) | copy-start | bytes 786436
  71.1 46.8 %copy-start.14 = (bf16[384,256]{1,0:T(8,128)(2,1)S(1)}, bf16[384,256]{1,0:T(8,128)(2,1)}, u32[]{:S(2)}) copy-start(bf16[384,256]{1,0:T(8,128)(2,1)} %constant.33.clone.rest_0_.rest_2_) | copy-start | bytes 589828
  77.4 30.1 %copy-start.10 = (f32[152,1664]{1,0:T(8,128)}, f32[152,1664]{1,0:T(8,128)S(1)}, u32[]{:S(2)}) copy-start(f32[152,1664]{1,0:T(8,128)S(1)} %get-tuple-element.28.field_ref) | copy-start | bytes 3035140
  107.5 24.6 %all-to-all-start.2 = ((f32[64,1,256]{2,1,0:T(1,128)}), f32[64,1,256]{2,1,0:T(1,128)S(1)}, u32[]{:S(2)}, u32[]{:S(2)}) async-start(f32[64,1,256]{2,1,0:T(1,128)} %bitcast.4), calls=%async_computation.2 | async-start | bytes 131072 | tf_op jit(solution)/shard_map/all_to_all | solution.py:572
  117.9 1.2 copy-start.11

commit v3 on v2

--- a/solution.py
+++ b/solution.py
@@ -158,12 +158,28 @@
     return condition.astype(f32).astype(bf16)
 
 
-def pack_kernel(f_ref, shapes_ref, links_ref, c_ref, cb_ref, msg_ref, strip, packed, slots):
+def face_groups(face):
+    inward, along, outward = classes(face)
+    upper = [(i, None) for i in inward] + [(outward[0], outward[1]), (outward[2], outward[3]), (along[8], None)]
+    return upper, along[:8], outward[4]
+
+
+def pack_kernel(*refs):
+    given, made, refs = refs[:10], refs[10:15], refs[15:]
+    here, ready, (strip, packed, came, gone) = refs[:10], refs[10:15], refs[15:]
+    f_ref, faces, edges, count_ref, owner_ref, pos_ref, nor_ref, cell_ref, hist_ref, table_ref = here
+    c_ref, cb_ref, msg_ref, spec, facts = ready
+    arrivals = [pltpu.make_async_copy(a, b, came.at[n]) for n, (a, b) in enumerate(zip(given, here))]
+    leaving = [pltpu.make_async_copy(a, b, gone.at[n]) for n, (a, b) in enumerate(zip(ready, made))]
+    for copy in arrivals:
+        copy.start()
     cell = lax.broadcasted_iota(jnp.int32, (CELLS, 384), 0)
     pick = onehot(cell == strip_rows())
     last = lax.broadcasted_iota(jnp.int32, (128, 128), 0)
     lane = lax.broadcasted_iota(jnp.int32, (128, 128), 1)
     turn = onehot(last == (HALO - 1 - lane // BS) * BS + lane % BS)
+    for copy in arrivals:
+        copy.wait()
     for lo, hi in tiles_of(CELLS, 256):
         fs = [f_ref[0, i, :, lo:hi] for i in range(19)]
         for i, c in enumerate(collide(fs)):
@@ -175,54 +191,99 @@
     strip[:, 128:256] = jnp.dot(rounded[:, CELLS - 128 :], turn, preferred_element_type=f32)
     strip[:, 256:640] = jnp.dot(rounded, pick, preferred_element_type=f32)
     lane4 = lax.broadcasted_iota(jnp.int32, (4, 128), 1)
+    row4 = lax.broadcasted_iota(jnp.int32, (4, 128), 0)
     for face in range(4):
-        inward, along, outward = classes(face)
+        upper, lower, cut_up = face_groups(face)
 
         def rows(i):
             return strip[4 * i : 4 * i + 4, face * 128 : face * 128 + 128]
 
-        groups = [rows(i) for i in inward] + [rows(i) for i in along]
-        fifth = rows(outward[4])
-        groups[5] = jnp.where(lane4 < 96, groups[5], pltpu.roll(fifth, 96, 1))
-        groups[6] = jnp.where(lane4 < 96, groups[6], pltpu.roll(fifth, 64, 1))
-        for a, b in ((0, 1), (2, 3)):
-            shifted = pltpu.roll(rows(outward[b]), 64, 1)
-            groups.append(jnp.where(lane4 < 64, rows(outward[a]), shifted))
-        for g, value in enumerate(groups):
-            packed[face * 64 + 4 * g : face * 64 + 4 * g + 4, :] = value
-    lane16 = lax.broadcasted_iota(jnp.int32, (16, 128), 1)
+        near, next_to = pltpu.roll(rows(cut_up), 96, 1), pltpu.roll(rows(cut_up), 64, 1)
+        for slot in range(8):
+            at = face * 64 + 8 * slot
+            a, b = upper[slot]
+            value = rows(a)
+            if b is not None:
+                value = jnp.where(lane4 < 64, value, pltpu.roll(rows(b), 64, 1))
+            packed[at : at + 4, :] = value
+            piece = (near if slot < 4 else next_to)[slot % 4 : slot % 4 + 1]
+            value = jnp.where((lane4 >= 96) & (row4 == 0), piece, rows(lower[slot]))
+            packed[at + 4 : at + 8, :] = value
     packed[256:320, :] = strip[0:64, 512:640]
-    packed[256:272, :] = jnp.where(lane16 < 64, strip[0:16, 512:640], strip[64:80, 512:640])
-    slots[0:32, 0:8, :] = packed[0:256, :].reshape(32, 8, 128)
-    for message in range(4, 8):
-        slots[message * 8 : message * 8 + 8, 0:8, :] = packed[256:320, :].reshape(8, 8, 128)
-    info = shapes_ref[...].astype(f32)
-    links = links_ref[...].astype(f32)
-    geometry = [jnp.concatenate([info[2 * r : 2 * r + 1], info[2 * r + 1 : 2 * r + 2]], axis=1) for r in range(3)]
-    row = lax.broadcasted_iota(jnp.int32, (8, 128), 0)
+    for n in range(3):
+        at = 256 + 8 * n
+        packed[at : at + 4, :] = jnp.where(lane4 < 64, packed[at : at + 4, :], strip[64 + 4 * n : 68 + 4 * n, 512:640])
+    for message in range(5, 8):
+        packed[64 * message : 64 * message + 64, :] = packed[256:320, :]
+
+    owner, count = owner_ref[...], count_ref[0]
+    step = lax.broadcasted_iota(jnp.int32, (64, 128), 0)
+    slot = lax.broadcasted_iota(jnp.int32, (1, 128), 1)
+    asked = ((step == owner // P_OWN) & (slot < count)).astype(f32)
+    turned = (((0,), (0,)), ((), ()))
+    same = lax.dot_general(asked.astype(bf16), asked.astype(bf16), turned, preferred_element_type=f32)
+    order = jnp.sum(jnp.where(last < lane, same, 0.0), axis=0, keepdims=True)
+    place = (owner % P_OWN).astype(f32)
+    kind = lax.broadcasted_iota(jnp.int32, (64, 1), 0) // 8
+    source = jnp.zeros((64, 1), f32)
     for message in range(8):
-        line, column = (0, (1, 0, 3, 2)[message]) if message < 4 else (1, 7 - message)
-        block = jnp.broadcast_to(links[line : line + 1, column : column + 1], (8, 128))
-        for r in range(3):
-            block = jnp.where(row == r, geometry[r], block)
-        slots[message * 8 : message * 8 + 8, 8:16, :] = jnp.broadcast_to(block[None], (8, 8, 128))
-    msg_ref[...] = slots[...].astype(bf16)
-
-
-def forward_kernel(in_ref, out_ref, geo_ref, rows, moved):
-    rows[...] = in_ref[...].astype(f32).reshape(1024, 128)
+        block = faces[0, (1, 0, 3, 2)[message]] if message < 4 else edges[0, 7 - message]
+        source = jnp.where(kind == message, jnp.full((64, 1), block, jnp.int32).astype(f32), source)
+    lane64 = lax.broadcasted_iota(jnp.int32, (64, 128), 1)
+    extra = [source]
+    for n in range(2):
+        mine = jnp.where(order == n, asked, 0.0)
+        facts[64 * n : 64 * n + 64, :] = mine
+        extra.append(jnp.sum(mine * place, axis=1, keepdims=True))
+    for n in range(3):
+        at = pl.ds(5 + n, 64, stride=8)
+        packed[at, :] = jnp.where(lane64 < 96, packed[at, :], extra[n])
+    msg_ref[...] = packed[...].reshape(64, 8, 128).astype(bf16)
+    for copy in leaving[:3]:
+        copy.start()
+    facts[136:160, :] = jnp.zeros((24, 128), f32)
+    facts[144:147, 0:P_OWN] = pos_ref[...].astype(f32)
+    facts[147:150, 0:P_OWN] = nor_ref[...].astype(f32)
+    nt = (((1,), (1,)), ((), ()))
+    spec[0:128, :] = lax.dot_general(table_ref[...], hist_ref[:, 0:256], nt, preferred_element_type=f32)
+    spec[128:256, :] = lax.dot_general(table_ref[...], hist_ref[:, 256:512], nt, preferred_element_type=f32)
+    newest = onehot(lax.broadcasted_iota(jnp.int32, (8, 256), 1) == SAMPLES - 1)
+    facts[128:136, :] = lax.dot_general(newest, hist_ref[:, 0:256], nt, preferred_element_type=f32)
+    spot = cell_ref[...]
+    facts[136:137, :] = (spot // CELLS).astype(f32)
+    facts[137:138, :] = jnp.full((1, 128), count, jnp.int32).astype(f32)
+    across = spot % CELLS
+    facts[138:139, :] = ((across // BS + HALO) * PITCH + across % BS + HALO).astype(f32)
+    for copy in leaving[3:]:
+        copy.start()
+    for copy in leaving:
+        copy.wait()
+
+
+def forward_kernel(in_ref, facts_ref, out_ref, kept_ref, rows, moved, shape):
+    rows[...] = in_ref[...].astype(f32).reshape(512, 128)
 
     def every(r):
-        return rows[pl.ds(r, 64, stride=16), :]
-
-    wanted = every(11)[:, 0:64].astype(jnp.int32)
-    mine = onehot(wanted == lax.broadcasted_iota(jnp.int32, (64, 64), 1))
+        return rows[pl.ds(r, 64, stride=8), :]
+
+    square = lax.broadcasted_iota(jnp.int32, (64, 64), 1).astype(f32)
+    lane64 = lax.broadcasted_iota(jnp.int32, (64, 128), 1)
+    mine = onehot(every(5)[:, 96:97] == square)
     sent = jnp.concatenate([every(r) for r in range(8)], axis=1).astype(bf16)
     picked = jnp.dot(mine, sent, preferred_element_type=f32)
+    shape[...] = jnp.zeros((128, P_OWN), f32)
+    shape[96:112, :] = facts_ref[144:160, 0:P_OWN]
+    table = shape[...].astype(bf16)
+    nt = (((1,), (1,)), ((), ()))
     for r in range(8):
-        moved[pl.ds(r, 64, stride=8), :] = picked[:, 128 * r : 128 * r + 128]
+        value = picked[:, 128 * r : 128 * r + 128]
+        if r in (5, 6):
+            question = onehot(every(r + 1)[:, 96:97] == square)
+            answer = lax.dot_general(question, table, nt, preferred_element_type=f32)
+            value = jnp.where(lane64 < 96, value, answer)
+        moved[pl.ds(r, 64, stride=8), :] = value
     out_ref[...] = moved[...].reshape(64, 8, 128).astype(bf16)
-    geo_ref[...] = jnp.concatenate([every(r) for r in range(8, 11)], axis=1).astype(bf16)
+    kept_ref[...] = facts_ref[...]
 
 
 OWN_ROW, HIGH_ROW = 2, 6
@@ -238,7 +299,18 @@
         ref[16 * i : 16 * i + 2, lanes] = value[2:4]
 
 
-def early_kernel(bands, c_ref, low_ref, high_ref, state, rows):
+def early_kernel(bands, c_ref, low_ref, high_ref, arrived_ref, facts_ref, state, notes, chosen, rows, answers):
+    answers[...] = arrived_ref[...].astype(f32).reshape(512, 128)
+    turned = (((0,), (0,)), ((), ()))
+    found = jnp.zeros((128, 128), f32)
+    for n in range(2):
+        answer = answers[pl.ds(5 + n, 64, stride=8), :].astype(bf16)
+        who = facts_ref[64 * n : 64 * n + 64, :].astype(bf16)
+        found = found + lax.dot_general(answer, who, turned, preferred_element_type=f32)
+    notes[0:8, :] = found[96:104]
+    notes[8:24, :] = facts_ref[128:144, :]
+    spot = facts_ref[138:139, :].astype(jnp.int32)
+    chosen[...] = onehot(lax.broadcasted_iota(jnp.int32, (LANES, 128), 0) == spot)
     low = low_ref[...].astype(f32)
     high = high_ref[...].astype(f32)
     for i in range(19):
@@ -259,33 +331,22 @@
         state[:, lo:hi] = placed + jnp.dot(fine, table, preferred_element_type=f32)
 
 
-def slots_kernel(slot_ref, geo_ref, hist_ref, table_ref, spec, notes, chosen):
-    nt = (((1,), (1,)), ((), ()))
-    spec[0:128, :] = lax.dot_general(table_ref[...], hist_ref[:, 0:256], nt, preferred_element_type=f32)
-    spec[128:256, :] = lax.dot_general(table_ref[...], hist_ref[:, 256:512], nt, preferred_element_type=f32)
-    newest = onehot(lax.broadcasted_iota(jnp.int32, (8, 256), 1) == SAMPLES - 1)
-    notes[8:16, :] = lax.dot_general(newest, hist_ref[:, 0:256], nt, preferred_element_type=f32)
-    cell, owner, count = slot_ref[0:1, :], slot_ref[1:2, :], slot_ref[2:3, :]
-    step = lax.broadcasted_iota(jnp.int32, (64, 128), 0)
-    which = onehot(step == owner // P_OWN)
-    place = (step == owner % P_OWN).astype(f32)
-    turned = (((0,), (0,)), ((), ()))
-    picked = lax.dot_general(geo_ref[...], which, turned, preferred_element_type=f32)
-    for c in range(6):
-        notes[c : c + 1, :] = jnp.sum(picked[64 * c : 64 * c + 64] * place, axis=0, keepdims=True)
-    notes[6:7, :] = count.astype(f32)
-    notes[7:8, :] = (cell // CELLS).astype(f32)
-    across = cell % CELLS
-    spot = (across // BS + HALO) * PITCH + across % BS + HALO
-    chosen[...] = onehot(lax.broadcasted_iota(jnp.int32, (LANES, 128), 0) == spot)
+def halo_rows(lane):
+    y, z = lane // PITCH - HALO, lane % PITCH - HALO
+    dy = jnp.where(y < 0, -1 - y, y - BS)
+    dz = jnp.where(z < 0, -1 - z, z - BS)
+    middle_y, middle_z = (y >= 0) & (y < BS), (z >= 0) & (z < BS)
+    edge = 2 * (y < 0).astype(jnp.int32) + (z < 0).astype(jnp.int32)
+    row = 512 + edge * 16 + dy * HALO + dz
+    row = jnp.where(middle_z, jnp.where(y < 0, 128, 0) + dy * BS + z, row)
+    row = jnp.where(middle_y, jnp.where(z < 0, 384, 256) + dz * BS + y, row)
+    return jnp.where((middle_y & middle_z) | (y >= BS + HALO), -1, row)
 
 
 def flow_kernel(
-    halo_bands, state_ref, own_ref, low_ref, high_ref, spec_ref, notes_ref, chosen_ref, late_ref,
-    *rest,
+    halo_bands, state_ref, own_ref, low_ref, high_ref, notes_ref, chosen_ref,
+    out_ref, field_ref, packed, halo, here, there, seen, late,
 ):
-    halo_refs = rest[: len(halo_bands)]
-    out_ref, field_ref, packed, halo, here, there, seen = rest[len(halo_bands) :]
     lane4 = lax.broadcasted_iota(jnp.int32, (4, 128), 1)
     lane64 = lax.broadcasted_iota(jnp.int32, (64, 128), 1)
     for i in range(19):
@@ -293,29 +354,35 @@
     for slab, ref in ((0, own_ref), (-1, low_ref), (1, high_ref)):
         packed[...] = ref[...].astype(f32).reshape(512, 128)
         for face in range(4):
-            inward, along, outward = classes(face)
+            upper, lower, cut_up = face_groups(face)
             lanes = slice(face * 128, face * 128 + 128)
-
-            def group(g):
-                return packed[face * 64 + 4 * g : face * 64 + 4 * g + 4, :]
-
-            for g, i in enumerate(inward + along):
-                place_slab(halo, i, slab, group(g), lanes)
-            for g, (a, b) in ((14, (0, 1)), (15, (2, 3))):
-                place_slab(halo, outward[a], slab, group(g), lanes)
-                place_slab(halo, outward[b], slab, pltpu.roll(group(g), 64, 1), lanes)
-            last = jnp.where(lane4 < 32, pltpu.roll(group(5), 32, 1), pltpu.roll(group(6), 64, 1))
-            place_slab(halo, outward[4], slab, last, lanes)
+            for slot in range(8):
+                at = face * 64 + 8 * slot
+                a, b = upper[slot]
+                place_slab(halo, a, slab, packed[at : at + 4, :], lanes)
+                if b is not None:
+                    place_slab(halo, b, slab, pltpu.roll(packed[at : at + 4, :], 64, 1), lanes)
+                place_slab(halo, lower[slot], slab, packed[at + 4 : at + 8, :], lanes)
+            near = packed[pl.ds(face * 64 + 4, 4, stride=8), :]
+            next_to = packed[pl.ds(face * 64 + 36, 4, stride=8), :]
+            value = jnp.where(lane4 < 32, pltpu.roll(near, 32, 1), pltpu.roll(next_to, 64, 1))
+            place_slab(halo, cut_up, slab, value, lanes)
         corner = packed[256:320, :]
         for e in range(1, 4):
             corner = jnp.where((lane64 % 64) // 16 == e, packed[256 + 64 * e : 320 + 64 * e, :], corner)
         packed[256:320, :] = corner
         for i in range(19):
-            rows = packed[256 + 4 * (i % 16) : 260 + 4 * (i % 16), :]
+            at = 256 + (4 * i if i < 16 else 8 * (i - 16))
+            rows = packed[at : at + 4, :]
             rows = jnp.where((lane4 < 64) == (i < 16), rows, 0.0)
             place_slab(halo, i, slab, rows, slice(512, 640))
-    for (lo, hi, a, b), halo_ref in zip(halo_bands, halo_refs):
-        added = jnp.dot(halo[:, a:b].astype(bf16), halo_ref[...], preferred_element_type=f32)
+    for lo, hi, a, b in halo_bands:
+        source = halo_rows(lax.broadcasted_iota(jnp.int32, (1, hi - lo), 1) + lo)
+        row = lax.broadcasted_iota(jnp.int32, (b - a, hi - lo), 0) + a
+        match = row == source
+        if b > 512:
+            match = match | (row == jnp.where(source >= 512, source + 64, -1))
+        added = jnp.dot(halo[:, a:b].astype(bf16), onehot(match), preferred_element_type=f32)
         for i in range(19):
             here[i, :, lo:hi] = state_ref[16 * i : 16 * i + 16, lo:hi] + added[16 * i : 16 * i + 16] + WEIGHT[i]
 
@@ -356,24 +423,20 @@
         read = read + jnp.dot(piece, chosen_ref[...], preferred_element_type=f32)
         rest_of = rest_of - piece.astype(f32)
     before = notes_ref[8:9, :]
-    layer = notes_ref[7:8, :]
-    press, rate = [], []
+    layer = notes_ref[16:17, :]
     for t in range(STEPS):
         value = jnp.zeros((1, 128), f32)
         for x in range(SLAB):
             row = 8 * t + OWN_ROW + x
             value = jnp.where(layer == x, read[row : row + 1], value)
         value = GAIN * value
-        press.append(value.astype(bf16).astype(f32))
-        rate.append((value - before).astype(bf16).astype(f32))
+        late[t : t + 1, :] = value
+        late[STEPS + t : STEPS + t + 1, :] = value - before
         before = value
-    alive = lax.broadcasted_iota(jnp.int32, (1, 128), 1).astype(f32) < notes_ref[6:7, :]
-    for g, late in ((0, press), (1, rate)):
-        total = spec_ref[128 * g : 128 * g + 128, :]
-        for t in range(STEPS):
-            total = total + late_ref[:, t : t + 1] * late[t]
-        out_ref[128 * g : 128 * g + 128, :] = jnp.where(alive, total, 0.0).astype(bf16)
-    out_ref[256:272, :] = notes_ref[...].astype(bf16)
+    late[8:16, :] = notes_ref[0:8, :]
+    late[14:15, :] = notes_ref[17:18, :]
+    for o in range(8):
+        out_ref[o] = late[...].astype(bf16)
 
 
 def field_kernel(bands, field_ref, *rest):
@@ -400,33 +463,52 @@
 EARS = 32
 
 
-def radiate_kernel(all_ref, listen_ref, out_ref, rows, spots, sums, goal):
+def radiate_kernel(
+    spec_in, table_in, all_in, listen_in, out_ref,
+    rows, spots, sums, goal, every, spec_ref, table_ref, all_ref, listen_ref, came,
+):
+    pairs = [(all_in, all_ref), (table_in, table_ref), (listen_in, listen_ref)]
+    pairs += [(spec_in.at[o], spec_ref.at[o]) for o in range(8)]
+    copies = [pltpu.make_async_copy(a, b, came.at[n]) for n, (a, b) in enumerate(pairs)]
+    for copy in copies:
+        copy.start()
+    for copy in copies[:3]:
+        copy.wait()
     slot = lax.broadcasted_iota(jnp.int32, (128, 128), 0).astype(f32)
     base = jnp.zeros((1, 128), f32)
     for o in range(8):
-        live = all_ref[o, 256:272, :].astype(f32)[6:7]
-        goal[128 * o : 128 * o + 128, :] = jnp.where(slot < live, slot + base, -1.0)
+        at = slice(128 * o, 128 * o + 128)
+        copies[3 + o].wait()
+        late = all_ref[o].astype(f32)
+        for g in range(2):
+            total = spec_ref[o, 128 * g : 128 * g + 128, :]
+            for t in range(STEPS):
+                total = total + table_ref[:, t : t + 1] * late[STEPS * g + t : STEPS * g + t + 1]
+            every[128 * g : 128 * g + 128, at] = total.astype(bf16)
+        every[256:272, at] = all_ref[o]
+        live = late[14:15]
+        goal[at, :] = jnp.where(slot < live, slot + base, -1.0)
         base = base + live
     used = jnp.max(base).astype(jnp.int32)
-    everything = jnp.concatenate([all_ref[o] for o in range(8)], axis=1)
     for axis in range(3):
         spots[axis] = jnp.broadcast_to(listen_ref[axis : axis + 1, :], (128, 128)).T
     lane = lax.broadcasted_iota(jnp.int32, (1, 128), 1)
-
     lanes = lax.broadcasted_iota(jnp.int32, (EARS, 128), 1)
+    shape = (EARS // 8, 8, 128)
 
     def panels(p, first, final):
         here = onehot(goal[...] == (lane + 128 * p).astype(f32))
-        rows[...] = jnp.dot(everything, here, preferred_element_type=f32)
+        flat = jnp.dot(every[...], here, preferred_element_type=f32)
+        rows[...] = jnp.broadcast_to(flat[:, None, :], (272, 8, 128))
 
         def listeners(m, _):
             ears = pl.ds(pl.multiple_of(m * EARS, EARS), EARS)
-            distance_sq = jnp.zeros((EARS, 128), f32)
-            facing = jnp.zeros((EARS, 128), f32)
+            distance_sq = jnp.zeros(shape, f32)
+            facing = jnp.zeros(shape, f32)
             for axis in range(3):
-                offset = spots[axis, ears, :] - rows[256 + axis : 257 + axis, :]
+                offset = spots[axis, ears, :].reshape(shape) - rows[264 + axis]
                 distance_sq = distance_sq + offset * offset
-                facing = facing + rows[259 + axis : 260 + axis, :] * offset
+                facing = facing + rows[267 + axis] * offset
             distance = jnp.sqrt(distance_sq)
             far = facing / (4.0 * math.pi * SOUND * distance_sq)
             ratio = SOUND / distance
@@ -434,15 +516,16 @@
             square = angle * angle
             cosine = series(square, COSINE)
             double = cosine + cosine
-            c_before, s_before = far, jnp.zeros((EARS, 128), f32)
+            c_before, s_before = far, jnp.zeros(shape, f32)
             c_now, s_now = far * cosine, far * (angle * series(square, SINE))
             result = jnp.zeros((EARS, 128), f32)
             for k in range(BINS):
-                weight_real = rows[128 + k : 129 + k, :] + ratio * rows[k : k + 1, :]
-                weight_imag = rows[192 + k : 193 + k, :] + ratio * rows[64 + k : 65 + k, :]
+                weight_real = rows[128 + k] + ratio * rows[k]
+                weight_imag = rows[192 + k] + ratio * rows[64 + k]
                 real = weight_real * c_now + weight_imag * s_now
                 imag = weight_imag * c_now - weight_real * s_now
                 for n, value in ((k, real), (BINS + k, imag)):
+                    value = value.reshape(EARS, 128)
                     at = slice(128 * n, 128 * n + 128)
                     if first:
                         sums[ears, at] = value
@@ -467,14 +550,15 @@
     panels(tiles - 1, False, True)
 
 
-def call(kernel, outs, operands, scratch=(), megabytes=32, flops=0):
-    vmem = pl.BlockSpec(memory_space=pltpu.VMEM)
+def call(kernel, outs, operands, scratch=(), megabytes=32, flops=0, fetch=False, store=False):
+    vmem, anywhere = (pl.BlockSpec(memory_space=space) for space in (pltpu.VMEM, pl.ANY))
+    block = anywhere if fetch else vmem
     return pl.pallas_call(
         kernel,
         out_shape=tuple(jax.ShapeDtypeStruct(s, d) for s, d in outs),
-        in_specs=[vmem] * len(operands),
-        out_specs=tuple(vmem for _ in outs),
-        scratch_shapes=[pltpu.VMEM(s, f32) for s in scratch],
+        in_specs=[block] * len(operands),
+        out_specs=tuple(anywhere if store else vmem for _ in outs),
+        scratch_shapes=[pltpu.VMEM(s, f32) if isinstance(s, tuple) else s for s in scratch],
         compiler_params=pltpu.CompilerParams(vmem_limit_bytes=megabytes * 2**20),
         cost_estimate=pl.CostEstimate(flops=flops, bytes_accessed=2**20, transcendentals=0),
     )(*operands)
@@ -506,15 +590,39 @@
     shifted = np.concatenate([np.zeros((STEPS, 128), table.dtype), table[: SAMPLES - STEPS]]).T
     late = np.zeros((128, 128), np.float32)
     late[:, :STEPS] = table[SAMPLES - STEPS :].astype(np.float32).T
-    shapes = jnp.concatenate([panel_pos, panel_normal])
-    links = jnp.concatenate([block_faces, block_edges])
-    slot_facts = jnp.stack([probe_cell, panel_owner, jnp.broadcast_to(panel_count, probe_cell.shape)])
-    collided, rounded, message = call(
+    operands = [
+        populations,
+        block_faces,
+        block_edges,
+        panel_count,
+        panel_owner.reshape(1, 128),
+        panel_pos,
+        panel_normal,
+        probe_cell.reshape(1, 128),
+        history,
+        jnp.asarray(shifted),
+    ]
+    results = [
+        ((80, CELLS), f32),
+        ((80, CELLS), bf16),
+        ((64, 8, 128), bf16),
+        ((256, 128), f32),
+        ((160, 128), f32),
+    ]
+    collided, rounded, message, spec, facts = call(
         pack_kernel,
-        [((80, CELLS), f32), ((80, CELLS), bf16), ((64, 16, 128), bf16)],
-        [populations, shapes, links],
-        scratch=[(80, 640), (320, 128), (64, 16, 128)],
+        results,
+        operands,
+        scratch=[
+            (pltpu.SMEM if 0 < n < 4 else pltpu.VMEM)(a.shape, a.dtype) for n, a in enumerate(operands)
+        ]
+        + [pltpu.VMEM(s, d) for s, d in results]
+        + [(80, 640), (512, 128), pltpu.SemaphoreType.DMA((10,)), pltpu.SemaphoreType.DMA((5,))],
+        megabytes=60,
+        fetch=True,
+        store=True,
     )
+    all_spec = lax.all_gather(spec, "obs", axis=0, tiled=False)
     ring = lax.axis_size("obs")
     up = [(i, (i + 1) % ring) for i in range(ring)]
     down = [(i, (i - 1) % ring) for i in range(ring)]
@@ -524,36 +632,26 @@
 
     low, high = beside(rounded)
     spread = lax.all_to_all(message, "blk", 0, 0, tiled=True)
-    sent, owners_geometry = call(
+    sent, facts = call(
         forward_kernel,
-        [((64, 8, 128), bf16), ((64, 384), bf16)],
-        [spread],
-        scratch=[(1024, 128), (512, 128)],
+        [((64, 8, 128), bf16), ((160, 128), f32)],
+        [spread, facts],
+        scratch=[(512, 128), (512, 128), (128, P_OWN)],
     )
     arrived = lax.all_to_all(sent, "blk", 0, 0, tiled=True)
-    spec, notes, chosen = call(
-        slots_kernel,
-        [((256, 128), f32), ((16, 128), f32), ((LANES, 128), bf16)],
-        [slot_facts, owners_geometry, history, jnp.asarray(shifted)],
+    arrived_low, arrived_high = beside(arrived)
+    state, notes, chosen = call(
+        functools.partial(early_kernel, bands),
+        [((304, LANES), f32), ((24, 128), f32), ((LANES, 128), bf16)],
+        [collided, low, high, arrived, facts],
+        scratch=[(304, CELLS), (512, 128)],
         flops=10**8,
     )
-    (state,) = call(
-        functools.partial(early_kernel, bands),
-        [((304, LANES), f32)],
-        [collided, low, high],
-        scratch=[(304, CELLS)],
-        flops=10**8,
-    )
-    arrived, spec, notes, chosen = lax.optimization_barrier((arrived, spec, notes, chosen))
-    arrived_low, arrived_high = beside(arrived)
     payload, field = call(
         functools.partial(flow_kernel, halo_bands),
-        [((272, 128), bf16), ((152, LANES), f32)],
-        [
-            state, arrived, arrived_low, arrived_high, spec, notes, chosen, jnp.asarray(late),
-            *cut(around, halo_bands),
-        ],
-        scratch=[(512, 128), (304, 640), (19, 16, LANES), (19, 16, LANES), (32, LANES)],
+        [((8, 16, 128), bf16), ((152, LANES), f32)],
+        [state, arrived, arrived_low, arrived_high, notes, chosen],
+        scratch=[(512, 128), (304, 640), (19, 16, LANES), (19, 16, LANES), (32, LANES), (16, 128)],
     )
     (populations_out,) = call(
         functools.partial(field_kernel, back_bands),
@@ -561,13 +659,25 @@
         [field, *cut(back, back_bands)],
         flops=10**9,
     )
-    gathered = lax.all_gather(payload, "obs", axis=0, tiled=False)
+    newest = lax.all_to_all(payload, "obs", 0, 0, tiled=True)
     (partial_value,) = call(
         radiate_kernel,
         [((128, 128), f32)],
-        [gathered, observers],
-        scratch=[(272, 128), (3, 128, 128), (128, 16384), (1024, 128)],
-        megabytes=20,
+        [all_spec, jnp.asarray(late), newest, observers],
+        scratch=[
+            (272, 8, 128),
+            (3, 128, 128),
+            (128, 16384),
+            (1024, 128),
+            pltpu.VMEM((272, 1024), bf16),
+            (8, 256, 128),
+            (128, 128),
+            pltpu.VMEM((8, 16, 128), bf16),
+            (3, 128),
+            pltpu.SemaphoreType.DMA((11,)),
+        ],
+        megabytes=60,
+        fetch=True,
     )
     pieces = lax.all_to_all(partial_value.reshape(64, 256), "blk", 0, 0, tiled=True)
     summed = jnp.sum(pieces, axis=0)

time: 133 us -> 136 us (1.023)
  between operations: 1.51 us -> 14.8 us
  blocking collectives: 53 us -> 43.3 us
  waiting for transfers between devices: 22 us -> 27 us
  starting transfers between devices: 25.4 us -> 23.1 us
  local copies, waits for them, and re-layouts: 4.07 us -> 1.86 us
  other arithmetic: 2.78 us -> 0.66 us
    all_gather x1 -> x0, blocking collectives: 14.5 us -> none  [body(): gathered = lax.all_gather(payload, 'obs', axis=0, tiled=False)]
    all_to_all x0 -> x1, blocking collectives: none -> 9.05 us  [body(): newest = lax.all_to_all(payload, 'obs', 0, 0, tiled=True)]
    all_to_all x1, blocking collectives: 38.4 us -> 34.2 us  [body(): spread = lax.all_to_all(message, 'blk', 0, 0, tiled=True)]
    all_to_all x1, waiting for transfers between devices: 8.46 us -> 12 us  [body(): arrived = lax.all_to_all(sent, 'blk', 0, 0, tiled=True)]
    unnamed x32 -> x8, local copies, waits for them, and re-layouts: 3.99 us -> 1.86 us
    all_to_all x1, starting transfers between devices: 10.4 us -> 8.95 us  [body(): lax.all_to_all(partial_value.reshape(64, 256), 'blk', 0, 0, tiled=True)]
    concatenate x2 -> x0, other arithmetic: 1.39 us -> none  [the longest x1 0.7 us: body(): shapes = jnp.concatenate([panel_pos, panel_normal])]
    pallas_call x7 -> x6, Pallas kernels: 23.9 us -> 24.8 us  [call(): pl.pallas_call(kernel, out_shape=tuple((jax.ShapeDtypeStruct(s, d) for s,...]
  transfers between devices with their start and end apart: 6 -> 7, of which waited for: 3 -> 3; matrix products, arithmetic and copies ran while one was open for 1% -> 0% of each run, Pallas kernels for 2% -> 6%
where the time goes in v3:
time: 136 us; the launch traced here: 135 us
  blocking collectives  43.3 us (32%)
  waiting for transfers between devices  27 us (20%)
  Pallas kernels  24.8 us (18%)
  starting transfers between devices  23.1 us (17%)
  between operations  14.8 us (11%)
  local copies, waits for them, and re-layouts  1.86 us (1%)
    all_to_all x1, blocking collectives, body(): spread = lax.all_to_all(message, 'blk', 0, 0, tiled=True)  34.2 us
    pallas_call x6, Pallas kernels, call(): pl.pallas_call(kernel, out_shape=tuple((jax.ShapeDtypeStruct(s, d) for s,...  24.8 us
    all_to_all x1, waiting for transfers between devices, body(): lax.all_to_all(partial_value.reshape(64, 256), 'blk', 0, 0, tiled=True)  12.8 us
    all_to_all x1, waiting for transfers between devices, body(): arrived = lax.all_to_all(sent, 'blk', 0, 0, tiled=True)  12 us
    all_to_all x1, blocking collectives, body(): newest = lax.all_to_all(payload, 'obs', 0, 0, tiled=True)  9.05 us
    all_to_all x1, starting transfers between devices, body(): lax.all_to_all(partial_value.reshape(64, 256), 'blk', 0, 0, tiled=True)  8.95 us
    ppermute x4, starting transfers between devices, beside(): return (lax.ppermute(value, 'obs', up), lax.ppermute(value, 'obs', down))  7.69 us
    all_to_all x1, starting transfers between devices, body(): arrived = lax.all_to_all(sent, 'blk', 0, 0, tiled=True)  6.4 us
  transfers between devices with their start and end apart: 7, of which 3 were waited for; matrix products, arithmetic and copies ran while one was open for 0% of the time, Pallas kernels for 6%

profile of v3, /device:TPU:1, one launch (start us, length us, event | category | flops | bytes accessed | tf_op | source)
XLA Modules:
  0.0 135.4 jit_solution(18139543185298470807)
XLA Ops:
  7.2 0.0 all-gather.3.cloned.1.call-start
  7.9 2.5 %shard_map.167 = (f32[80,1024]{1,0:T(8,128)}, bf16[80,1024]{1,0:T(8,128)(2,1)}, bf16[64,8,128]{2,1,0:T(8,128)(2,1)}, f32[256,128]{1,0:T(8,128)}, f32[160,128]{1,0:T(8,128)}) custom-call(f32[1,19,4,1024]{3,2,1,0:T(4,128)} %refs_0_.1, s32[1,4]{1,0:T(1,128)} %refs_1_.1, s32[1,4]{1,0:T(1,128)} %refs_2_.1, s32[1]{0:T(128)S(6)} %copy.19.refs_3_, ...), custom_call_target="tpu_custom_call" | custom-call | bytes 1048576 | tf_op jit(solution)/shard_map/pallas_call | solution.py:556
  10.4 0.0 all-gather.3.cloned.1.call-update
  10.4 34.2 %all_to_all.24.in_ref = bf16[64,8,128]{2,1,0:T(8,128)(2,1)S(1)} all-to-all(bf16[64,8,128]{2,1,0:T(8,128)(2,1)} %get-tuple-element.16), channel_id=1, replica_groups=mesh['blk'=64,'obs'=8] {'blk'}, dimensions={0} | all-to-all | bytes 262144 | tf_op jit(solution)/shard_map/all_to_all | solution.py:634
  44.6 0.0 copy-start.1
  44.6 0.9 copy-done.1
  45.5 0.9 shard_map.168
  46.4 6.4 %all-to-all-start.1 = ((bf16[64,8,128]{2,1,0:T(8,128)(2,1)}), bf16[64,8,128]{2,1,0:T(8,128)(2,1)S(1)}, u32[]{:S(2)}, u32[]{:S(2)}) async-start(bf16[64,8,128]{2,1,0:T(8,128)(2,1)} %get-tuple-element.18), calls=%async_computation.1 | async-start | bytes 262144 | tf_op jit(solution)/shard_map/all_to_all | solution.py:641
  52.8 3.0 %collective-permute-start = (bf16[80,1024]{1,0:T(8,128)(2,1)}, bf16[80,1024]{1,0:T(8,128)(2,1)S(1)}, u32[]{:S(2)}, u32[]{:S(2)}) collective-permute-start(bf16[80,1024]{1,0:T(8,128)(2,1)} %get-tuple-element.15), channel_id=1, source_target_pairs={{0,1},{1,2},{2,3},{3,4},{4,5},{5,6},{6,7},{7,0},{8,9},{9,10},{10,1... | collective-permute-start | bytes 491528 | tf_op jit(solution)/shard_map/ppermute | solution.py:631
  55.8 0.0 collective-permute-start.1
  55.8 12.0 %all-to-all-done.1.arrived_ref.own_ref = bf16[64,8,128]{2,1,0:T(8,128)(2,1)S(1)} async-done(((bf16[64,8,128]{2,1,0:T(8,128)(2,1)}), bf16[64,8,128]{2,1,0:T(8,128)(2,1)S(1)}, u32[]{:S(2)}, u32[]{:S(2)}) %all-to-all-start.1) | async-done | bytes 131104 | tf_op jit(solution)/shard_map/all_to_all | solution.py:641
  67.8 4.7 %collective-permute-start.2 = (bf16[64,8,128]{2,1,0:T(8,128)(2,1)S(1)}, bf16[64,8,128]{2,1,0:T(8,128)(2,1)S(1)}, u32[]{:S(2)}, u32[]{:S(2)}) collective-permute-start(bf16[64,8,128]{2,1,0:T(8,128)(2,1)S(1)} %all-to-all-done.1.arrived_ref.own_ref), channel_id=1, source_target_pairs={{0,1},{1,2},{2,3},{3,4},{4,5},{5,6},{6,7},{7,0},{8,9},{9,10},{10,1... | collective-permute-start | bytes 393224 | tf_op jit(solution)/shard_map/ppermute | solution.py:631
  72.5 0.0 collective-permute-start.3
  72.5 0.0 collective-permute-done.low_ref
  72.5 0.0 collective-permute-done.1.high_ref
  72.5 0.0 copy-start
  72.5 1.0 copy-done
  73.5 1.2 shard_map.169
  74.7 0.0 collective-permute-done.2.low_ref
  74.7 2.2 %collective-permute-done.3.high_ref = bf16[64,8,128]{2,1,0:T(8,128)(2,1)S(1)} collective-permute-done((bf16[64,8,128]{2,1,0:T(8,128)(2,1)S(1)}, bf16[64,8,128]{2,1,0:T(8,128)(2,1)S(1)}, u32[]{:S(2)}, u32[]{:S(2)}) %collective-permute-start.3) | collective-permute-done | bytes 131104 | tf_op jit(solution)/shard_map/ppermute | solution.py:631
  76.9 0.0 copy-start.2
  76.9 0.0 copy-start.3
  76.9 4.5 %shard_map.170 = (bf16[8,16,128]{2,1,0:T(8,128)(2,1)S(1)}, f32[152,1664]{1,0:T(8,128)S(1)}) custom-call(f32[304,1664]{1,0:T(8,128)S(1)} %get-tuple-element.20.state_ref, bf16[64,8,128]{2,1,0:T(8,128)(2,1)S(1)} %all-to-all-done.1.arrived_ref.own_ref, bf16[64,8,128]{2,1,0:T(8,128)(2,1)S(1)} %collective-permute-done.2.low_ref, ...), custom_call_target="tpu_custom_call" | custom-call | bytes 1048576 | tf_op jit(solution)/shard_map/pallas_call | solution.py:556
  81.4 9.1 %all_to_all.25.all_in = bf16[8,16,128]{2,1,0:T(8,128)(2,1)} all-to-all(bf16[8,16,128]{2,1,0:T(8,128)(2,1)S(1)} %get-tuple-element.25), channel_id=1, replica_groups=mesh['blk'=64,'obs'=8] {'obs'}, dimensions={0} | all-to-all | bytes 65536 | tf_op jit(solution)/shard_map/all_to_all | solution.py:662
  90.4 0.0 all-gather.3.cloned.1.call-done
  90.4 14.4 %shard_map.172 = f32[128,128]{1,0:T(8,128)} custom-call(f32[8,256,128]{2,1,0:T(8,128)} %bitcast.5, f32[128,128]{1,0:T(8,128)} %constant.13.clone.table_in, bf16[8,16,128]{2,1,0:T(8,128)(2,1)} %all_to_all.25.all_in, f32[3,128]{1,0:T(4,128)} %listen_in.1), custom_call_target="tpu_custom_call" | custom-call | bytes 1048576 | tf_op jit(solution)/shard_map/pallas_call | solution.py:556
  104.9 9.0 %all-to-all-start.3 = ((f32[64,1,256]{2,1,0:T(1,128)}), f32[64,1,256]{2,1,0:T(1,128)S(1)}, u32[]{:S(2)}, u32[]{:S(2)}) async-start(f32[64,1,256]{2,1,0:T(1,128)} %bitcast.6), calls=%async_computation.3 | async-start | bytes 131072 | tf_op jit(solution)/shard_map/all_to_all | solution.py:682
  113.9 0.0 copy-done.2
  113.9 0.0 copy-done.3
  113.9 1.3 shard_map.171
  115.1 12.8 %all-to-all-done.3 = f32[64,1,256]{2,1,0:T(1,128)S(1)} async-done(((f32[64,1,256]{2,1,0:T(1,128)}), f32[64,1,256]{2,1,0:T(1,128)S(1)}, u32[]{:S(2)}, u32[]{:S(2)}) %all-to-all-start.3) | async-done | bytes 65568 | tf_op jit(solution)/shard_map/all_to_all | solution.py:682
  127.9 0.7 reduce_sum.9
Async XLA Ops:
  7.2 83.3 %all-gather.3.cloned.1.call-start = ((), (), s32[]{:S(2)}) async-start(), calls=%async_computation.4 | async-start | bytes 1179648 | tf_op jit(solution)/shard_map/all_gather | solution.py:625
  44.6 0.9 copy-start.1
  46.4 21.4 %all-to-all-start.1 = ((bf16[64,8,128]{2,1,0:T(8,128)(2,1)}), bf16[64,8,128]{2,1,0:T(8,128)(2,1)S(1)}, u32[]{:S(2)}, u32[]{:S(2)}) async-start(bf16[64,8,128]{2,1,0:T(8,128)(2,1)} %get-tuple-element.18), calls=%async_computation.1 | async-start | bytes 262144 | tf_op jit(solution)/shard_map/all_to_all | solution.py:641
  52.8 19.7 %collective-permute-start = (bf16[80,1024]{1,0:T(8,128)(2,1)}, bf16[80,1024]{1,0:T(8,128)(2,1)S(1)}, u32[]{:S(2)}, u32[]{:S(2)}) collective-permute-start(bf16[80,1024]{1,0:T(8,128)(2,1)} %get-tuple-element.15), channel_id=1, source_target_pairs={{0,1},{1,2},{2,3},{3,4},{4,5},{5,6},{6,7},{7,0},{8,9},{9,10},{10,1... | collective-permute-start | bytes 491528 | tf_op jit(solution)/shard_map/ppermute | solution.py:631
  55.8 16.7 %collective-permute-start.1 = (bf16[80,1024]{1,0:T(8,128)(2,1)}, bf16[80,1024]{1,0:T(8,128)(2,1)S(1)}, u32[]{:S(2)}, u32[]{:S(2)}) collective-permute-start(bf16[80,1024]{1,0:T(8,128)(2,1)} %get-tuple-element.15), channel_id=1, source_target_pairs={{0,7},{1,0},{2,1},{3,2},{4,3},{5,4},{6,5},{7,6},{8,15},{9,8},{10,9... | collective-permute-start | bytes 491528 | tf_op jit(solution)/shard_map/ppermute | solution.py:631
  67.8 6.9 %collective-permute-start.2 = (bf16[64,8,128]{2,1,0:T(8,128)(2,1)S(1)}, bf16[64,8,128]{2,1,0:T(8,128)(2,1)S(1)}, u32[]{:S(2)}, u32[]{:S(2)}) collective-permute-start(bf16[64,8,128]{2,1,0:T(8,128)(2,1)S(1)} %all-to-all-done.1.arrived_ref.own_ref), channel_id=1, source_target_pairs={{0,1},{1,2},{2,3},{3,4},{4,5},{5,6},{6,7},{7,0},{8,9},{9,10},{10,1... | collective-permute-start | bytes 393224 | tf_op jit(solution)/shard_map/ppermute | solution.py:631
  72.5 4.4 %collective-permute-start.3 = (bf16[64,8,128]{2,1,0:T(8,128)(2,1)S(1)}, bf16[64,8,128]{2,1,0:T(8,128)(2,1)S(1)}, u32[]{:S(2)}, u32[]{:S(2)}) collective-permute-start(bf16[64,8,128]{2,1,0:T(8,128)(2,1)S(1)} %all-to-all-done.1.arrived_ref.own_ref), channel_id=1, source_target_pairs={{0,7},{1,0},{2,1},{3,2},{4,3},{5,4},{6,5},{7,6},{8,15},{9,8},{10,9... | collective-permute-start | bytes 393224 | tf_op jit(solution)/shard_map/ppermute | solution.py:631
  72.5 1.0 copy-start
  76.9 37.0 %copy-start.2 = (bf16[512,256]{1,0:T(8,128)(2,1)S(1)}, bf16[512,256]{1,0:T(8,128)(2,1)}, u32[]{:S(2)}) copy-start(bf16[512,256]{1,0:T(8,128)(2,1)} %constant.12.clone.rest_1_.rest_3_) | copy-start | bytes 786436
  76.9 37.0 %copy-start.3 = (bf16[384,256]{1,0:T(8,128)(2,1)S(1)}, bf16[384,256]{1,0:T(8,128)(2,1)}, u32[]{:S(2)}) copy-start(bf16[384,256]{1,0:T(8,128)(2,1)} %constant.11.clone.rest_0_.rest_2_) | copy-start | bytes 589828
  104.9 23.0 %all-to-all-start.3 = ((f32[64,1,256]{2,1,0:T(1,128)}), f32[64,1,256]{2,1,0:T(1,128)S(1)}, u32[]{:S(2)}, u32[]{:S(2)}) async-start(f32[64,1,256]{2,1,0:T(1,128)} %bitcast.6), calls=%async_computation.3 | async-start | bytes 131072 | tf_op jit(solution)/shard_map/all_to_all | solution.py:682
Sparse Core Ops, SparseCore 0:
  10.5 36.7 all-gather.2

commit v4 on v3

--- a/solution.py
+++ b/solution.py
@@ -165,10 +165,10 @@
 
 
 def pack_kernel(*refs):
-    given, made, refs = refs[:10], refs[10:15], refs[15:]
-    here, ready, (strip, packed, came, gone) = refs[:10], refs[10:15], refs[15:]
-    f_ref, faces, edges, count_ref, owner_ref, pos_ref, nor_ref, cell_ref, hist_ref, table_ref = here
-    c_ref, cb_ref, msg_ref, spec, facts = ready
+    given, made, refs = refs[:8], refs[8:12], refs[12:]
+    here, ready, (strip, packed, came, gone) = refs[:8], refs[8:12], refs[12:]
+    f_ref, faces, edges, count_ref, owner_ref, pos_ref, nor_ref, cell_ref = here
+    c_ref, cb_ref, msg_ref, facts = ready
     arrivals = [pltpu.make_async_copy(a, b, came.at[n]) for n, (a, b) in enumerate(zip(given, here))]
     leaving = [pltpu.make_async_copy(a, b, gone.at[n]) for n, (a, b) in enumerate(zip(ready, made))]
     for copy in arrivals:
@@ -241,14 +241,9 @@
     msg_ref[...] = packed[...].reshape(64, 8, 128).astype(bf16)
     for copy in leaving[:3]:
         copy.start()
-    facts[136:160, :] = jnp.zeros((24, 128), f32)
+    facts[128:160, :] = jnp.zeros((32, 128), f32)
     facts[144:147, 0:P_OWN] = pos_ref[...].astype(f32)
     facts[147:150, 0:P_OWN] = nor_ref[...].astype(f32)
-    nt = (((1,), (1,)), ((), ()))
-    spec[0:128, :] = lax.dot_general(table_ref[...], hist_ref[:, 0:256], nt, preferred_element_type=f32)
-    spec[128:256, :] = lax.dot_general(table_ref[...], hist_ref[:, 256:512], nt, preferred_element_type=f32)
-    newest = onehot(lax.broadcasted_iota(jnp.int32, (8, 256), 1) == SAMPLES - 1)
-    facts[128:136, :] = lax.dot_general(newest, hist_ref[:, 0:256], nt, preferred_element_type=f32)
     spot = cell_ref[...]
     facts[136:137, :] = (spot // CELLS).astype(f32)
     facts[137:138, :] = jnp.full((1, 128), count, jnp.int32).astype(f32)
@@ -299,7 +294,19 @@
         ref[16 * i : 16 * i + 2, lanes] = value[2:4]
 
 
-def early_kernel(bands, c_ref, low_ref, high_ref, arrived_ref, facts_ref, state, notes, chosen, rows, answers):
+def slots_kernel(facts_ref, hist_ref, table_ref, late_ref, spec, late, chosen):
+    nt = (((1,), (1,)), ((), ()))
+    spec[0:128, :] = lax.dot_general(table_ref[...], hist_ref[:, 0:256], nt, preferred_element_type=f32)
+    spec[128:256, :] = lax.dot_general(table_ref[...], hist_ref[:, 256:512], nt, preferred_element_type=f32)
+    newest = onehot(lax.broadcasted_iota(jnp.int32, (8, 256), 1) == SAMPLES - 1)
+    spec[256:264, :] = lax.dot_general(newest, hist_ref[:, 0:256], nt, preferred_element_type=f32)
+    spec[264:272, :] = facts_ref[136:144, :]
+    late[...] = late_ref[...]
+    spot = facts_ref[138:139, :].astype(jnp.int32)
+    chosen[...] = onehot(lax.broadcasted_iota(jnp.int32, (LANES, 128), 0) == spot)
+
+
+def early_kernel(bands, c_ref, low_ref, high_ref, arrived_ref, facts_ref, state, geo, rows, answers):
     answers[...] = arrived_ref[...].astype(f32).reshape(512, 128)
     turned = (((0,), (0,)), ((), ()))
     found = jnp.zeros((128, 128), f32)
@@ -307,10 +314,7 @@
         answer = answers[pl.ds(5 + n, 64, stride=8), :].astype(bf16)
         who = facts_ref[64 * n : 64 * n + 64, :].astype(bf16)
         found = found + lax.dot_general(answer, who, turned, preferred_element_type=f32)
-    notes[0:8, :] = found[96:104]
-    notes[8:24, :] = facts_ref[128:144, :]
-    spot = facts_ref[138:139, :].astype(jnp.int32)
-    chosen[...] = onehot(lax.broadcasted_iota(jnp.int32, (LANES, 128), 0) == spot)
+    geo[...] = found[96:104]
     low = low_ref[...].astype(f32)
     high = high_ref[...].astype(f32)
     for i in range(19):
@@ -344,7 +348,7 @@
 
 
 def flow_kernel(
-    halo_bands, state_ref, own_ref, low_ref, high_ref, notes_ref, chosen_ref,
+    halo_bands, state_ref, own_ref, low_ref, high_ref, spec_ref, table_ref, chosen_ref, geo_ref,
     out_ref, field_ref, packed, halo, here, there, seen, late,
 ):
     lane4 = lax.broadcasted_iota(jnp.int32, (4, 128), 1)
@@ -422,21 +426,26 @@
         piece = rest_of.astype(bf16)
         read = read + jnp.dot(piece, chosen_ref[...], preferred_element_type=f32)
         rest_of = rest_of - piece.astype(f32)
-    before = notes_ref[8:9, :]
-    layer = notes_ref[16:17, :]
+    before = spec_ref[256:257, :]
+    layer = spec_ref[264:265, :]
+    news = [[], []]
     for t in range(STEPS):
         value = jnp.zeros((1, 128), f32)
         for x in range(SLAB):
             row = 8 * t + OWN_ROW + x
             value = jnp.where(layer == x, read[row : row + 1], value)
         value = GAIN * value
-        late[t : t + 1, :] = value
-        late[STEPS + t : STEPS + t + 1, :] = value - before
+        news[0].append(value.astype(bf16).astype(f32))
+        news[1].append((value - before).astype(bf16).astype(f32))
         before = value
-    late[8:16, :] = notes_ref[0:8, :]
-    late[14:15, :] = notes_ref[17:18, :]
-    for o in range(8):
-        out_ref[o] = late[...].astype(bf16)
+    for g in range(2):
+        total = spec_ref[128 * g : 128 * g + 128, :]
+        for t in range(STEPS):
+            total = total + table_ref[:, t : t + 1] * news[g][t]
+        out_ref[128 * g : 128 * g + 128, :] = total.astype(bf16)
+    late[0:8, :] = geo_ref[...]
+    late[8:16, :] = spec_ref[264:272, :]
+    out_ref[256:272, :] = late[...].astype(bf16)
 
 
 def field_kernel(bands, field_ref, *rest):
@@ -463,32 +472,14 @@
 EARS = 32
 
 
-def radiate_kernel(
-    spec_in, table_in, all_in, listen_in, out_ref,
-    rows, spots, sums, goal, every, spec_ref, table_ref, all_ref, listen_ref, came,
-):
-    pairs = [(all_in, all_ref), (table_in, table_ref), (listen_in, listen_ref)]
-    pairs += [(spec_in.at[o], spec_ref.at[o]) for o in range(8)]
-    copies = [pltpu.make_async_copy(a, b, came.at[n]) for n, (a, b) in enumerate(pairs)]
-    for copy in copies:
-        copy.start()
-    for copy in copies[:3]:
-        copy.wait()
+def radiate_kernel(all_ref, listen_ref, out_ref, rows, spots, sums, goal):
     slot = lax.broadcasted_iota(jnp.int32, (128, 128), 0).astype(f32)
     base = jnp.zeros((1, 128), f32)
     for o in range(8):
-        at = slice(128 * o, 128 * o + 128)
-        copies[3 + o].wait()
-        late = all_ref[o].astype(f32)
-        for g in range(2):
-            total = spec_ref[o, 128 * g : 128 * g + 128, :]
-            for t in range(STEPS):
-                total = total + table_ref[:, t : t + 1] * late[STEPS * g + t : STEPS * g + t + 1]
-            every[128 * g : 128 * g + 128, at] = total.astype(bf16)
-        every[256:272, at] = all_ref[o]
-        live = late[14:15]
-        goal[at, :] = jnp.where(slot < live, slot + base, -1.0)
+        live = all_ref[o, 256:272, :].astype(f32)[9:10]
+        goal[128 * o : 128 * o + 128, :] = jnp.where(slot < live, slot + base, -1.0)
         base = base + live
+    everything = jnp.concatenate([all_ref[o] for o in range(8)], axis=1)
     used = jnp.max(base).astype(jnp.int32)
     for axis in range(3):
         spots[axis] = jnp.broadcast_to(listen_ref[axis : axis + 1, :], (128, 128)).T
@@ -498,7 +489,7 @@
 
     def panels(p, first, final):
         here = onehot(goal[...] == (lane + 128 * p).astype(f32))
-        flat = jnp.dot(every[...], here, preferred_element_type=f32)
+        flat = jnp.dot(everything, here, preferred_element_type=f32)
         rows[...] = jnp.broadcast_to(flat[:, None, :], (272, 8, 128))
 
         def listeners(m, _):
@@ -506,9 +497,9 @@
             distance_sq = jnp.zeros(shape, f32)
             facing = jnp.zeros(shape, f32)
             for axis in range(3):
-                offset = spots[axis, ears, :].reshape(shape) - rows[264 + axis]
+                offset = spots[axis, ears, :].reshape(shape) - rows[256 + axis]
                 distance_sq = distance_sq + offset * offset
-                facing = facing + rows[267 + axis] * offset
+                facing = facing + rows[259 + axis] * offset
             distance = jnp.sqrt(distance_sq)
             far = facing / (4.0 * math.pi * SOUND * distance_sq)
             ratio = SOUND / distance
@@ -599,17 +590,14 @@
         panel_pos,
         panel_normal,
         probe_cell.reshape(1, 128),
-        history,
-        jnp.asarray(shifted),
     ]
     results = [
         ((80, CELLS), f32),
         ((80, CELLS), bf16),
         ((64, 8, 128), bf16),
-        ((256, 128), f32),
         ((160, 128), f32),
     ]
-    collided, rounded, message, spec, facts = call(
+    collided, rounded, message, facts = call(
         pack_kernel,
         results,
         operands,
@@ -617,12 +605,11 @@
             (pltpu.SMEM if 0 < n < 4 else pltpu.VMEM)(a.shape, a.dtype) for n, a in enumerate(operands)
         ]
         + [pltpu.VMEM(s, d) for s, d in results]
-        + [(80, 640), (512, 128), pltpu.SemaphoreType.DMA((10,)), pltpu.SemaphoreType.DMA((5,))],
+        + [(80, 640), (512, 128), pltpu.SemaphoreType.DMA((8,)), pltpu.SemaphoreType.DMA((4,))],
         megabytes=60,
         fetch=True,
         store=True,
     )
-    all_spec = lax.all_gather(spec, "obs", axis=0, tiled=False)
     ring = lax.axis_size("obs")
     up = [(i, (i + 1) % ring) for i in range(ring)]
     down = [(i, (i - 1) % ring) for i in range(ring)]
@@ -639,18 +626,25 @@
         scratch=[(512, 128), (512, 128), (128, P_OWN)],
     )
     arrived = lax.all_to_all(sent, "blk", 0, 0, tiled=True)
+    spec, newest_table, chosen = call(
+        slots_kernel,
+        [((272, 128), f32), ((128, 128), f32), ((LANES, 128), bf16)],
+        [facts, history, jnp.asarray(shifted), jnp.asarray(late)],
+        flops=10**8,
+    )
+    arrived, spec, newest_table, chosen = lax.optimization_barrier((arrived, spec, newest_table, chosen))
     arrived_low, arrived_high = beside(arrived)
-    state, notes, chosen = call(
+    state, geometry = call(
         functools.partial(early_kernel, bands),
-        [((304, LANES), f32), ((24, 128), f32), ((LANES, 128), bf16)],
+        [((304, LANES), f32), ((8, 128), f32)],
         [collided, low, high, arrived, facts],
         scratch=[(304, CELLS), (512, 128)],
         flops=10**8,
     )
     payload, field = call(
         functools.partial(flow_kernel, halo_bands),
-        [((8, 16, 128), bf16), ((152, LANES), f32)],
-        [state, arrived, arrived_low, arrived_high, notes, chosen],
+        [((272, 128), bf16), ((152, LANES), f32)],
+        [state, arrived, arrived_low, arrived_high, spec, newest_table, chosen, geometry],
         scratch=[(512, 128), (304, 640), (19, 16, LANES), (19, 16, LANES), (32, LANES), (16, 128)],
     )
     (populations_out,) = call(
@@ -659,25 +653,13 @@
         [field, *cut(back, back_bands)],
         flops=10**9,
     )
-    newest = lax.all_to_all(payload, "obs", 0, 0, tiled=True)
+    gathered = lax.all_gather(payload, "obs", axis=0, tiled=False)
     (partial_value,) = call(
         radiate_kernel,
         [((128, 128), f32)],
-        [all_spec, jnp.asarray(late), newest, observers],
-        scratch=[
-            (272, 8, 128),
-            (3, 128, 128),
-            (128, 16384),
-            (1024, 128),
-            pltpu.VMEM((272, 1024), bf16),
-            (8, 256, 128),
-            (128, 128),
-            pltpu.VMEM((8, 16, 128), bf16),
-            (3, 128),
-            pltpu.SemaphoreType.DMA((11,)),
-        ],
-        megabytes=60,
-        fetch=True,
+        [gathered, observers],
+        scratch=[(272, 8, 128), (3, 128, 128), (128, 16384), (1024, 128)],
+        megabytes=20,
     )
     pieces = lax.all_to_all(partial_value.reshape(64, 256), "blk", 0, 0, tiled=True)
     summed = jnp.sum(pieces, axis=0)

time: 136 us -> 126 us (0.926)
  between operations: 14.8 us -> 1.36 us
  blocking collectives: 43.3 us -> 48.7 us
  waiting for transfers between devices: 27 us -> 22.9 us
  local copies, waits for them, and re-layouts: 1.86 us -> 4.45 us
    all_gather x0 -> x1, blocking collectives: none -> 14.5 us  [body(): gathered = lax.all_gather(payload, 'obs', axis=0, tiled=False)]
    all_to_all x1 -> x0, blocking collectives: 9.05 us -> none  [body(): newest = lax.all_to_all(payload, 'obs', 0, 0, tiled=True)]
    all_to_all x1, waiting for transfers between devices: 12 us -> 9.15 us  [body(): arrived = lax.all_to_all(sent, 'blk', 0, 0, tiled=True)]
    unnamed x8 -> x16, local copies, waits for them, and re-layouts: 1.86 us -> 4.45 us
    pallas_call x6 -> x7, Pallas kernels: 24.8 us -> 25.6 us  [call(): pl.pallas_call(kernel, out_shape=tuple((jax.ShapeDtypeStruct(s, d) for s,...]
  transfers between devices with their start and end apart: 7 -> 6, of which waited for: 3 -> 3; matrix products, arithmetic and copies ran while one was open for 0% -> 0% of each run, Pallas kernels for 6% -> 2%
where the time goes in v4:
time: 126 us
  blocking collectives  48.7 us (39%)
  Pallas kernels  25.6 us (20%)
  waiting for transfers between devices  22.9 us (18%)
  starting transfers between devices  22 us (17%)
  local copies, waits for them, and re-layouts  4.45 us (4%)
  between operations  1.36 us (1%)
    all_to_all x1, blocking collectives, body(): spread = lax.all_to_all(message, 'blk', 0, 0, tiled=True)  34.2 us
    pallas_call x7, Pallas kernels, call(): pl.pallas_call(kernel, out_shape=tuple((jax.ShapeDtypeStruct(s, d) for s,...  25.6 us
    all_gather x1, blocking collectives, body(): gathered = lax.all_gather(payload, 'obs', axis=0, tiled=False)  14.5 us
    all_to_all x1, waiting for transfers between devices, body(): lax.all_to_all(partial_value.reshape(64, 256), 'blk', 0, 0, tiled=True)  12.9 us
    all_to_all x1, waiting for transfers between devices, body(): arrived = lax.all_to_all(sent, 'blk', 0, 0, tiled=True)  9.15 us
    all_to_all x1, starting transfers between devices, body(): lax.all_to_all(partial_value.reshape(64, 256), 'blk', 0, 0, tiled=True)  7.86 us
    ppermute x4, starting transfers between devices, beside(): return (lax.ppermute(value, 'obs', up), lax.ppermute(value, 'obs', down))  7.71 us
    all_to_all x1, starting transfers between devices, body(): arrived = lax.all_to_all(sent, 'blk', 0, 0, tiled=True)  6.41 us
  transfers between devices with their start and end apart: 6, of which 3 were waited for; matrix products, arithmetic and copies ran while one was open for 0% of the time, Pallas kernels for 2%

profile of v4, /device:TPU:1, one launch (start us, length us, event | category | flops | bytes accessed | tf_op | source)
XLA Modules:
  0.0 125.7 jit_solution(5167429266790408052)
XLA Ops:
  1.3 2.3 %shard_map.167 = (f32[80,1024]{1,0:T(8,128)}, bf16[80,1024]{1,0:T(8,128)(2,1)}, bf16[64,8,128]{2,1,0:T(8,128)(2,1)}, f32[160,128]{1,0:T(8,128)}) custom-call(f32[1,19,4,1024]{3,2,1,0:T(4,128)} %refs_0_.1, s32[1,4]{1,0:T(1,128)} %refs_1_.1, s32[1,4]{1,0:T(1,128)} %refs_2_.1, s32[1]{0:T(128)S(6)} %copy.19.refs_3_, s32[1,128]{1,0:T(1,128)} %bitcast.7, ...), custom_call_target="tpu_custom_call" | custom-call | bytes 1048576 | tf_op jit(solution)/shard_map/pallas_call | solution.py:547
  3.6 34.2 %all_to_all.19.in_ref = bf16[64,8,128]{2,1,0:T(8,128)(2,1)S(1)} all-to-all(bf16[64,8,128]{2,1,0:T(8,128)(2,1)} %get-tuple-element.21), channel_id=1, replica_groups=mesh['blk'=64,'obs'=8] {'blk'}, dimensions={0} | all-to-all | bytes 262144 | tf_op jit(solution)/shard_map/all_to_all | solution.py:621
  37.8 0.0 copy-start.1
  37.8 0.9 copy-done.1
  38.7 0.9 shard_map.168
  39.6 6.4 %all-to-all-start.1 = ((bf16[64,8,128]{2,1,0:T(8,128)(2,1)}), bf16[64,8,128]{2,1,0:T(8,128)(2,1)S(1)}, u32[]{:S(2)}, u32[]{:S(2)}) async-start(bf16[64,8,128]{2,1,0:T(8,128)(2,1)} %get-tuple-element.23), calls=%async_computation.1 | async-start | bytes 262144 | tf_op jit(solution)/shard_map/all_to_all | solution.py:628
  46.1 1.9 %collective-permute-start.1 = (bf16[80,1024]{1,0:T(8,128)(2,1)}, bf16[80,1024]{1,0:T(8,128)(2,1)S(1)}, u32[]{:S(2)}, u32[]{:S(2)}) collective-permute-start(bf16[80,1024]{1,0:T(8,128)(2,1)} %get-tuple-element.20), channel_id=1, source_target_pairs={{0,7},{1,0},{2,1},{3,2},{4,3},{5,4},{6,5},{7,6},{8,15},{9,8},{10,9... | collective-permute-start | bytes 491528 | tf_op jit(solution)/shard_map/ppermute | solution.py:618
  48.0 1.1 collective-permute-start
  49.1 0.0 copy-start.3
  49.1 0.9 copy-done.3
  50.0 0.0 copy-start.6
  50.0 0.8 copy-done.6
  50.9 0.0 copy-start.7
  50.9 0.8 copy-done.7
  51.7 0.3 shard_map.169
  52.0 9.2 %all-to-all-done.1.arrived_ref.own_ref = bf16[64,8,128]{2,1,0:T(8,128)(2,1)S(1)} async-done(((bf16[64,8,128]{2,1,0:T(8,128)(2,1)}), bf16[64,8,128]{2,1,0:T(8,128)(2,1)S(1)}, u32[]{:S(2)}, u32[]{:S(2)}) %all-to-all-start.1) | async-done | bytes 131104 | tf_op jit(solution)/shard_map/all_to_all | solution.py:628
  61.1 3.6 %collective-permute-start.3 = (bf16[64,8,128]{2,1,0:T(8,128)(2,1)S(1)}, bf16[64,8,128]{2,1,0:T(8,128)(2,1)S(1)}, u32[]{:S(2)}, u32[]{:S(2)}) collective-permute-start(bf16[64,8,128]{2,1,0:T(8,128)(2,1)S(1)} %all-to-all-done.1.arrived_ref.own_ref), channel_id=1, source_target_pairs={{0,7},{1,0},{2,1},{3,2},{4,3},{5,4},{6,5},{7,6},{8,15},{9,8},{10,9... | collective-permute-start | bytes 393224 | tf_op jit(solution)/shard_map/ppermute | solution.py:618
  64.7 1.1 collective-permute-start.2
  65.8 0.0 collective-permute-done.1.high_ref
  65.8 0.0 collective-permute-done.low_ref
  65.8 0.0 copy-start
  65.8 1.0 copy-done
  66.8 1.1 shard_map.170
  67.8 0.0 copy-start.2
  67.8 0.9 collective-permute-done.3.high_ref
  68.7 0.0 collective-permute-done.2.low_ref
  68.7 0.0 copy-start.4
  68.7 0.0 copy-start.5
  68.7 4.5 %shard_map.171 = (bf16[272,128]{1,0:T(8,128)(2,1)S(1)}, f32[152,1664]{1,0:T(8,128)S(1)}) custom-call(f32[304,1664]{1,0:T(8,128)S(1)} %get-tuple-element.29.state_ref, bf16[64,8,128]{2,1,0:T(8,128)(2,1)S(1)} %all-to-all-done.1.arrived_ref.own_ref, bf16[64,8,128]{2,1,0:T(8,128)(2,1)S(1)} %collective-permute-done.2.low_ref, ...), custom_call_target="tpu_custom_call" | custom-call | bytes 1048576 | tf_op jit(solution)/shard_map/pallas_call | solution.py:547
  73.3 14.5 %all-gather = bf16[2176,128]{1,0:T(8,128)(2,1)S(1)} all-gather(bf16[272,128]{1,0:T(8,128)(2,1)S(1)} %get-tuple-element.35), channel_id=2, replica_groups=mesh['blk'=64,'obs'=8] {'obs'}, dimensions={0}, use_global_device_ids=true | all-gather | bytes 626688 | tf_op jit(solution)/shard_map/all_gather | solution.py:656
  87.8 0.0 copy-done.2
  87.8 15.3 %shard_map.173 = f32[128,128]{1,0:T(8,128)} custom-call(bf16[8,272,128]{2,1,0:T(8,128)(2,1)S(1)} %bitcast.5, f32[3,128]{1,0:T(4,128)S(1)} %copy-done.2), custom_call_target="tpu_custom_call" | custom-call | bytes 1048576 | tf_op jit(solution)/shard_map/pallas_call | solution.py:547
  103.1 7.9 %all-to-all-start.2 = ((f32[64,1,256]{2,1,0:T(1,128)}), f32[64,1,256]{2,1,0:T(1,128)S(1)}, u32[]{:S(2)}, u32[]{:S(2)}) async-start(f32[64,1,256]{2,1,0:T(1,128)} %bitcast.3), calls=%async_computation.2 | async-start | bytes 131072 | tf_op jit(solution)/shard_map/all_to_all | solution.py:664
  110.9 0.0 copy-done.4
  111.0 0.0 copy-done.5
  111.0 1.3 %shard_map.172 = f32[1,19,4,1024]{3,2,1,0:T(4,128)} custom-call(f32[152,1664]{1,0:T(8,128)S(1)} %get-tuple-element.34.field_ref, bf16[384,256]{1,0:T(8,128)(2,1)S(1)} %copy-done.5, bf16[512,256]{1,0:T(8,128)(2,1)S(1)} %copy-done.4, bf16[384,256]{1,0:T(8,128)(2,1)S(1)} %copy-done.5, bf16[512,256]{1,0:T(8,128)(2,1)S(1)} %copy-done.4), custom_call_target="tpu_custom_call" | custom-call | flops 1000000000 | bytes 1048576 | tf_op jit(solution)/shard_map/pallas_call | solution.py:547
  112.2 12.9 %all-to-all-done.2 = f32[64,1,256]{2,1,0:T(1,128)S(1)} async-done(((f32[64,1,256]{2,1,0:T(1,128)}), f32[64,1,256]{2,1,0:T(1,128)S(1)}, u32[]{:S(2)}, u32[]{:S(2)}) %all-to-all-start.2) | async-done | bytes 65568 | tf_op jit(solution)/shard_map/all_to_all | solution.py:664
  125.1 0.7 reduce_sum.9
Async XLA Ops:
  37.8 0.9 copy-start.1
  39.6 21.5 %all-to-all-start.1 = ((bf16[64,8,128]{2,1,0:T(8,128)(2,1)}), bf16[64,8,128]{2,1,0:T(8,128)(2,1)S(1)}, u32[]{:S(2)}, u32[]{:S(2)}) async-start(bf16[64,8,128]{2,1,0:T(8,128)(2,1)} %get-tuple-element.23), calls=%async_computation.1 | async-start | bytes 262144 | tf_op jit(solution)/shard_map/all_to_all | solution.py:628
  46.1 19.7 %collective-permute-start.1 = (bf16[80,1024]{1,0:T(8,128)(2,1)}, bf16[80,1024]{1,0:T(8,128)(2,1)S(1)}, u32[]{:S(2)}, u32[]{:S(2)}) collective-permute-start(bf16[80,1024]{1,0:T(8,128)(2,1)} %get-tuple-element.20), channel_id=1, source_target_pairs={{0,7},{1,0},{2,1},{3,2},{4,3},{5,4},{6,5},{7,6},{8,15},{9,8},{10,9... | collective-permute-start | bytes 491528 | tf_op jit(solution)/shard_map/ppermute | solution.py:618
  48.0 17.8 %collective-permute-start = (bf16[80,1024]{1,0:T(8,128)(2,1)}, bf16[80,1024]{1,0:T(8,128)(2,1)S(1)}, u32[]{:S(2)}, u32[]{:S(2)}) collective-permute-start(bf16[80,1024]{1,0:T(8,128)(2,1)} %get-tuple-element.20), channel_id=1, source_target_pairs={{0,1},{1,2},{2,3},{3,4},{4,5},{5,6},{6,7},{7,0},{8,9},{9,10},{10,1... | collective-permute-start | bytes 491528 | tf_op jit(solution)/shard_map/ppermute | solution.py:618
  49.1 0.9 copy-start.3
  50.0 0.8 copy-start.6
  50.9 0.8 copy-start.7
  61.1 7.6 %collective-permute-start.3 = (bf16[64,8,128]{2,1,0:T(8,128)(2,1)S(1)}, bf16[64,8,128]{2,1,0:T(8,128)(2,1)S(1)}, u32[]{:S(2)}, u32[]{:S(2)}) collective-permute-start(bf16[64,8,128]{2,1,0:T(8,128)(2,1)S(1)} %all-to-all-done.1.arrived_ref.own_ref), channel_id=1, source_target_pairs={{0,7},{1,0},{2,1},{3,2},{4,3},{5,4},{6,5},{7,6},{8,15},{9,8},{10,9... | collective-permute-start | bytes 393224 | tf_op jit(solution)/shard_map/ppermute | solution.py:618
  64.7 4.0 %collective-permute-start.2 = (bf16[64,8,128]{2,1,0:T(8,128)(2,1)S(1)}, bf16[64,8,128]{2,1,0:T(8,128)(2,1)S(1)}, u32[]{:S(2)}, u32[]{:S(2)}) collective-permute-start(bf16[64,8,128]{2,1,0:T(8,128)(2,1)S(1)} %all-to-all-done.1.arrived_ref.own_ref), channel_id=1, source_target_pairs={{0,1},{1,2},{2,3},{3,4},{4,5},{5,6},{6,7},{7,0},{8,9},{9,10},{10,1... | collective-permute-start | bytes 393224 | tf_op jit(solution)/shard_map/ppermute | solution.py:618
  65.8 1.0 copy-start
  67.8 20.0 %copy-start.2 = (f32[3,128]{1,0:T(4,128)S(1)}, f32[3,128]{1,0:T(4,128)}, u32[]{:S(2)}) copy-start(f32[3,128]{1,0:T(4,128)} %listen_ref.1) | copy-start | bytes 4612
  68.7 42.2 %copy-start.4 = (bf16[512,256]{1,0:T(8,128)(2,1)S(1)}, bf16[512,256]{1,0:T(8,128)(2,1)}, u32[]{:S(2)}) copy-start(bf16[512,256]{1,0:T(8,128)(2,1)} %constant.13.clone.rest_1_.rest_3_) | copy-start | bytes 786436
  68.7 42.2 %copy-start.5 = (bf16[384,256]{1,0:T(8,128)(2,1)S(1)}, bf16[384,256]{1,0:T(8,128)(2,1)}, u32[]{:S(2)}) copy-start(bf16[384,256]{1,0:T(8,128)(2,1)} %constant.12.clone.rest_0_.rest_2_) | copy-start | bytes 589828
  103.1 22.0 %all-to-all-start.2 = ((f32[64,1,256]{2,1,0:T(1,128)}), f32[64,1,256]{2,1,0:T(1,128)S(1)}, u32[]{:S(2)}, u32[]{:S(2)}) async-start(f32[64,1,256]{2,1,0:T(1,128)} %bitcast.3), calls=%async_computation.2 | async-start | bytes 131072 | tf_op jit(solution)/shard_map/all_to_all | solution.py:664

commit v5 on v4

--- a/solution.py
+++ b/solution.py
@@ -115,33 +115,34 @@
     rho = fs[0]
     for f in fs[1:]:
         rho = rho + f
-    speed = []
+    between = [fs[a] - fs[b] for a, b in PAIRS]
+    triple = 3.0 / rho
+    fast = []
     for axis in range(3):
-        up = [f for f, v in zip(fs, VEL) if v[axis] == 1]
-        down = [f for f, v in zip(fs, VEL) if v[axis] == -1]
-        speed.append(sum(up[1:], up[0]) - sum(down[1:], down[0]))
-    inverse = 1.0 / rho
-    speed = [s * inverse for s in speed]
-    squared = speed[0] * speed[0] + speed[1] * speed[1] + speed[2] * speed[2]
-    base = 1.0 - 1.5 * squared
+        momentum = None
+        for (a, _), value in zip(PAIRS, between):
+            if VEL[a][axis] == 1:
+                momentum = value if momentum is None else momentum + value
+            elif VEL[a][axis] == -1:
+                momentum = momentum - value
+        fast.append(momentum * triple)
+    squared = fast[0] * fast[0] + fast[1] * fast[1] + fast[2] * fast[2]
+    base = 2.0 - (1.0 / 3.0) * squared
+    scales = [(RELAX / 18.0) * rho, (RELAX / 36.0) * rho, (RELAX / 72.0) * rho]
     out = [None] * 19
-    out[0] = (RELAX * WEIGHT[0]) * rho * base + (1.0 - RELAX) * fs[0]
-    axis_scale = (RELAX / 18.0) * rho
-    diagonal_scale = (RELAX / 36.0) * rho
+    out[0] = (0.5 * RELAX * WEIGHT[0]) * rho * base + (1.0 - RELAX) * fs[0]
     for a, b in PAIRS:
         along = None
         for axis in range(3):
-            if VEL[a][axis] != 0:
-                term = speed[axis]
-                if along is None:
-                    along = term if VEL[a][axis] == 1 else -term
-                else:
-                    along = along + term if VEL[a][axis] == 1 else along - term
-        scale = axis_scale if a < 7 else diagonal_scale
-        even = scale * (base + 4.5 * (along * along))
-        odd = scale * (3.0 * along)
-        out[a] = even + odd + (1.0 - RELAX) * fs[a]
-        out[b] = even - odd + (1.0 - RELAX) * fs[b]
+            if VEL[a][axis] == 1:
+                along = fast[axis] if along is None else along + fast[axis]
+            elif VEL[a][axis] == -1:
+                along = along - fast[axis]
+        full, half = scales[:2] if a < 7 else scales[1:]
+        even = half * (base + along * along)
+        odd = full * along
+        out[a] = (even + odd) + (1.0 - RELAX) * fs[a]
+        out[b] = (even - odd) + (1.0 - RELAX) * fs[b]
     return out
 
 
@@ -294,7 +295,19 @@
         ref[16 * i : 16 * i + 2, lanes] = value[2:4]
 
 
-def slots_kernel(facts_ref, hist_ref, table_ref, late_ref, spec, late, chosen):
+def halo_rows(lane):
+    y, z = lane // PITCH - HALO, lane % PITCH - HALO
+    dy = jnp.where(y < 0, -1 - y, y - BS)
+    dz = jnp.where(z < 0, -1 - z, z - BS)
+    middle_y, middle_z = (y >= 0) & (y < BS), (z >= 0) & (z < BS)
+    edge = 2 * (y < 0).astype(jnp.int32) + (z < 0).astype(jnp.int32)
+    row = 512 + edge * 16 + dy * HALO + dz
+    row = jnp.where(middle_z, jnp.where(y < 0, 128, 0) + dy * BS + z, row)
+    row = jnp.where(middle_y, jnp.where(z < 0, 384, 256) + dz * BS + y, row)
+    return jnp.where((middle_y & middle_z) | (y >= BS + HALO), -1, row)
+
+
+def slots_kernel(halo_bands, facts_ref, hist_ref, table_ref, late_ref, spec, late, chosen, *tables):
     nt = (((1,), (1,)), ((), ()))
     spec[0:128, :] = lax.dot_general(table_ref[...], hist_ref[:, 0:256], nt, preferred_element_type=f32)
     spec[128:256, :] = lax.dot_general(table_ref[...], hist_ref[:, 256:512], nt, preferred_element_type=f32)
@@ -304,6 +317,13 @@
     late[...] = late_ref[...]
     spot = facts_ref[138:139, :].astype(jnp.int32)
     chosen[...] = onehot(lax.broadcasted_iota(jnp.int32, (LANES, 128), 0) == spot)
+    for (lo, hi, a, b), table in zip(halo_bands, tables):
+        source = halo_rows(lax.broadcasted_iota(jnp.int32, (1, hi - lo), 1) + lo)
+        row = lax.broadcasted_iota(jnp.int32, (b - a, hi - lo), 0) + a
+        match = row == source
+        if b > 512:
+            match = match | (row == jnp.where(source >= 512, source + 64, -1))
+        table[...] = onehot(match)
 
 
 def early_kernel(bands, c_ref, low_ref, high_ref, arrived_ref, facts_ref, state, geo, rows, answers):
@@ -335,22 +355,11 @@
         state[:, lo:hi] = placed + jnp.dot(fine, table, preferred_element_type=f32)
 
 
-def halo_rows(lane):
-    y, z = lane // PITCH - HALO, lane % PITCH - HALO
-    dy = jnp.where(y < 0, -1 - y, y - BS)
-    dz = jnp.where(z < 0, -1 - z, z - BS)
-    middle_y, middle_z = (y >= 0) & (y < BS), (z >= 0) & (z < BS)
-    edge = 2 * (y < 0).astype(jnp.int32) + (z < 0).astype(jnp.int32)
-    row = 512 + edge * 16 + dy * HALO + dz
-    row = jnp.where(middle_z, jnp.where(y < 0, 128, 0) + dy * BS + z, row)
-    row = jnp.where(middle_y, jnp.where(z < 0, 384, 256) + dz * BS + y, row)
-    return jnp.where((middle_y & middle_z) | (y >= BS + HALO), -1, row)
-
-
 def flow_kernel(
-    halo_bands, state_ref, own_ref, low_ref, high_ref, spec_ref, table_ref, chosen_ref, geo_ref,
-    out_ref, field_ref, packed, halo, here, there, seen, late,
+    halo_bands, state_ref, own_ref, low_ref, high_ref, spec_ref, table_ref, chosen_ref, geo_ref, *rest,
 ):
+    tables, rest = rest[: len(halo_bands)], rest[len(halo_bands) :]
+    out_ref, field_ref, packed, halo, here, there, seen, late = rest
     lane4 = lax.broadcasted_iota(jnp.int32, (4, 128), 1)
     lane64 = lax.broadcasted_iota(jnp.int32, (64, 128), 1)
     for i in range(19):
@@ -380,13 +389,8 @@
             rows = packed[at : at + 4, :]
             rows = jnp.where((lane4 < 64) == (i < 16), rows, 0.0)
             place_slab(halo, i, slab, rows, slice(512, 640))
-    for lo, hi, a, b in halo_bands:
-        source = halo_rows(lax.broadcasted_iota(jnp.int32, (1, hi - lo), 1) + lo)
-        row = lax.broadcasted_iota(jnp.int32, (b - a, hi - lo), 0) + a
-        match = row == source
-        if b > 512:
-            match = match | (row == jnp.where(source >= 512, source + 64, -1))
-        added = jnp.dot(halo[:, a:b].astype(bf16), onehot(match), preferred_element_type=f32)
+    for (lo, hi, a, b), table in zip(halo_bands, tables):
+        added = jnp.dot(halo[:, a:b].astype(bf16), table[...], preferred_element_type=f32)
         for i in range(19):
             here[i, :, lo:hi] = state_ref[16 * i : 16 * i + 16, lo:hi] + added[16 * i : 16 * i + 16] + WEIGHT[i]
 
@@ -626,13 +630,16 @@
         scratch=[(512, 128), (512, 128), (128, P_OWN)],
     )
     arrived = lax.all_to_all(sent, "blk", 0, 0, tiled=True)
-    spec, newest_table, chosen = call(
-        slots_kernel,
-        [((272, 128), f32), ((128, 128), f32), ((LANES, 128), bf16)],
+    spec, newest_table, chosen, *tables = call(
+        functools.partial(slots_kernel, halo_bands),
+        [((272, 128), f32), ((128, 128), f32), ((LANES, 128), bf16)]
+        + [((b - a, hi - lo), bf16) for lo, hi, a, b in halo_bands],
         [facts, history, jnp.asarray(shifted), jnp.asarray(late)],
         flops=10**8,
     )
-    arrived, spec, newest_table, chosen = lax.optimization_barrier((arrived, spec, newest_table, chosen))
+    arrived, spec, newest_table, chosen, tables = lax.optimization_barrier(
+        (arrived, spec, newest_table, chosen, tables)
+    )
     arrived_low, arrived_high = beside(arrived)
     state, geometry = call(
         functools.partial(early_kernel, bands),
@@ -644,7 +651,7 @@
     payload, field = call(
         functools.partial(flow_kernel, halo_bands),
         [((272, 128), bf16), ((152, LANES), f32)],
-        [state, arrived, arrived_low, arrived_high, spec, newest_table, chosen, geometry],
+        [state, arrived, arrived_low, arrived_high, spec, newest_table, chosen, geometry, *tables],
         scratch=[(512, 128), (304, 640), (19, 16, LANES), (19, 16, LANES), (32, LANES), (16, 128)],
     )
     (populations_out,) = call(

time: 126 us -> 126 us (level)
  Pallas kernels: 25.6 us -> 22.9 us
  starting transfers between devices: 22 us -> 24.1 us
  waiting for transfers between devices: 22.9 us -> 21.5 us
    pallas_call x7, Pallas kernels: 25.6 us -> 22.9 us  [call(): pl.pallas_call(kernel, out_shape=tuple((jax.ShapeDtypeStruct(s, d) for s,...]
    all_to_all x1, starting transfers between devices: 7.86 us -> 9.93 us  [body(): lax.all_to_all(partial_value.reshape(64, 256), 'blk', 0, 0, tiled=True)]
where the time goes in v5:
time: 126 us; the launch traced here: 125 us
  blocking collectives  48.7 us (39%)
  starting transfers between devices  24.1 us (19%)
  Pallas kernels  22.9 us (18%)
  waiting for transfers between devices  21.5 us (17%)
  local copies, waits for them, and re-layouts  5.37 us (4%)
  between operations  1.35 us (1%)
    all_to_all x1, blocking collectives, body(): spread = lax.all_to_all(message, 'blk', 0, 0, tiled=True)  34.2 us
    pallas_call x7, Pallas kernels, call(): pl.pallas_call(kernel, out_shape=tuple((jax.ShapeDtypeStruct(s, d) for s,...  22.9 us
    all_gather x1, blocking collectives, body(): gathered = lax.all_gather(payload, 'obs', axis=0, tiled=False)  14.5 us
    all_to_all x1, waiting for transfers between devices, body(): lax.all_to_all(partial_value.reshape(64, 256), 'blk', 0, 0, tiled=True)  11.9 us
    all_to_all x1, starting transfers between devices, body(): lax.all_to_all(partial_value.reshape(64, 256), 'blk', 0, 0, tiled=True)  9.93 us
    all_to_all x1, waiting for transfers between devices, body(): arrived = lax.all_to_all(sent, 'blk', 0, 0, tiled=True)  8.64 us
    ppermute x4, starting transfers between devices, beside(): return (lax.ppermute(value, 'obs', up), lax.ppermute(value, 'obs', down))  7.72 us
    all_to_all x1, starting transfers between devices, body(): arrived = lax.all_to_all(sent, 'blk', 0, 0, tiled=True)  6.4 us
  transfers between devices with their start and end apart: 6, of which 3 were waited for; matrix products, arithmetic and copies ran while one was open for 0% of the time, Pallas kernels for 2%

profile of v5, /device:TPU:1, one launch (start us, length us, event | category | flops | bytes accessed | tf_op | source)
XLA Modules:
  0.0 124.6 jit_solution(12593565331266689110)
XLA Ops:
  1.3 2.3 %shard_map.167 = (f32[80,1024]{1,0:T(8,128)}, bf16[80,1024]{1,0:T(8,128)(2,1)}, bf16[64,8,128]{2,1,0:T(8,128)(2,1)}, f32[160,128]{1,0:T(8,128)}) custom-call(f32[1,19,4,1024]{3,2,1,0:T(4,128)} %refs_0_.1, s32[1,4]{1,0:T(1,128)} %refs_1_.1, s32[1,4]{1,0:T(1,128)} %refs_2_.1, s32[1]{0:T(128)S(6)} %copy.19.refs_3_, s32[1,128]{1,0:T(1,128)} %bitcast.7, ...), custom_call_target="tpu_custom_call" | custom-call | bytes 1048576 | tf_op jit(solution)/shard_map/pallas_call | solution.py:551
  3.6 34.2 %all_to_all.19.in_ref = bf16[64,8,128]{2,1,0:T(8,128)(2,1)S(1)} all-to-all(bf16[64,8,128]{2,1,0:T(8,128)(2,1)} %get-tuple-element.35), channel_id=1, replica_groups=mesh['blk'=64,'obs'=8] {'blk'}, dimensions={0} | all-to-all | bytes 262144 | tf_op jit(solution)/shard_map/all_to_all | solution.py:625
  37.8 0.0 copy-start.1
  37.8 0.9 copy-done.1
  38.7 0.9 shard_map.168
  39.6 6.4 %all-to-all-start.1 = ((bf16[64,8,128]{2,1,0:T(8,128)(2,1)}), bf16[64,8,128]{2,1,0:T(8,128)(2,1)S(1)}, u32[]{:S(2)}, u32[]{:S(2)}) async-start(bf16[64,8,128]{2,1,0:T(8,128)(2,1)} %get-tuple-element.37), calls=%async_computation.1 | async-start | bytes 262144 | tf_op jit(solution)/shard_map/all_to_all | solution.py:632
  46.0 1.9 %collective-permute-start.1 = (bf16[80,1024]{1,0:T(8,128)(2,1)}, bf16[80,1024]{1,0:T(8,128)(2,1)S(1)}, u32[]{:S(2)}, u32[]{:S(2)}) collective-permute-start(bf16[80,1024]{1,0:T(8,128)(2,1)} %get-tuple-element.34), channel_id=1, source_target_pairs={{0,7},{1,0},{2,1},{3,2},{4,3},{5,4},{6,5},{7,6},{8,15},{9,8},{10,9... | collective-permute-start | bytes 491528 | tf_op jit(solution)/shard_map/ppermute | solution.py:622
  48.0 1.1 collective-permute-start
  49.1 0.0 copy-start.3
  49.1 0.9 copy-done.3
  50.0 0.0 copy-start.6
  50.0 0.8 copy-done.6
  50.9 0.0 copy-start.7
  50.9 0.8 copy-done.7
  51.7 0.8 shard_map.169
  52.5 8.6 %all-to-all-done.1.arrived_ref.own_ref = bf16[64,8,128]{2,1,0:T(8,128)(2,1)S(1)} async-done(((bf16[64,8,128]{2,1,0:T(8,128)(2,1)}), bf16[64,8,128]{2,1,0:T(8,128)(2,1)S(1)}, u32[]{:S(2)}, u32[]{:S(2)}) %all-to-all-start.1) | async-done | bytes 131104 | tf_op jit(solution)/shard_map/all_to_all | solution.py:632
  61.1 3.6 %collective-permute-start.3 = (bf16[64,8,128]{2,1,0:T(8,128)(2,1)S(1)}, bf16[64,8,128]{2,1,0:T(8,128)(2,1)S(1)}, u32[]{:S(2)}, u32[]{:S(2)}) collective-permute-start(bf16[64,8,128]{2,1,0:T(8,128)(2,1)S(1)} %all-to-all-done.1.arrived_ref.own_ref), channel_id=1, source_target_pairs={{0,7},{1,0},{2,1},{3,2},{4,3},{5,4},{6,5},{7,6},{8,15},{9,8},{10,9... | collective-permute-start | bytes 393224 | tf_op jit(solution)/shard_map/ppermute | solution.py:622
  64.7 1.1 collective-permute-start.2
  65.8 0.0 collective-permute-done.1.high_ref
  65.8 0.0 collective-permute-done.low_ref
  65.8 0.0 copy-start
  65.8 1.0 copy-done
  66.7 1.1 shard_map.170
  67.8 0.9 collective-permute-done.3.high_ref
  68.7 0.0 collective-permute-done.2.low_ref
  68.7 0.0 copy-start.2
  68.7 0.0 copy-start.4
  68.7 4.2 %shard_map.171 = (bf16[272,128]{1,0:T(8,128)(2,1)S(1)}, f32[152,1664]{1,0:T(8,128)S(1)}) custom-call(f32[304,1664]{1,0:T(8,128)S(1)} %get-tuple-element.50.state_ref, bf16[64,8,128]{2,1,0:T(8,128)(2,1)S(1)} %all-to-all-done.1.arrived_ref.own_ref, bf16[64,8,128]{2,1,0:T(8,128)(2,1)S(1)} %collective-permute-done.2.low_ref, ...), custom_call_target="tpu_custom_call" | custom-call | bytes 1048576 | tf_op jit(solution)/shard_map/pallas_call | solution.py:551
  72.9 14.5 %all-gather = bf16[2176,128]{1,0:T(8,128)(2,1)S(1)} all-gather(bf16[272,128]{1,0:T(8,128)(2,1)S(1)} %get-tuple-element.63), channel_id=2, replica_groups=mesh['blk'=64,'obs'=8] {'obs'}, dimensions={0}, use_global_device_ids=true | all-gather | bytes 626688 | tf_op jit(solution)/shard_map/all_gather | solution.py:663
  87.4 0.0 copy-done.2
  87.4 12.4 %shard_map.173 = f32[128,128]{1,0:T(8,128)} custom-call(bf16[8,272,128]{2,1,0:T(8,128)(2,1)S(1)} %bitcast.5, f32[3,128]{1,0:T(4,128)S(1)} %copy-done.2), custom_call_target="tpu_custom_call" | custom-call | bytes 1048576 | tf_op jit(solution)/shard_map/pallas_call | solution.py:551
  99.8 9.9 %all-to-all-start.2 = ((f32[64,1,256]{2,1,0:T(1,128)}), f32[64,1,256]{2,1,0:T(1,128)S(1)}, u32[]{:S(2)}, u32[]{:S(2)}) async-start(f32[64,1,256]{2,1,0:T(1,128)} %bitcast.3), calls=%async_computation.2 | async-start | bytes 131072 | tf_op jit(solution)/shard_map/all_to_all | solution.py:671
  109.8 0.0 copy-done.4
  109.8 0.0 copy-start.5
  109.8 0.9 copy-done.5
  110.7 1.3 %shard_map.172 = f32[1,19,4,1024]{3,2,1,0:T(4,128)} custom-call(f32[152,1664]{1,0:T(8,128)S(1)} %get-tuple-element.62.field_ref, bf16[384,256]{1,0:T(8,128)(2,1)S(1)} %copy-done.5, bf16[512,256]{1,0:T(8,128)(2,1)S(1)} %copy-done.4, bf16[384,256]{1,0:T(8,128)(2,1)S(1)} %copy-done.5, bf16[512,256]{1,0:T(8,128)(2,1)S(1)} %copy-done.4), custom_call_target="tpu_custom_call" | custom-call | flops 1000000000 | bytes 1048576 | tf_op jit(solution)/shard_map/pallas_call | solution.py:551
  112.0 11.9 %all-to-all-done.2 = f32[64,1,256]{2,1,0:T(1,128)S(1)} async-done(((f32[64,1,256]{2,1,0:T(1,128)}), f32[64,1,256]{2,1,0:T(1,128)S(1)}, u32[]{:S(2)}, u32[]{:S(2)}) %all-to-all-start.2) | async-done | bytes 65568 | tf_op jit(solution)/shard_map/all_to_all | solution.py:671
  123.9 0.7 reduce_sum.9
Async XLA Ops:
  37.8 0.9 copy-start.1
  39.6 21.5 %all-to-all-start.1 = ((bf16[64,8,128]{2,1,0:T(8,128)(2,1)}), bf16[64,8,128]{2,1,0:T(8,128)(2,1)S(1)}, u32[]{:S(2)}, u32[]{:S(2)}) async-start(bf16[64,8,128]{2,1,0:T(8,128)(2,1)} %get-tuple-element.37), calls=%async_computation.1 | async-start | bytes 262144 | tf_op jit(solution)/shard_map/all_to_all | solution.py:632
  46.0 19.7 %collective-permute-start.1 = (bf16[80,1024]{1,0:T(8,128)(2,1)}, bf16[80,1024]{1,0:T(8,128)(2,1)S(1)}, u32[]{:S(2)}, u32[]{:S(2)}) collective-permute-start(bf16[80,1024]{1,0:T(8,128)(2,1)} %get-tuple-element.34), channel_id=1, source_target_pairs={{0,7},{1,0},{2,1},{3,2},{4,3},{5,4},{6,5},{7,6},{8,15},{9,8},{10,9... | collective-permute-start | bytes 491528 | tf_op jit(solution)/shard_map/ppermute | solution.py:622
  48.0 17.8 %collective-permute-start = (bf16[80,1024]{1,0:T(8,128)(2,1)}, bf16[80,1024]{1,0:T(8,128)(2,1)S(1)}, u32[]{:S(2)}, u32[]{:S(2)}) collective-permute-start(bf16[80,1024]{1,0:T(8,128)(2,1)} %get-tuple-element.34), channel_id=1, source_target_pairs={{0,1},{1,2},{2,3},{3,4},{4,5},{5,6},{6,7},{7,0},{8,9},{9,10},{10,1... | collective-permute-start | bytes 491528 | tf_op jit(solution)/shard_map/ppermute | solution.py:622
  49.1 0.9 copy-start.3
  50.0 0.8 copy-start.6
  50.9 0.8 copy-start.7
  61.1 7.6 %collective-permute-start.3 = (bf16[64,8,128]{2,1,0:T(8,128)(2,1)S(1)}, bf16[64,8,128]{2,1,0:T(8,128)(2,1)S(1)}, u32[]{:S(2)}, u32[]{:S(2)}) collective-permute-start(bf16[64,8,128]{2,1,0:T(8,128)(2,1)S(1)} %all-to-all-done.1.arrived_ref.own_ref), channel_id=1, source_target_pairs={{0,7},{1,0},{2,1},{3,2},{4,3},{5,4},{6,5},{7,6},{8,15},{9,8},{10,9... | collective-permute-start | bytes 393224 | tf_op jit(solution)/shard_map/ppermute | solution.py:622
  64.7 4.0 %collective-permute-start.2 = (bf16[64,8,128]{2,1,0:T(8,128)(2,1)S(1)}, bf16[64,8,128]{2,1,0:T(8,128)(2,1)S(1)}, u32[]{:S(2)}, u32[]{:S(2)}) collective-permute-start(bf16[64,8,128]{2,1,0:T(8,128)(2,1)S(1)} %all-to-all-done.1.arrived_ref.own_ref), channel_id=1, source_target_pairs={{0,1},{1,2},{2,3},{3,4},{4,5},{5,6},{6,7},{7,0},{8,9},{9,10},{10,1... | collective-permute-start | bytes 393224 | tf_op jit(solution)/shard_map/ppermute | solution.py:622
  65.8 1.0 copy-start
  68.7 18.7 %copy-start.2 = (f32[3,128]{1,0:T(4,128)S(1)}, f32[3,128]{1,0:T(4,128)}, u32[]{:S(2)}) copy-start(f32[3,128]{1,0:T(4,128)} %listen_ref.1) | copy-start | bytes 4612
  68.7 41.1 %copy-start.4 = (bf16[512,256]{1,0:T(8,128)(2,1)S(1)}, bf16[512,256]{1,0:T(8,128)(2,1)}, u32[]{:S(2)}) copy-start(bf16[512,256]{1,0:T(8,128)(2,1)} %constant.13.clone.rest_1_.rest_3_) | copy-start | bytes 786436
  99.8 24.1 %all-to-all-start.2 = ((f32[64,1,256]{2,1,0:T(1,128)}), f32[64,1,256]{2,1,0:T(1,128)S(1)}, u32[]{:S(2)}, u32[]{:S(2)}) async-start(f32[64,1,256]{2,1,0:T(1,128)} %bitcast.3), calls=%async_computation.2 | async-start | bytes 131072 | tf_op jit(solution)/shard_map/all_to_all | solution.py:671
  109.8 0.9 copy-start.5
